TPU v7x, 32 devices: a whole 2x2x4 slice. The times are simulated.
32 devices in a mesh: dp: 8 (over y, x, core), tensor: 4 (over z).
Axes of the slice: x: 2, y: 2, z: 4, core: 2. Of those that a mesh axis runs over, the one named last changes fastest.
Arguments:
- tokens: bfloat16 [8, 512, 1024], P('dp'), may hold values from -6 to 6
- segment_ids: int32 [8, 512], P('dp'), may hold values from 0 to 9, never falling along the last dimension, each value on 1 to 200 neighbouring positions
- cotangent: bfloat16 [8, 512, 1024], P('dp'), may hold values from -6 to 6
- qkv_weight: bfloat16 [2, 1024, 3, 1024], P(None, None, None, 'tensor'), may hold values from -0.1875 to 0.1875
- qv_bias: bfloat16 [2, 2, 1024], P(None, None, 'tensor'), may hold values from -3 to 3
- proj_weight: bfloat16 [2, 1024, 1024], P(None, 'tensor'), may hold values from -1 to 1
- proj_bias: bfloat16 [2, 1024], replicated, may hold values from -2 to 2
- first_gain: bfloat16 [2, 1024], replicated, may hold values from 0.099609375 to 1.8984375
- first_shift: bfloat16 [2, 1024], replicated, may hold values from -2 to 2
- up_weight: bfloat16 [2, 1024, 4096], P(None, None, 'tensor'), may hold values from -0.1875 to 0.1875
- up_bias: bfloat16 [2, 4096], P(None, 'tensor'), may hold values from -3 to 3
- down_weight: bfloat16 [2, 4096, 1024], P(None, 'tensor'), may hold values from -0.09375 to 0.09375
- down_bias: bfloat16 [2, 1024], replicated, may hold values from -2 to 2
- second_gain: bfloat16 [2, 1024], replicated, may hold values from 0.099609375 to 1.8984375
- second_shift: bfloat16 [2, 1024], replicated, may hold values from -2 to 2
Outputs:
- mixed: float32 [8, 512, 1024], P('dp')
- input_grad: float32 [8, 512, 1024], P('dp')
- qkv_weight_grad: float32 [2, 1024, 3, 1024], P(None, None, None, 'tensor')
- qv_bias_grad: float32 [2, 2, 1024], P(None, None, 'tensor')
- proj_weight_grad: float32 [2, 1024, 1024], P(None, 'tensor')
- proj_bias_grad: float32 [2, 1024], replicated
- first_gain_grad: float32 [2, 1024], replicated
- first_shift_grad: float32 [2, 1024], replicated
- up_weight_grad: float32 [2, 1024, 4096], P(None, None, 'tensor')
- up_bias_grad: float32 [2, 4096], P(None, 'tensor')
- down_weight_grad: float32 [2, 4096, 1024], P(None, 'tensor')
- down_bias_grad: float32 [2, 1024], replicated
- second_gain_grad: float32 [2, 1024], replicated
- second_shift_grad: float32 [2, 1024], replicated
Inputs may be any that keep to these rules, and one draw needn't show every extreme that they name: `segment_ids`: within a sequence the document number never falls; every document holds 1 to 200 tokens, and tokens attend only within their document.
All inputs are finite; a program needn't handle non-finite values.
Results may differ from a plain program's by a relative error of at most 0.034.
Values may be sent and summed in bfloat16 or wider, within the bound.
A program may use at most 192 MiB of HBM per device.

v0:
```python
import jax
import jax.numpy as jnp
from jax import lax
from jax.sharding import PartitionSpec as P

HEAD = 64


norm_eps = 1e-12
masked_value = -1000000000.0


def layer_norm(residual, norm_gain, norm_shift):
    centred = residual - jnp.mean(residual, axis=-1, keepdims=True)
    spread = jnp.mean(centred * centred, axis=-1, keepdims=True)
    return centred * lax.rsqrt(spread + norm_eps) * norm_gain + norm_shift


def gelu_exact(pre_act):
    return jax.nn.gelu(pre_act, approximate=False)


def masked_scores(query_rows, key_rows, seg_row):
    score_scale = query_rows.shape[-1] ** (-0.5)
    raw_scores = (
        jnp.einsum("qhd,khd->hqk", query_rows, key_rows, preferred_element_type=jnp.float32)
        * score_scale
    )
    same_doc = seg_row[:, None] == seg_row[None, :]
    return jnp.where(same_doc[None], raw_scores, masked_value)


def attend_forward(block_items):
    query_rows, key_rows, value_rows, seg_row = block_items
    scores = masked_scores(query_rows, key_rows, seg_row)
    row_max = jnp.max(scores, axis=-1, keepdims=True)
    exponent = jnp.exp(scores - row_max)
    row_total = jnp.sum(exponent, axis=-1, keepdims=True)
    probs_low = (exponent / row_total).astype(jnp.bfloat16)
    context = jnp.einsum("hqk,khd->qhd", probs_low, value_rows, preferred_element_type=jnp.float32)
    return (context.astype(jnp.bfloat16), row_max + jnp.log(row_total))


def attend_backward(block_items):
    query_rows, key_rows, value_rows, seg_row, log_total, grad_context = block_items
    score_scale = query_rows.shape[-1] ** (-0.5)
    scores = masked_scores(query_rows, key_rows, seg_row)
    probability = jnp.exp(scores - log_total)
    grad_probs = jnp.einsum(
        "qhd,khd->hqk", grad_context, value_rows, preferred_element_type=jnp.float32
    )
    row_inner = jnp.sum(probability * grad_probs, axis=-1, keepdims=True)
    grad_scores = (probability * (grad_probs - row_inner)).astype(jnp.bfloat16)
    grad_query = (
        jnp.einsum("hqk,khd->qhd", grad_scores, key_rows, preferred_element_type=jnp.float32)
        * score_scale
    )
    grad_key = (
        jnp.einsum("hqk,qhd->khd", grad_scores, query_rows, preferred_element_type=jnp.float32)
        * score_scale
    )
    grad_value = jnp.einsum(
        "hqk,qhd->khd",
        probability.astype(jnp.bfloat16),
        grad_context,
        preferred_element_type=jnp.float32,
    )
    return jnp.stack([grad_query, grad_key, grad_value], axis=1).astype(jnp.bfloat16)


def layer_forward(own_rows, full_low, params, seg_ids, reduce_rows, widen_rows):
    (
        qkv_w,
        qv_b,
        proj_w,
        proj_b,
        gain_one,
        shift_one,
        up_w,
        up_b,
        down_w,
        down_b,
        gain_two,
        shift_two,
    ) = params
    row_count, model_width = full_low.shape
    local_width = qkv_w.shape[-1]
    seq_count, length = seg_ids.shape
    projected = jnp.dot(
        full_low, qkv_w.reshape(model_width, 3 * local_width), preferred_element_type=jnp.float32
    )
    projected = projected.reshape(row_count, 3, local_width)
    zero_row = jnp.zeros_like(qv_b[0])
    projected = (projected + jnp.stack([qv_b[0], zero_row, qv_b[1]]).astype(jnp.float32)).astype(
        jnp.bfloat16
    )
    split_heads = projected.reshape(seq_count, length, 3, local_width // HEAD, HEAD)
    context, log_total = lax.map(
        attend_forward, (split_heads[:, :, 0], split_heads[:, :, 1], split_heads[:, :, 2], seg_ids)
    )
    context = context.reshape(row_count, local_width)
    attn_out = reduce_rows(
        jnp.dot(context, proj_w, preferred_element_type=jnp.float32)
    ) + proj_b.astype(jnp.float32)
    first_sum = own_rows + attn_out
    normed = layer_norm(first_sum, gain_one.astype(jnp.float32), shift_one.astype(jnp.float32))
    normed_low = widen_rows(normed.astype(jnp.bfloat16))
    pre_act = jnp.dot(normed_low, up_w, preferred_element_type=jnp.float32) + up_b.astype(
        jnp.float32
    )
    act_low = gelu_exact(pre_act).astype(jnp.bfloat16)
    ffn_out = reduce_rows(
        jnp.dot(act_low, down_w, preferred_element_type=jnp.float32)
    ) + down_b.astype(jnp.float32)
    second_sum = normed + ffn_out
    output = layer_norm(second_sum, gain_two.astype(jnp.float32), shift_two.astype(jnp.float32))
    kept_values = (
        full_low,
        projected,
        log_total,
        context,
        first_sum,
        normed_low,
        pre_act,
        second_sum,
    )
    return (output, kept_values)


def layer_backward(grad_own, kept_values, params, seg_ids, reduce_rows, widen_rows):
    (
        qkv_w,
        qv_b,
        proj_w,
        proj_b,
        gain_one,
        shift_one,
        up_w,
        up_b,
        down_w,
        down_b,
        gain_two,
        shift_two,
    ) = params
    full_low, projected, log_total, context, first_sum, normed_low, pre_act, second_sum = (
        kept_values
    )
    row_count, model_width = full_low.shape
    local_width = qkv_w.shape[-1]
    seq_count, length = seg_ids.shape
    unused, norm_pull = jax.vjp(
        layer_norm, second_sum, gain_two.astype(jnp.float32), shift_two.astype(jnp.float32)
    )
    grad_second, grad_gain_two, grad_shift_two = norm_pull(grad_own)
    branch_low = grad_second.astype(jnp.bfloat16)
    grad_down_b = jnp.sum(branch_low.astype(jnp.float32), axis=0)
    branch_full = widen_rows(branch_low)
    act_value, gelu_pull = jax.vjp(gelu_exact, pre_act)
    act_low = act_value.astype(jnp.bfloat16)
    grad_down_w = jnp.einsum("rf,rd->fd", act_low, branch_full, preferred_element_type=jnp.float32)
    grad_act = jnp.einsum("rd,fd->rf", branch_full, down_w, preferred_element_type=jnp.float32)
    (grad_pre,) = gelu_pull(grad_act)
    pre_low = grad_pre.astype(jnp.bfloat16)
    grad_up_b = jnp.sum(pre_low.astype(jnp.float32), axis=0)
    grad_up_w = jnp.einsum("rd,rf->df", normed_low, pre_low, preferred_element_type=jnp.float32)
    grad_normed = grad_second + reduce_rows(
        jnp.einsum("rf,df->rd", pre_low, up_w, preferred_element_type=jnp.float32)
    )
    unused, norm_pull = jax.vjp(
        layer_norm, first_sum, gain_one.astype(jnp.float32), shift_one.astype(jnp.float32)
    )
    grad_first, grad_gain_one, grad_shift_one = norm_pull(grad_normed)
    attn_low = grad_first.astype(jnp.bfloat16)
    grad_proj_b = jnp.sum(attn_low.astype(jnp.float32), axis=0)
    attn_full = widen_rows(attn_low)
    grad_proj_w = jnp.einsum("rc,rd->cd", context, attn_full, preferred_element_type=jnp.float32)
    grad_context = jnp.einsum(
        "rd,cd->rc", attn_full, proj_w, preferred_element_type=jnp.float32
    ).astype(jnp.bfloat16)
    head_count = local_width // HEAD
    split_heads = projected.reshape(seq_count, length, 3, head_count, HEAD)
    grad_heads = lax.map(
        attend_backward,
        (
            split_heads[:, :, 0],
            split_heads[:, :, 1],
            split_heads[:, :, 2],
            seg_ids,
            log_total,
            grad_context.reshape(seq_count, length, head_count, HEAD),
        ),
    )
    grad_proj = grad_heads.reshape(row_count, 3 * local_width)
    grad_qkv_w = jnp.einsum(
        "rd,rc->dc", full_low, grad_proj, preferred_element_type=jnp.float32
    ).reshape(model_width, 3, local_width)
    grad_sums = jnp.sum(grad_proj.astype(jnp.float32).reshape(row_count, 3, local_width), axis=0)
    grad_qv_b = jnp.stack([grad_sums[0], grad_sums[2]])
    flat_weight = qkv_w.reshape(model_width, 3 * local_width)
    grad_input = grad_first + reduce_rows(
        jnp.einsum("rc,dc->rd", grad_proj, flat_weight, preferred_element_type=jnp.float32)
    )
    big_layer = (grad_qkv_w, grad_proj_w, grad_up_w, grad_down_w)
    sharded_layer = (grad_qv_b, grad_up_b)
    shared_layer = (
        grad_proj_b,
        grad_gain_one,
        grad_shift_one,
        grad_down_b,
        grad_gain_two,
        grad_shift_two,
    )
    return (grad_input, big_layer, sharded_layer, shared_layer)


def local(
    tokens,
    segment_ids,
    cotangent,
    qkv_weight,
    qv_bias,
    proj_weight,
    proj_bias,
    first_gain,
    first_shift,
    up_weight,
    up_bias,
    down_weight,
    down_bias,
    second_gain,
    second_shift,
):
    seq_count, length, model_width = tokens.shape
    row_count = seq_count * length
    layers = qkv_weight.shape[0]
    tensor_size = lax.axis_size("tensor")
    share_rows = row_count // tensor_size
    tensor_pos = lax.axis_index("tensor")
    row_start = tensor_pos * share_rows

    def reduce_rows(partial_sum):
        return lax.psum_scatter(
            partial_sum.astype(jnp.bfloat16), "tensor", scatter_dimension=0, tiled=True
        ).astype(jnp.float32)

    def widen_rows(low_rows):
        return lax.all_gather(low_rows, "tensor", axis=0, tiled=True)

    def own_part(full_rows):
        return lax.dynamic_slice_in_dim(full_rows, row_start, share_rows, 0)

    def whole_rows(part_rows):
        return lax.all_gather(part_rows.astype(jnp.bfloat16), "tensor", axis=0, tiled=True).astype(
            part_rows.dtype
        )

    all_params = (
        qkv_weight,
        qv_bias,
        proj_weight,
        proj_bias,
        first_gain,
        first_shift,
        up_weight,
        up_bias,
        down_weight,
        down_bias,
        second_gain,
        second_shift,
    )
    flat_rows = tokens.reshape(row_count, model_width)
    own_rows = own_part(flat_rows.astype(jnp.float32))
    full_low = flat_rows
    kept_layers = []
    for layer_idx in range(layers):
        params = tuple((stacked[layer_idx] for stacked in all_params))
        output, kept_values = layer_forward(
            own_rows, full_low, params, segment_ids, reduce_rows, widen_rows
        )
        kept_layers.append(kept_values)
        own_rows = output
        if layer_idx + 1 < layers:
            full_low = widen_rows(output.astype(jnp.bfloat16))
    final_out = whole_rows(own_rows).reshape(seq_count, length, model_width)
    grad_own = own_part(cotangent.reshape(row_count, model_width).astype(jnp.float32))
    big_grads = [None] * layers
    sharded_grads = [None] * layers
    shared_grads = [None] * layers
    for layer_idx in range(layers - 1, -1, -1):
        params = tuple((stacked[layer_idx] for stacked in all_params))
        grad_own, big_layer, sharded_layer, shared_layer = layer_backward(
            grad_own, kept_layers[layer_idx], params, segment_ids, reduce_rows, widen_rows
        )
        big_grads[layer_idx] = big_layer
        sharded_grads[layer_idx] = sharded_layer
        shared_grads[layer_idx] = shared_layer
    input_grad = whole_rows(grad_own).reshape(seq_count, length, model_width)
    stacked_big = tuple(
        (
            jnp.stack([big_grads[layer_pos][member] for layer_pos in range(layers)])
            for member in range(4)
        )
    )
    stacked_big = (
        lax.psum_scatter(stacked_big[0], "dp", scatter_dimension=1, tiled=True),
        lax.psum_scatter(stacked_big[1], "dp", scatter_dimension=2, tiled=True),
        lax.psum_scatter(stacked_big[2], "dp", scatter_dimension=1, tiled=True),
        lax.psum_scatter(stacked_big[3], "dp", scatter_dimension=2, tiled=True),
    )
    whole_big = (
        lax.all_gather(stacked_big[0].astype(jnp.bfloat16), "dp", axis=1, tiled=True).astype(
            jnp.float32
        ),
        lax.all_gather(stacked_big[1].astype(jnp.bfloat16), "dp", axis=2, tiled=True).astype(
            jnp.float32
        ),
        lax.all_gather(stacked_big[2].astype(jnp.bfloat16), "dp", axis=1, tiled=True).astype(
            jnp.float32
        ),
        lax.all_gather(stacked_big[3].astype(jnp.bfloat16), "dp", axis=2, tiled=True).astype(
            jnp.float32
        ),
    )
    qv_stack = jnp.stack([sharded_grads[layer_pos][0] for layer_pos in range(layers)])
    up_stack = jnp.stack([sharded_grads[layer_pos][1] for layer_pos in range(layers)])
    shared_stack = tuple(
        (
            jnp.stack([shared_grads[layer_pos][member] for layer_pos in range(layers)])
            for member in range(6)
        )
    )
    local_width = qv_bias.shape[-1]
    local_hidden = up_bias.shape[-1]
    qv_pad = lax.dynamic_update_slice_in_dim(
        jnp.zeros((layers, 2, local_width * tensor_size), jnp.float32),
        qv_stack,
        tensor_pos * local_width,
        2,
    )
    up_pad = lax.dynamic_update_slice_in_dim(
        jnp.zeros((layers, local_hidden * tensor_size), jnp.float32),
        up_stack,
        tensor_pos * local_hidden,
        1,
    )
    totals = lax.psum(
        (
            qv_pad,
            up_pad,
            shared_stack[0],
            shared_stack[1],
            shared_stack[2],
            shared_stack[3],
            shared_stack[4],
            shared_stack[5],
        ),
        ("dp", "tensor"),
    )
    qv_total = lax.dynamic_slice_in_dim(totals[0], tensor_pos * local_width, local_width, 2)
    up_total = lax.dynamic_slice_in_dim(totals[1], tensor_pos * local_hidden, local_hidden, 1)
    return (
        final_out,
        input_grad,
        whole_big[0],
        qv_total,
        whole_big[1],
        totals[2],
        totals[3],
        totals[4],
        whole_big[2],
        up_total,
        whole_big[3],
        totals[5],
        totals[6],
        totals[7],
    )


def solution(mesh):
    return jax.shard_map(
        local,
        mesh=mesh,
        in_specs=(
            P("dp", None, None),
            P("dp", None),
            P("dp", None, None),
            P(None, None, None, "tensor"),
            P(None, None, "tensor"),
            P(None, "tensor", None),
            P(),
            P(),
            P(),
            P(None, None, "tensor"),
            P(None, "tensor"),
            P(None, "tensor", None),
            P(),
            P(),
            P(),
        ),
        out_specs=(
            P("dp", None, None),
            P("dp", None, None),
            P(None, None, None, "tensor"),
            P(None, None, "tensor"),
            P(None, "tensor", None),
            P(),
            P(),
            P(),
            P(None, None, "tensor"),
            P(None, "tensor"),
            P(None, "tensor", None),
            P(),
            P(),
            P(),
        ),
        check_vma=False,
    )
```

profile of v0, /device:TPU:0, one launch (start us, length us, event | category | flops | bytes accessed | tf_op | source)
XLA Modules:
  0.0 1131.4 jit_solution(13184422954730825900)
XLA Ops:
  8.0 3.2 fusion.131
  11.2 2.7 copy.61
  14.3 2.4 add_convert_fusion.3
  22.5 29.9 %reduce-scatter.13.cloned.1.call-done = bf16[128,1024]{1,0:T(8,128)(2,1)} async-done(((bf16[512,1024]{1,0:T(8,128)(2,1)}), bf16[128,1024]{1,0:T(8,128)(2,1)}) %reduce-scatter.13.cloned.1.call-update) | async-done | bytes 262160 | tf_op jit(solution)/shard_map/reduce_scatter | solution.py:242
  54.7 1.8 fusion.108
  56.6 26.7 %all-gather.14.cloned.1.call-done = bf16[512,1024]{1,0:T(8,128)(2,1)} async-done(((bf16[128,1024]{1,0:T(8,128)(2,1)}), bf16[512,1024]{1,0:T(8,128)(2,1)}) %all-gather.14.cloned.1.call-update) | async-done | bytes 1048592 | tf_op jit(solution)/shard_map/all_gather | solution.py:247
  83.3 8.6 multiply_convert_fusion.3
  92.9 2.2 fusion.55
  95.3 26.7 %reduce-scatter.15.cloned.1.call-done = bf16[128,1024]{1,0:T(8,128)(2,1)} async-done(((bf16[512,1024]{1,0:T(8,128)(2,1)}), bf16[128,1024]{1,0:T(8,128)(2,1)}) %reduce-scatter.15.cloned.1.call-update) | async-done | bytes 262160 | tf_op jit(solution)/shard_map/reduce_scatter | solution.py:242
  124.8 1.8 copy.62
  126.6 24.5 %all-gather.16.cloned.1.call-done = bf16[512,1024]{1,0:T(8,128)(2,1)} async-done(((bf16[128,1024]{1,0:T(8,128)(2,1)}), bf16[512,1024]{1,0:T(8,128)(2,1)}) %all-gather.16.cloned.1.call-update) | async-done | bytes 1048592 | tf_op jit(solution)/shard_map/all_gather | solution.py:247
  151.1 2.8 add_convert_fusion.2
  159.9 26.7 %reduce-scatter.17.cloned.1.call-done = bf16[128,1024]{1,0:T(8,128)(2,1)} async-done(((bf16[512,1024]{1,0:T(8,128)(2,1)}), bf16[128,1024]{1,0:T(8,128)(2,1)}) %reduce-scatter.17.cloned.1.call-update) | async-done | bytes 262160 | tf_op jit(solution)/shard_map/reduce_scatter | solution.py:242
  189.0 26.7 %all-gather.18.cloned.1.call-done = bf16[512,1024]{1,0:T(8,128)(2,1)} async-done(((bf16[128,1024]{1,0:T(8,128)(2,1)}), bf16[512,1024]{1,0:T(8,128)(2,1)}) %all-gather.18.cloned.1.call-update) | async-done | bytes 1048592 | tf_op jit(solution)/shard_map/all_gather | solution.py:247
  215.7 8.6 multiply_convert_fusion.2
  224.4 2.3 fusion.61
  226.7 26.7 %reduce-scatter.19.cloned.1.call-done = bf16[128,1024]{1,0:T(8,128)(2,1)} async-done(((bf16[512,1024]{1,0:T(8,128)(2,1)}), bf16[128,1024]{1,0:T(8,128)(2,1)}) %reduce-scatter.19.cloned.1.call-update) | async-done | bytes 262160 | tf_op jit(solution)/shard_map/reduce_scatter | solution.py:242
  256.2 1.9 fusion.125
  259.2 26.5 %all-gather.22.cloned.1.call-done = bf16[512,1024]{1,0:T(8,128)(2,1)} async-done(((bf16[128,1024]{1,0:T(8,128)(2,1)}), bf16[512,1024]{1,0:T(8,128)(2,1)}) %all-gather.22.cloned.1.call-update) | async-done | bytes 1048592 | tf_op jit(solution)/shard_map/all_gather | solution.py:247
  285.7 5.3 convert_reduce_fusion
  292.0 2.3 fusion.58
  294.4 26.7 %reduce-scatter.21.cloned.1.call-done = bf16[128,1024]{1,0:T(8,128)(2,1)} async-done(((bf16[512,1024]{1,0:T(8,128)(2,1)}), bf16[128,1024]{1,0:T(8,128)(2,1)}) %reduce-scatter.21.cloned.1.call-update) | async-done | bytes 262160 | tf_op jit(solution)/shard_map/reduce_scatter | solution.py:242
  324.6 26.7 %all-gather.24.cloned.1.call-done = bf16[512,1024]{1,0:T(8,128)(2,1)} async-done(((bf16[128,1024]{1,0:T(8,128)(2,1)}), bf16[512,1024]{1,0:T(8,128)(2,1)}) %all-gather.24.cloned.1.call-update) | async-done | bytes 1048592 | tf_op jit(solution)/shard_map/all_gather | solution.py:247
  351.3 1.8 convolution_convert_fusion.5
  353.1 3.4 multiply_reduce_fusion.1
  361.0 2.0 convolution_convert_fusion.1
  363.0 26.8 %reduce-scatter.23.cloned.1.call-done = bf16[128,1024]{1,0:T(8,128)(2,1)} async-done(((bf16[512,1024]{1,0:T(8,128)(2,1)}), bf16[128,1024]{1,0:T(8,128)(2,1)}) %reduce-scatter.23.cloned.1.call-update) | async-done | bytes 262160 | tf_op jit(solution)/shard_map/reduce_scatter | solution.py:242
  393.3 26.7 %all-gather.26.cloned.1.call-done = bf16[512,1024]{1,0:T(8,128)(2,1)} async-done(((bf16[128,1024]{1,0:T(8,128)(2,1)}), bf16[512,1024]{1,0:T(8,128)(2,1)}) %all-gather.26.cloned.1.call-update) | async-done | bytes 1048592 | tf_op jit(solution)/shard_map/all_gather | solution.py:247
  420.0 5.3 convert_reduce_fusion.1
  425.2 2.3 fusion.52
  427.8 26.5 %reduce-scatter.25.cloned.1.call-done = bf16[128,1024]{1,0:T(8,128)(2,1)} async-done(((bf16[512,1024]{1,0:T(8,128)(2,1)}), bf16[128,1024]{1,0:T(8,128)(2,1)}) %reduce-scatter.25.cloned.1.call-update) | async-done | bytes 262160 | tf_op jit(solution)/shard_map/reduce_scatter | solution.py:242
  457.9 26.7 %all-gather.28.cloned.1.call-done = bf16[512,1024]{1,0:T(8,128)(2,1)} async-done(((bf16[128,1024]{1,0:T(8,128)(2,1)}), bf16[512,1024]{1,0:T(8,128)(2,1)}) %all-gather.28.cloned.1.call-update) | async-done | bytes 1048592 | tf_op jit(solution)/shard_map/all_gather | solution.py:247
  484.6 1.7 convolution_convert_fusion.4
  486.3 3.3 multiply_reduce_fusion
  494.0 2.0 convolution_convert_fusion
  497.8 1.5 pad_maximum_fusion.3
  500.7 2.7 convolution_bitcast_fusion.4
  504.4 2.4 copy.50
  506.7 6.4 pad_maximum_fusion.2
  514.3 2.5 convolution_bitcast_fusion
  518.2 4.2 pad_maximum_fusion.1
  526.6 4.2 pad_maximum_fusion
  535.6 1.8 add_convert_fusion.4
  537.4 29.0 %reduce-scatter.31.cloned.1.call-done = f32[2,256,128]{2,1,0:T(8,128)} async-done(((f32[2,256,1024]{2,1,0:T(8,128)}), f32[2,256,128]{2,1,0:T(8,128)}) %reduce-scatter.31.cloned.1.call-update) | async-done | bytes 262160 | tf_op jit(solution)/shard_map/reduce_scatter | solution.py:306
  566.5 1.6 convert_element_type.335
  568.2 64.3 %reduce-scatter.29.cloned.1.call-done = f32[2,128,3,256]{3,1,2,0:T(8,128)} async-done(((f32[2,1024,3,256]{3,1,2,0:T(8,128)}), f32[2,128,3,256]{3,1,2,0:T(8,128)}) %reduce-scatter.29.cloned.1.call-update) | async-done | bytes 786448 | tf_op jit(solution)/shard_map/reduce_scatter | solution.py:305
  632.4 1.9 convert_element_type.331
  634.4 73.2 %reduce-scatter.35.cloned.1.call-done = f32[2,1024,128]{2,1,0:T(8,128)} async-done(((f32[2,1024,1024]{2,1,0:T(8,128)}), f32[2,1024,128]{2,1,0:T(8,128)}) %reduce-scatter.35.cloned.1.call-update) | async-done | bytes 1048592 | tf_op jit(solution)/shard_map/reduce_scatter | solution.py:308
  707.6 2.1 convert_element_type.343
  709.8 73.5 %reduce-scatter.33.cloned.1.call-done = f32[2,128,1024]{2,1,0:T(8,128)} async-done(((f32[2,1024,1024]{2,1,0:T(8,128)}), f32[2,128,1024]{2,1,0:T(8,128)}) %reduce-scatter.33.cloned.1.call-update) | async-done | bytes 1048592 | tf_op jit(solution)/shard_map/reduce_scatter | solution.py:307
  783.3 2.1 convert_element_type.339
  785.4 27.3 %all-gather.20.cloned.1.call-done = bf16[512,1024]{1,0:T(8,128)(2,1)} async-done(((bf16[128,1024]{1,0:T(8,128)(2,1)}), bf16[512,1024]{1,0:T(8,128)(2,1)}) %all-gather.20.cloned.1.call-update) | async-done | bytes 1048592 | tf_op jit(solution)/shard_map/all_gather | solution.py:253
  812.7 2.8 bitcast_convert_fusion.1
  815.5 128.1 %all-reduce.3.cloned.1.call-done = (f32[2,2,1024]{2,1,0:T(2,128)}, f32[2,1024]{1,0:T(2,128)}, f32[2,1024]{1,0:T(2,128)}, f32[2,1024]{1,0:T(2,128)}, f32[2,4096]{...) async-done(((f32[2,2,1024]{2,1,0:T(2,128)}, f32[2,1024]{1,0:T(2,128)}, f32[2,1024]{1,0:T(2,128)}, f32[2,1024]{1,0:T(2,128)}, ...) | async-done | bytes 98320 | tf_op jit(solution)/shard_map/psum | solution.py:346
  946.2 28.7 %all-gather.30.cloned.1.call-done = bf16[512,1024]{1,0:T(8,128)(2,1)} async-done(((bf16[128,1024]{1,0:T(8,128)(2,1)}), bf16[512,1024]{1,0:T(8,128)(2,1)}) %all-gather.30.cloned.1.call-update) | async-done | bytes 1048592 | tf_op jit(solution)/shard_map/all_gather | solution.py:253
  974.9 2.8 bitcast_convert_fusion
  977.6 22.9 %all-gather.34.cloned.1.call-done = bf16[2,256,1024]{2,1,0:T(8,128)(2,1)} async-done(((bf16[2,256,128]{2,1,0:T(8,128)(2,1)}), bf16[2,256,1024]{2,1,0:T(8,128)(2,1)}) %all-gather.34.cloned.1.call-update) | async-done | bytes 1048592 | tf_op jit(solution)/shard_map/all_gather | solution.py:314
  1000.6 2.8 convert_element_type.336
  1003.4 32.1 %all-gather.32.cloned.1.call-done = bf16[2,1024,3,256]{3,1,2,0:T(8,128)(2,1)} async-done(((bf16[2,128,3,256]{3,1,2,0:T(8,128)(2,1)}), bf16[2,1024,3,256]{3,1,2,0:T(8,128)(2,1)}) %all-gather.32.cloned.1.call-update) | async-done | bytes 3145744 | tf_op jit(solution)/shard_map/all_gather | solution.py:311
  1035.4 5.2 convert_element_type.332
  1040.6 34.3 %all-gather.38.cloned.1.call-done = bf16[2,1024,1024]{2,1,0:T(8,128)(2,1)} async-done(((bf16[2,1024,128]{2,1,0:T(8,128)(2,1)}), bf16[2,1024,1024]{2,1,0:T(8,128)(2,1)}) %all-gather.38.cloned.1.call-update) | async-done | bytes 4194320 | tf_op jit(solution)/shard_map/all_gather | solution.py:320
  1074.9 6.6 convert_element_type.344
  1081.6 32.6 %all-gather.36.cloned.1.call-done = bf16[2,1024,1024]{2,1,0:T(8,128)(2,1)} async-done(((bf16[2,128,1024]{2,1,0:T(8,128)(2,1)}), bf16[2,1024,1024]{2,1,0:T(8,128)(2,1)}) %all-gather.36.cloned.1.call-update) | async-done | bytes 4194320 | tf_op jit(solution)/shard_map/all_gather | solution.py:317
  1114.2 6.6 convert_element_type.340
  (274 shorter events, 67.9 us)
Async XLA Ops:
  7.2 45.2 %reduce-scatter.13.cloned.1.call-start = ((), (), s32[]{:S(2)}) async-start(), calls=%async_computation.12 | async-start | bytes 1310720 | tf_op jit(solution)/shard_map/reduce_scatter | solution.py:242
  11.2 2.7 copy-start.39
  11.2 3.1 copy-start.5
  14.1 2.6 copy-start.28
  17.7 2.0 copy-start
  20.5 36.0 %copy-start.16 = (bf16[4,64,512]{2,1,0:T(8,128)(2,1)}, bf16[4,64,512]{2,1,0:T(8,128)(2,1)S(1)}, u32[]{:S(2)}) copy-start(bf16[4,64,512]{2,1,0:T(8,128)(2,1)S(1)} %fusion.83) | copy-start | bytes 786436
  20.6 1.9 copy-start.34
  20.9 35.7 %copy-start.35 = (bf16[2,1024]{1,0:T(2,128)(2,1)S(1)}, bf16[2,1024]{1,0:T(2,128)(2,1)}, u32[]{:S(2)}) copy-start(bf16[2,1024]{1,0:T(2,128)(2,1)} %param.25) | copy-start | bytes 12292
  22.4 60.9 %all-gather.14.cloned.1.call-start = ((), (), s32[]{:S(2)}) async-start(), calls=%async_computation.13 | async-start | bytes 1310720 | tf_op jit(solution)/shard_map/all_gather | solution.py:247
  56.5 65.4 %reduce-scatter.15.cloned.1.call-start = ((), (), s32[]{:S(2)}) async-start(), calls=%async_computation.14 | async-start | bytes 1310720 | tf_op jit(solution)/shard_map/reduce_scatter | solution.py:242
  83.3 9.6 copy-start.46
  92.9 2.3 copy-start.36
  92.9 2.4 copy-start.37
  92.9 2.4 copy-start.38
  92.9 29.1 %copy-start.4 = (bf16[128,1024]{1,0:T(8,128)(2,1)S(1)}, bf16[128,1024]{1,0:T(8,128)(2,1)}, u32[]{:S(2)}) copy-start(bf16[128,1024]{1,0:T(8,128)(2,1)} %reduce-scatter.13.cloned.1.call-done) | copy-start | bytes 786436
  95.2 55.9 %all-gather.16.cloned.1.call-start = ((), (), s32[]{:S(2)}) async-start(), calls=%async_computation.15 | async-start | bytes 1310720 | tf_op jit(solution)/shard_map/all_gather | solution.py:247
  124.3 62.3 %reduce-scatter.17.cloned.1.call-start = ((), (), s32[]{:S(2)}) async-start(), calls=%async_computation.16 | async-start | bytes 1310720 | tf_op jit(solution)/shard_map/reduce_scatter | solution.py:242
  151.1 2.8 copy-start.29
  154.8 2.0 copy-start.2
  159.8 55.9 %all-gather.18.cloned.1.call-start = ((), (), s32[]{:S(2)}) async-start(), calls=%async_computation.17 | async-start | bytes 1310720 | tf_op jit(solution)/shard_map/all_gather | solution.py:247
  189.0 64.5 %reduce-scatter.19.cloned.1.call-start = ((), (), s32[]{:S(2)}) async-start(), calls=%async_computation.18 | async-start | bytes 1310720 | tf_op jit(solution)/shard_map/reduce_scatter | solution.py:242
  215.7 8.6 copy-start.47
  224.3 2.3 copy-start.57
  226.7 59.0 %all-gather.22.cloned.1.call-start = ((), (), s32[]{:S(2)}) async-start(), calls=%async_computation.20 | async-start | bytes 1310720 | tf_op jit(solution)/shard_map/all_gather | solution.py:247
  259.0 62.2 %reduce-scatter.21.cloned.1.call-start = ((), (), s32[]{:S(2)}) async-start(), calls=%async_computation.21 | async-start | bytes 1310720 | tf_op jit(solution)/shard_map/reduce_scatter | solution.py:242
  285.7 6.3 copy-start.48
  294.3 57.0 %all-gather.24.cloned.1.call-start = ((), (), s32[]{:S(2)}) async-start(), calls=%async_computation.22 | async-start | bytes 1310720 | tf_op jit(solution)/shard_map/all_gather | solution.py:247
  324.6 65.2 %reduce-scatter.23.cloned.1.call-start = ((), (), s32[]{:S(2)}) async-start(), calls=%async_computation.23 | async-start | bytes 1310720 | tf_op jit(solution)/shard_map/reduce_scatter | solution.py:242
  353.1 3.5 copy-start.3
  363.0 57.0 %all-gather.26.cloned.1.call-start = ((), (), s32[]{:S(2)}) async-start(), calls=%async_computation.24 | async-start | bytes 1310720 | tf_op jit(solution)/shard_map/all_gather | solution.py:247
  393.2 61.1 %reduce-scatter.25.cloned.1.call-start = ((), (), s32[]{:S(2)}) async-start(), calls=%async_computation.25 | async-start | bytes 1310720 | tf_op jit(solution)/shard_map/reduce_scatter | solution.py:242
  420.0 5.3 copy-start.49
  425.2 2.3 copy-start.60
  427.5 57.0 %copy-start.15 = (bf16[2,256,1024]{2,1,0:T(8,128)(2,1)S(1)}, bf16[2,256,1024]{2,1,0:T(8,128)(2,1)}, u32[]{:S(2)}) copy-start(bf16[2,256,1024]{2,1,0:T(8,128)(2,1)} %param.20) | copy-start | bytes 3145732
  427.5 57.0 %all-gather.28.cloned.1.call-start = ((), (), s32[]{:S(2)}) async-start(), calls=%async_computation.26 | async-start | bytes 1310720 | tf_op jit(solution)/shard_map/all_gather | solution.py:247
  457.0 32.6 %copy-start.9 = (f32[128,1024]{1,0:T(8,128)}, f32[128,1024]{1,0:T(8,128)S(1)}, u32[]{:S(2)}) copy-start(f32[128,1024]{1,0:T(8,128)S(1)} %get-tuple-element.136) | copy-start | bytes 1572868
  457.0 29.3 %copy-start.23 = (bf16[512,3,256]{0,2,1:T(8,128)(2,1)S(1)}, bf16[512,3,256]{0,2,1:T(8,128)(2,1)}, u32[]{:S(2)}) copy-start(bf16[512,3,256]{0,2,1:T(8,128)(2,1)} %copy-done.22) | copy-start | bytes 2359300
  457.9 77.7 %reduce-scatter.27.cloned.1.call-start = ((), (), s32[]{:S(2)}) async-start(), calls=%async_computation.27 | async-start | bytes 1310720 | tf_op jit(solution)/shard_map/reduce_scatter | solution.py:242
  486.3 3.5 copy-start.1
  494.0 2.1 copy-start.19
  494.0 2.1 copy-start.20
  496.0 70.4 %reduce-scatter.31.cloned.1.call-start = ((), (), s32[]{:S(2)}) async-start(), calls=%async_computation.31 | async-start | bytes 2359296 | tf_op jit(solution)/shard_map/reduce_scatter | solution.py:306
  499.3 133.2 %reduce-scatter.29.cloned.1.call-start = ((), (), s32[]{:S(2)}) async-start(), calls=%async_computation.29 | async-start | bytes 7077888 | tf_op jit(solution)/shard_map/reduce_scatter | solution.py:305
  500.7 2.7 copy-start.6
  500.7 2.7 copy-start.8
  513.1 3.7 copy-start.54
  513.2 3.7 copy-start.56
  513.2 194.5 %reduce-scatter.35.cloned.1.call-start = ((), (), s32[]{:S(2)}) async-start(), calls=%async_computation.35 | async-start | bytes 9437184 | tf_op jit(solution)/shard_map/reduce_scatter | solution.py:308
  522.5 2.8 copy-start.50
  522.5 260.9 %reduce-scatter.33.cloned.1.call-start = ((), (), s32[]{:S(2)}) async-start(), calls=%async_computation.33 | async-start | bytes 9437184 | tf_op jit(solution)/shard_map/reduce_scatter | solution.py:307
  530.9 4.7 copy-start.10
  530.9 281.8 %all-gather.20.cloned.1.call-start = ((), (), s32[]{:S(2)}) async-start(), calls=%async_computation.19 | async-start | bytes 1310720 | tf_op jit(solution)/shard_map/all_gather | solution.py:253
  531.5 412.1 %all-reduce.3.cloned.1.call-start = ((), (), s32[]{:S(2)}) async-start(), calls=%async_computation.37 | async-start | bytes 196608 | tf_op jit(solution)/shard_map/psum | solution.py:346
  535.5 439.4 %all-gather.30.cloned.1.call-start = ((), (), s32[]{:S(2)}) async-start(), calls=%async_computation.28 | async-start | bytes 1310720 | tf_op jit(solution)/shard_map/all_gather | solution.py:253
  537.4 463.2 %all-gather.34.cloned.1.call-start = ((), (), s32[]{:S(2)}) async-start(), calls=%async_computation.32 | async-start | bytes 1179648 | tf_op jit(solution)/shard_map/all_gather | solution.py:314
  568.1 467.3 %all-gather.32.cloned.1.call-start = ((), (), s32[]{:S(2)}) async-start(), calls=%async_computation.30 | async-start | bytes 3538944 | tf_op jit(solution)/shard_map/all_gather | solution.py:311
  634.4 440.5 %all-gather.38.cloned.1.call-start = ((), (), s32[]{:S(2)}) async-start(), calls=%async_computation.36 | async-start | bytes 4718592 | tf_op jit(solution)/shard_map/all_gather | solution.py:320
  709.8 404.4 %all-gather.36.cloned.1.call-start = ((), (), s32[]{:S(2)}) async-start(), calls=%async_computation.34 | async-start | bytes 4718592 | tf_op jit(solution)/shard_map/all_gather | solution.py:317
  1081.5 39.2 %copy-start.45 = (f32[2,1024]{1,0:T(2,128)S(1)}, f32[2,1024]{1,0:T(2,128)}, u32[]{:S(2)}) copy-start(f32[2,1024]{1,0:T(2,128)} %get-tuple-element.207) | copy-start | bytes 24580
  1081.6 39.8 %copy-start.44 = (f32[2,1024]{1,0:T(2,128)S(1)}, f32[2,1024]{1,0:T(2,128)}, u32[]{:S(2)}) copy-start(f32[2,1024]{1,0:T(2,128)} %get-tuple-element.208) | copy-start | bytes 24580
  1081.6 40.4 %copy-start.43 = (f32[2,1024]{1,0:T(2,128)S(1)}, f32[2,1024]{1,0:T(2,128)}, u32[]{:S(2)}) copy-start(f32[2,1024]{1,0:T(2,128)} %get-tuple-element.209) | copy-start | bytes 24580
  1081.6 41.0 %copy-start.42 = (f32[2,1024]{1,0:T(2,128)S(1)}, f32[2,1024]{1,0:T(2,128)}, u32[]{:S(2)}) copy-start(f32[2,1024]{1,0:T(2,128)} %get-tuple-element.213) | copy-start | bytes 24580
  1081.6 41.6 %copy-start.41 = (f32[2,1024]{1,0:T(2,128)S(1)}, f32[2,1024]{1,0:T(2,128)}, u32[]{:S(2)}) copy-start(f32[2,1024]{1,0:T(2,128)} %get-tuple-element.214) | copy-start | bytes 24580
  1081.6 42.2 %copy-start.40 = (f32[2,1024]{1,0:T(2,128)S(1)}, f32[2,1024]{1,0:T(2,128)}, u32[]{:S(2)}) copy-start(f32[2,1024]{1,0:T(2,128)} %get-tuple-element.215) | copy-start | bytes 24580
  (24 other events, 31.4 us)
Sparse Core Ops, SparseCore 0:
  22.5 29.8 reduce-scatter.12
  56.6 26.5 all-gather.13
  95.3 26.6 reduce-scatter.14
  124.4 26.5 all-gather.15
  160.0 26.6 reduce-scatter.16
  189.1 26.5 all-gather.17
  226.8 26.6 reduce-scatter.18
  259.1 26.5 all-gather.21
  294.4 26.6 reduce-scatter.20
  324.7 26.5 all-gather.23
  363.1 26.6 reduce-scatter.22
  393.3 26.5 all-gather.25
  427.7 26.6 reduce-scatter.24
  458.0 26.5 all-gather.27
  496.2 26.6 reduce-scatter.26
  526.5 39.8 reduce-scatter.30
  570.7 61.7 reduce-scatter.28
  636.3 71.2 reduce-scatter.34
  712.1 71.2 reduce-scatter.32
  784.7 27.9 all-gather.19
  820.3 123.2 all-reduce.2
  945.9 28.9 all-gather.29
  977.5 23.0 all-gather.33
  1003.1 32.3 all-gather.31
  1037.4 37.4 all-gather.37
  1077.4 36.7 all-gather.35
where the time goes:
time: 1140 us; the launch traced here: 1130 us
  waiting for transfers between devices  921 us (81%)
  other arithmetic  84.5 us (7%)
  matrix products  77.5 us (7%)
  local copies, waits for them, and re-layouts  30.6 us (3%)
  between operations  15.3 us (1%)
    reduce_scatter x8, waiting for transfers between devices, reduce_rows(): lax.psum_scatter(partial_sum.astype(jnp.bfloat16), 'tensor', scatter_dime...  190 us
    all_gather x7, waiting for transfers between devices, widen_rows(): return lax.all_gather(low_rows, 'tensor', axis=0, tiled=True)  184 us
    psum x1, waiting for transfers between devices, local(): lax.psum((qv_pad, up_pad, shared_stack[0], shared_stack[1], shared_stack[...  128 us
    reduce_scatter x1, waiting for transfers between devices, local(): lax.psum_scatter(stacked_big[2], 'dp', scatter_dimension=1, tiled=True)  73.5 us
    reduce_scatter x1, waiting for transfers between devices, local(): lax.psum_scatter(stacked_big[3], 'dp', scatter_dimension=2, tiled=True)  73.2 us
    reduce_scatter x1, waiting for transfers between devices, local(): lax.psum_scatter(stacked_big[0], 'dp', scatter_dimension=1, tiled=True)  64.3 us
    all_gather x2, waiting for transfers between devices, whole_rows(): lax.all_gather(part_rows.astype(jnp.bfloat16), 'tensor', axis=0, tiled=True)  55.9 us
    all_gather x1, waiting for transfers between devices, local(): lax.all_gather(stacked_big[3].astype(jnp.bfloat16), 'dp', axis=2, tiled=T...  34.3 us
  transfers between devices with their start and end apart: 26, of which 25 were waited for; matrix products, arithmetic and copies ran while one was open for 6% of the time, Pallas kernels for 0%

commit v1 on v0

--- a/solution.py
+++ b/solution.py
@@ -253,6 +253,19 @@
         return lax.all_gather(part_rows.astype(jnp.bfloat16), "tensor", axis=0, tiled=True).astype(
             part_rows.dtype
         )
+
+    def whole_grads(grads):
+        low = [g.astype(jnp.bfloat16).reshape(-1, model_width) for g in grads]
+        rows = [g.shape[0] for g in low]
+        share = lax.psum_scatter(
+            jnp.concatenate(low), "dp", scatter_dimension=0, tiled=True
+        )
+        whole = lax.all_gather(share, "dp", axis=0, tiled=True)
+        parts, at = [], 0
+        for g, count in zip(grads, rows):
+            parts.append(whole[at : at + count].reshape(g.shape))
+            at += count
+        return parts
 
     all_params = (
         qkv_weight,
@@ -295,84 +308,46 @@
         sharded_grads[layer_idx] = sharded_layer
         shared_grads[layer_idx] = shared_layer
     input_grad = whole_rows(grad_own).reshape(seq_count, length, model_width)
-    stacked_big = tuple(
-        (
-            jnp.stack([big_grads[layer_pos][member] for layer_pos in range(layers)])
-            for member in range(4)
-        )
-    )
-    stacked_big = (
-        lax.psum_scatter(stacked_big[0], "dp", scatter_dimension=1, tiled=True),
-        lax.psum_scatter(stacked_big[1], "dp", scatter_dimension=2, tiled=True),
-        lax.psum_scatter(stacked_big[2], "dp", scatter_dimension=1, tiled=True),
-        lax.psum_scatter(stacked_big[3], "dp", scatter_dimension=2, tiled=True),
-    )
-    whole_big = (
-        lax.all_gather(stacked_big[0].astype(jnp.bfloat16), "dp", axis=1, tiled=True).astype(
-            jnp.float32
-        ),
-        lax.all_gather(stacked_big[1].astype(jnp.bfloat16), "dp", axis=2, tiled=True).astype(
-            jnp.float32
-        ),
-        lax.all_gather(stacked_big[2].astype(jnp.bfloat16), "dp", axis=1, tiled=True).astype(
-            jnp.float32
-        ),
-        lax.all_gather(stacked_big[3].astype(jnp.bfloat16), "dp", axis=2, tiled=True).astype(
-            jnp.float32
-        ),
-    )
-    qv_stack = jnp.stack([sharded_grads[layer_pos][0] for layer_pos in range(layers)])
-    up_stack = jnp.stack([sharded_grads[layer_pos][1] for layer_pos in range(layers)])
-    shared_stack = tuple(
-        (
-            jnp.stack([shared_grads[layer_pos][member] for layer_pos in range(layers)])
+    layer_big = [whole_grads(big_grads[layer_pos]) for layer_pos in range(layers)]
+    whole_big = tuple(
+        jnp.stack([layer_big[layer_pos][member].astype(jnp.float32) for layer_pos in range(layers)])
+        for member in range(4)
+    )
+    sharded = jnp.concatenate(
+        [
+            jnp.stack([sharded_grads[p][0] for p in range(layers)]).reshape(-1),
+            jnp.stack([sharded_grads[p][1] for p in range(layers)]).reshape(-1),
+        ]
+    )
+    shared = jnp.concatenate(
+        [
+            jnp.stack([shared_grads[p][member] for p in range(layers)]).reshape(-1)
             for member in range(6)
-        )
-    )
+        ]
+    )
+    tensor_sums = lax.all_gather(shared, "tensor").sum(axis=0)
+    totals = lax.all_gather(jnp.concatenate([sharded, tensor_sums]), "dp").sum(axis=0)
     local_width = qv_bias.shape[-1]
     local_hidden = up_bias.shape[-1]
-    qv_pad = lax.dynamic_update_slice_in_dim(
-        jnp.zeros((layers, 2, local_width * tensor_size), jnp.float32),
-        qv_stack,
-        tensor_pos * local_width,
-        2,
-    )
-    up_pad = lax.dynamic_update_slice_in_dim(
-        jnp.zeros((layers, local_hidden * tensor_size), jnp.float32),
-        up_stack,
-        tensor_pos * local_hidden,
-        1,
-    )
-    totals = lax.psum(
-        (
-            qv_pad,
-            up_pad,
-            shared_stack[0],
-            shared_stack[1],
-            shared_stack[2],
-            shared_stack[3],
-            shared_stack[4],
-            shared_stack[5],
-        ),
-        ("dp", "tensor"),
-    )
-    qv_total = lax.dynamic_slice_in_dim(totals[0], tensor_pos * local_width, local_width, 2)
-    up_total = lax.dynamic_slice_in_dim(totals[1], tensor_pos * local_hidden, local_hidden, 1)
+    at = layers * 2 * local_width
+    qv_total = totals[:at].reshape(layers, 2, local_width)
+    up_total = totals[at : at + layers * local_hidden].reshape(layers, local_hidden)
+    rest = totals[at + layers * local_hidden :].reshape(6, layers, model_width)
     return (
         final_out,
         input_grad,
         whole_big[0],
         qv_total,
         whole_big[1],
-        totals[2],
-        totals[3],
-        totals[4],
+        rest[0],
+        rest[1],
+        rest[2],
         whole_big[2],
         up_total,
         whole_big[3],
-        totals[5],
-        totals[6],
-        totals[7],
+        rest[3],
+        rest[4],
+        rest[5],
     )
 
 

time: 1140 us -> 852 us (0.75)
  waiting for transfers between devices: 921 us -> 600 us
  blocking collectives: 0 us -> 24.7 us
  local copies, waits for them, and re-layouts: 30.6 us -> 54.3 us
  other arithmetic: 84.5 us -> 62.1 us
    psum x1 -> x0, waiting for transfers between devices: 128 us -> none  [local(): lax.psum((qv_pad, up_pad, shared_stack[0], shared_stack[1], shared_stack[...]
    reduce_scatter x4 -> x2, waiting for transfers between devices: 240 us -> 117 us  [whole_grads(): lax.psum_scatter(jnp.concatenate(low), 'dp', scatter_dimension=0, tiled=T...]
    all_gather x4 -> x2, waiting for transfers between devices: 122 us -> 80 us  [whole_grads(): whole = lax.all_gather(share, 'dp', axis=0, tiled=True)]
    convert_element_type x8 -> x0, other arithmetic: 29 us -> none  [the longest x1 6.63 us: local(): lax.all_gather(stacked_big[3].astype(jnp.bfloat16), 'dp', axis=2, tiled=T...]
    all_gather x2, waiting for transfers between devices: 55.9 us -> 28.3 us  [whole_rows(): lax.all_gather(part_rows.astype(jnp.bfloat16), 'tensor', axis=0, tiled=True)]
    all_gather x0 -> x2, blocking collectives: none -> 24.7 us  [the longest x1 14.6 us: local(): tensor_sums = lax.all_gather(shared, 'tensor').sum(axis=0)]
  transfers between devices with their start and end apart: 26 -> 21, of which waited for: 25 -> 19; matrix products, arithmetic and copies ran while one was open for 6% -> 7% of each run, Pallas kernels for 0% -> 0%
where the time goes in v1:
time: 852 us; the launch traced here: 844 us
  waiting for transfers between devices  600 us (70%)
  matrix products  85.2 us (10%)
  other arithmetic  62.1 us (7%)
  local copies, waits for them, and re-layouts  54.3 us (6%)
  blocking collectives  24.7 us (3%)
  between operations  15.4 us (2%)
    reduce_scatter x8, waiting for transfers between devices, reduce_rows(): lax.psum_scatter(partial_sum.astype(jnp.bfloat16), 'tensor', scatter_dime...  190 us
    all_gather x7, waiting for transfers between devices, widen_rows(): return lax.all_gather(low_rows, 'tensor', axis=0, tiled=True)  184 us
    reduce_scatter x2, waiting for transfers between devices, whole_grads(): lax.psum_scatter(jnp.concatenate(low), 'dp', scatter_dimension=0, tiled=T...  117 us
    all_gather x2, waiting for transfers between devices, whole_grads(): whole = lax.all_gather(share, 'dp', axis=0, tiled=True)  80 us
    all_gather x2, waiting for transfers between devices, whole_rows(): lax.all_gather(part_rows.astype(jnp.bfloat16), 'tensor', axis=0, tiled=True)  28.3 us
    unnamed x112, local copies, waits for them, and re-layouts  18.1 us
    dot_general x2, matrix products, layer_forward(): jnp.dot(normed_low, up_w, preferred_element_type=jnp.float32)  17.2 us
  transfers between devices with their start and end apart: 21, of which 19 were waited for; matrix products, arithmetic and copies ran while one was open for 7% of the time, Pallas kernels for 0%

profile of v1, /device:TPU:0, one launch (start us, length us, event | category | flops | bytes accessed | tf_op | source)
XLA Modules:
  0.0 844.0 jit_solution(14296975973559238818)
XLA Ops:
  9.0 3.3 fusion.131
  12.3 2.7 copy.93
  15.1 2.4 add_convert_fusion.3
  22.1 1.4 convolution_convert_fusion.9
  23.7 29.9 %reduce-scatter.11.cloned.1.call-done = bf16[128,1024]{1,0:T(8,128)(2,1)} async-done(((bf16[512,1024]{1,0:T(8,128)(2,1)}), bf16[128,1024]{1,0:T(8,128)(2,1)}) %reduce-scatter.11.cloned.1.call-update) | async-done | bytes 262160 | tf_op jit(solution)/shard_map/reduce_scatter | solution.py:242
  55.8 1.8 fusion.109
  57.7 26.7 %all-gather.14.cloned.1.call-done = bf16[512,1024]{1,0:T(8,128)(2,1)} async-done(((bf16[128,1024]{1,0:T(8,128)(2,1)}), bf16[512,1024]{1,0:T(8,128)(2,1)}) %all-gather.14.cloned.1.call-update) | async-done | bytes 1048592 | tf_op jit(solution)/shard_map/all_gather | solution.py:247
  84.4 8.6 %multiply_convert_fusion.3 = (bf16[512,1024]{1,0:T(8,128)(2,1)S(1)}, f32[512,1024]{1,0:T(8,128)}, f32[512,1024]{1,0:T(8,128)}) fusion(f32[1024]{0:T(1024)S(1)} %bitcast.381, bf16[512,1024]{1,0:T(8,128)(2,1)} %all-gather.14.cloned.1.call-done, bf16[2,1024,1024]{2,1,0:T(8,128)(2,1)} %param.24), kind=kOutput, calls=%fused_computation.66 | convolution fusion | flops 1108344832 | bytes 8392704 | tf_op jit(solution)/shard_map/dot_general | solution.py:108
  94.0 2.2 fusion.55
  96.4 26.7 %reduce-scatter.13.cloned.1.call-done = bf16[128,1024]{1,0:T(8,128)(2,1)} async-done(((bf16[512,1024]{1,0:T(8,128)(2,1)}), bf16[128,1024]{1,0:T(8,128)(2,1)}) %reduce-scatter.13.cloned.1.call-update) | async-done | bytes 262160 | tf_op jit(solution)/shard_map/reduce_scatter | solution.py:242
  125.9 1.7 copy.94
  127.7 24.5 %all-gather.16.cloned.1.call-done = bf16[512,1024]{1,0:T(8,128)(2,1)} async-done(((bf16[128,1024]{1,0:T(8,128)(2,1)}), bf16[512,1024]{1,0:T(8,128)(2,1)}) %all-gather.16.cloned.1.call-update) | async-done | bytes 1048592 | tf_op jit(solution)/shard_map/all_gather | solution.py:247
  152.2 2.8 add_convert_fusion.2
  160.7 26.7 %reduce-scatter.15.cloned.1.call-done = bf16[128,1024]{1,0:T(8,128)(2,1)} async-done(((bf16[512,1024]{1,0:T(8,128)(2,1)}), bf16[128,1024]{1,0:T(8,128)(2,1)}) %reduce-scatter.15.cloned.1.call-update) | async-done | bytes 262160 | tf_op jit(solution)/shard_map/reduce_scatter | solution.py:242
  189.8 26.7 %all-gather.18.cloned.1.call-done = bf16[512,1024]{1,0:T(8,128)(2,1)} async-done(((bf16[128,1024]{1,0:T(8,128)(2,1)}), bf16[512,1024]{1,0:T(8,128)(2,1)}) %all-gather.18.cloned.1.call-update) | async-done | bytes 1048592 | tf_op jit(solution)/shard_map/all_gather | solution.py:247
  216.5 8.6 %multiply_convert_fusion.2 = (bf16[512,1024]{1,0:T(8,128)(2,1)S(1)}, f32[512,1024]{1,0:T(8,128)}, f32[512,1024]{1,0:T(8,128)}) fusion(f32[1024]{0:T(1024)S(1)} %bitcast.384, bf16[512,1024]{1,0:T(8,128)(2,1)} %all-gather.18.cloned.1.call-done, bf16[2,1024,1024]{2,1,0:T(8,128)(2,1)} %param.24), kind=kOutput, calls=%fused_computation.53 | convolution fusion | flops 1108344832 | bytes 8392704 | tf_op jit(solution)/shard_map/dot_general | solution.py:108
  225.1 2.3 fusion.61
  227.5 26.7 %reduce-scatter.17.cloned.1.call-done = bf16[128,1024]{1,0:T(8,128)(2,1)} async-done(((bf16[512,1024]{1,0:T(8,128)(2,1)}), bf16[128,1024]{1,0:T(8,128)(2,1)}) %reduce-scatter.17.cloned.1.call-update) | async-done | bytes 262160 | tf_op jit(solution)/shard_map/reduce_scatter | solution.py:242
  257.0 1.9 fusion.125
  260.0 26.5 %all-gather.22.cloned.1.call-done = bf16[512,1024]{1,0:T(8,128)(2,1)} async-done(((bf16[128,1024]{1,0:T(8,128)(2,1)}), bf16[512,1024]{1,0:T(8,128)(2,1)}) %all-gather.22.cloned.1.call-update) | async-done | bytes 1048592 | tf_op jit(solution)/shard_map/all_gather | solution.py:247
  286.5 5.2 convert_reduce_fusion
  292.7 2.3 fusion.58
  295.0 26.7 %reduce-scatter.19.cloned.1.call-done = bf16[128,1024]{1,0:T(8,128)(2,1)} async-done(((bf16[512,1024]{1,0:T(8,128)(2,1)}), bf16[128,1024]{1,0:T(8,128)(2,1)}) %reduce-scatter.19.cloned.1.call-update) | async-done | bytes 262160 | tf_op jit(solution)/shard_map/reduce_scatter | solution.py:242
  325.3 26.7 %all-gather.24.cloned.1.call-done = bf16[512,1024]{1,0:T(8,128)(2,1)} async-done(((bf16[128,1024]{1,0:T(8,128)(2,1)}), bf16[512,1024]{1,0:T(8,128)(2,1)}) %all-gather.24.cloned.1.call-update) | async-done | bytes 1048592 | tf_op jit(solution)/shard_map/all_gather | solution.py:247
  352.0 1.9 convolution_convert_fusion.13
  353.9 3.1 fusion.73
  361.8 2.0 convolution_convert_fusion.7
  363.9 26.8 %reduce-scatter.21.cloned.1.call-done = bf16[128,1024]{1,0:T(8,128)(2,1)} async-done(((bf16[512,1024]{1,0:T(8,128)(2,1)}), bf16[128,1024]{1,0:T(8,128)(2,1)}) %reduce-scatter.21.cloned.1.call-update) | async-done | bytes 262160 | tf_op jit(solution)/shard_map/reduce_scatter | solution.py:242
  394.1 26.7 %all-gather.26.cloned.1.call-done = bf16[512,1024]{1,0:T(8,128)(2,1)} async-done(((bf16[128,1024]{1,0:T(8,128)(2,1)}), bf16[512,1024]{1,0:T(8,128)(2,1)}) %all-gather.26.cloned.1.call-update) | async-done | bytes 1048592 | tf_op jit(solution)/shard_map/all_gather | solution.py:247
  420.8 5.3 convert_reduce_fusion.1
  426.1 2.3 fusion.52
  428.8 26.3 %reduce-scatter.23.cloned.1.call-done = bf16[128,1024]{1,0:T(8,128)(2,1)} async-done(((bf16[512,1024]{1,0:T(8,128)(2,1)}), bf16[128,1024]{1,0:T(8,128)(2,1)}) %reduce-scatter.23.cloned.1.call-update) | async-done | bytes 262160 | tf_op jit(solution)/shard_map/reduce_scatter | solution.py:242
  458.8 26.7 %all-gather.28.cloned.1.call-done = bf16[512,1024]{1,0:T(8,128)(2,1)} async-done(((bf16[128,1024]{1,0:T(8,128)(2,1)}), bf16[512,1024]{1,0:T(8,128)(2,1)}) %all-gather.28.cloned.1.call-update) | async-done | bytes 1048592 | tf_op jit(solution)/shard_map/all_gather | solution.py:247
  485.5 1.8 convolution_convert_fusion.12
  487.3 3.1 fusion.87
  495.2 2.0 convolution_convert_fusion.6
  497.3 4.0 convolution_convert_fusion
  501.2 2.6 convolution_convert_fusion.1
  506.3 2.9 reshape.505
  509.1 1.8 convolution_convert_fusion.10
  510.9 5.4 pad_maximum_fusion.1
  517.6 3.9 convolution_convert_fusion.2
  521.5 2.6 convolution_convert_fusion.3
  527.1 1.7 convolution_convert_fusion.11
  528.8 5.5 pad_maximum_fusion
  535.3 1.8 add_convert_fusion.4
  537.2 51.0 %reduce-scatter.29.cloned.1.call-done = bf16[384,1024]{1,0:T(8,128)(2,1)} async-done(((bf16[3072,1024]{1,0:T(8,128)(2,1)}), bf16[384,1024]{1,0:T(8,128)(2,1)}) %reduce-scatter.29.cloned.1.call-update) | async-done | bytes 786448 | tf_op jit(solution)/shard_map/reduce_scatter | solution.py:260
  588.3 65.9 %reduce-scatter.27.cloned.1.call-done = bf16[384,1024]{1,0:T(8,128)(2,1)} async-done(((bf16[3072,1024]{1,0:T(8,128)(2,1)}), bf16[384,1024]{1,0:T(8,128)(2,1)}) %reduce-scatter.27.cloned.1.call-update) | async-done | bytes 786448 | tf_op jit(solution)/shard_map/reduce_scatter | solution.py:260
  655.2 28.3 %all-gather.20.cloned.1.call-done = bf16[512,1024]{1,0:T(8,128)(2,1)} async-done(((bf16[128,1024]{1,0:T(8,128)(2,1)}), bf16[512,1024]{1,0:T(8,128)(2,1)}) %all-gather.20.cloned.1.call-update) | async-done | bytes 1048592 | tf_op jit(solution)/shard_map/all_gather | solution.py:253
  683.5 2.8 bitcast_convert_fusion.1
  686.7 14.6 %all-gather = f32[49152]{0:T(1024)S(1)} all-gather(f32[12288]{0:T(1024)S(1)} %bitcast_dynamic-update-slice_fusion), channel_id=2, replica_groups=mesh['dp'=8,'tensor'=4] {'tensor'}, dimensions={0}, use_global_device_ids=true | all-gather | bytes 245760 | tf_op jit(solution)/shard_map/all_gather | solution.py:328
  701.7 10.1 %all-gather.1 = f32[122880]{0:T(1024)S(1)} all-gather(f32[15360]{0:T(1024)S(1)} %pad_maximum_fusion.3), channel_id=3, replica_groups=mesh['dp'=8,'tensor'=4] {'dp'}, dimensions={0}, use_global_device_ids=true | all-gather | bytes 552960 | tf_op jit(solution)/shard_map/all_gather | solution.py:329
  716.9 2.8 bitcast_convert_fusion
  719.7 41.3 %all-gather.34.cloned.1.call-done = bf16[3072,1024]{1,0:T(8,128)(2,1)} async-done(((bf16[384,1024]{1,0:T(8,128)(2,1)}), bf16[3072,1024]{1,0:T(8,128)(2,1)}) %all-gather.34.cloned.1.call-update) | async-done | bytes 6291472 | tf_op jit(solution)/shard_map/all_gather | solution.py:263
  762.4 2.3 convert_element_type.377
  765.7 4.0 slice_bitcast_fusion
  769.7 38.7 %all-gather.32.cloned.1.call-done = bf16[3072,1024]{1,0:T(8,128)(2,1)} async-done(((bf16[384,1024]{1,0:T(8,128)(2,1)}), bf16[3072,1024]{1,0:T(8,128)(2,1)}) %all-gather.32.cloned.1.call-update) | async-done | bytes 6291472 | tf_op jit(solution)/shard_map/all_gather | solution.py:263
  808.4 2.7 slice.371
  811.1 5.2 convert_element_type.372
  816.3 4.9 maximum_convert_fusion
  821.2 3.9 copy.82
  826.2 1.5 maximum_convert_fusion.4
  827.6 2.8 slice_bitcast_fusion.1
  830.5 6.5 maximum_convert_fusion.1
  (261 shorter events, 64.3 us)
Async XLA Ops:
  7.2 46.3 %reduce-scatter.11.cloned.1.call-start = ((), (), s32[]{:S(2)}) async-start(), calls=%async_computation.10 | async-start | bytes 1310720 | tf_op jit(solution)/shard_map/reduce_scatter | solution.py:242
  9.0 8.6 %copy-start.27 = (pred[512,512]{0,1:T(8,128)(4,1)}, pred[512,512]{0,1:T(8,128)(4,1)S(1)}, u32[]{:S(2)}) copy-start(pred[512,512]{0,1:T(8,128)(4,1)S(1)} %broadcast_compare_fusion) | copy-start | bytes 786436
  12.3 2.8 copy-start.9
  17.6 1.5 copy-start.19
  18.5 2.0 copy-start
  20.5 1.6 copy-start.12
  21.4 2.2 copy-start.29
  21.4 2.2 copy-start.30
  21.4 2.2 copy-start.31
  22.1 35.6 %copy-start.32 = (bf16[2,1024]{1,0:T(2,128)(2,1)S(1)}, bf16[2,1024]{1,0:T(2,128)(2,1)}, u32[]{:S(2)}) copy-start(bf16[2,1024]{1,0:T(2,128)(2,1)} %param.25) | copy-start | bytes 12292
  23.5 60.9 %all-gather.14.cloned.1.call-start = ((), (), s32[]{:S(2)}) async-start(), calls=%async_computation.11 | async-start | bytes 1310720 | tf_op jit(solution)/shard_map/all_gather | solution.py:247
  57.6 65.4 %reduce-scatter.13.cloned.1.call-start = ((), (), s32[]{:S(2)}) async-start(), calls=%async_computation.12 | async-start | bytes 1310720 | tf_op jit(solution)/shard_map/reduce_scatter | solution.py:242
  84.4 9.6 %copy-start.36 = (bf16[2,1024,1024]{2,1,0:T(8,128)(2,1)S(1)}, bf16[2,1024,1024]{2,1,0:T(8,128)(2,1)}, u32[]{:S(2)}) copy-start(bf16[2,1024,1024]{2,1,0:T(8,128)(2,1)} %param.26) | copy-start | bytes 12582916
  94.0 2.3 copy-start.33
  94.0 2.4 copy-start.34
  94.0 2.4 copy-start.35
  94.0 29.1 %copy-start.4 = (bf16[128,1024]{1,0:T(8,128)(2,1)S(1)}, bf16[128,1024]{1,0:T(8,128)(2,1)}, u32[]{:S(2)}) copy-start(bf16[128,1024]{1,0:T(8,128)(2,1)} %reduce-scatter.11.cloned.1.call-done) | copy-start | bytes 786436
  96.3 55.9 %all-gather.16.cloned.1.call-start = ((), (), s32[]{:S(2)}) async-start(), calls=%async_computation.13 | async-start | bytes 1310720 | tf_op jit(solution)/shard_map/all_gather | solution.py:247
  125.4 62.0 %reduce-scatter.15.cloned.1.call-start = ((), (), s32[]{:S(2)}) async-start(), calls=%async_computation.14 | async-start | bytes 1310720 | tf_op jit(solution)/shard_map/reduce_scatter | solution.py:242
  152.2 2.8 copy-start.28
  155.0 1.5 copy-start.21
  155.9 2.0 copy-start.2
  158.8 29.8 %copy-start.17 = (bf16[4,64,512]{2,1,0:T(8,128)(2,1)}, bf16[4,64,512]{2,1,0:T(8,128)(2,1)S(1)}, u32[]{:S(2)}) copy-start(bf16[4,64,512]{2,1,0:T(8,128)(2,1)S(1)} %fusion.83) | copy-start | bytes 786436
  160.6 55.9 %all-gather.18.cloned.1.call-start = ((), (), s32[]{:S(2)}) async-start(), calls=%async_computation.15 | async-start | bytes 1310720 | tf_op jit(solution)/shard_map/all_gather | solution.py:247
  189.7 64.5 %reduce-scatter.17.cloned.1.call-start = ((), (), s32[]{:S(2)}) async-start(), calls=%async_computation.16 | async-start | bytes 1310720 | tf_op jit(solution)/shard_map/reduce_scatter | solution.py:242
  216.5 8.6 %copy-start.37 = (bf16[2,1024,1024]{2,1,0:T(8,128)(2,1)S(1)}, bf16[2,1024,1024]{2,1,0:T(8,128)(2,1)}, u32[]{:S(2)}) copy-start(bf16[2,1024,1024]{2,1,0:T(8,128)(2,1)} %param.26) | copy-start | bytes 12582916
  225.1 2.3 copy-start.46
  227.5 59.0 %all-gather.22.cloned.1.call-start = ((), (), s32[]{:S(2)}) async-start(), calls=%async_computation.18 | async-start | bytes 1310720 | tf_op jit(solution)/shard_map/all_gather | solution.py:247
  259.7 62.1 %reduce-scatter.19.cloned.1.call-start = ((), (), s32[]{:S(2)}) async-start(), calls=%async_computation.19 | async-start | bytes 1310720 | tf_op jit(solution)/shard_map/reduce_scatter | solution.py:242
  286.5 6.2 copy-start.38
  295.0 57.0 %all-gather.24.cloned.1.call-start = ((), (), s32[]{:S(2)}) async-start(), calls=%async_computation.20 | async-start | bytes 1310720 | tf_op jit(solution)/shard_map/all_gather | solution.py:247
  325.2 65.4 %reduce-scatter.21.cloned.1.call-start = ((), (), s32[]{:S(2)}) async-start(), calls=%async_computation.21 | async-start | bytes 1310720 | tf_op jit(solution)/shard_map/reduce_scatter | solution.py:242
  352.0 5.0 copy-start.22
  353.9 3.5 copy-start.3
  360.3 1.6 copy-start.11
  363.8 57.0 %all-gather.26.cloned.1.call-start = ((), (), s32[]{:S(2)}) async-start(), calls=%async_computation.22 | async-start | bytes 1310720 | tf_op jit(solution)/shard_map/all_gather | solution.py:247
  394.1 61.1 %reduce-scatter.23.cloned.1.call-start = ((), (), s32[]{:S(2)}) async-start(), calls=%async_computation.23 | async-start | bytes 1310720 | tf_op jit(solution)/shard_map/reduce_scatter | solution.py:242
  420.8 5.3 copy-start.39
  426.1 2.3 copy-start.49
  428.4 57.1 %copy-start.14 = (bf16[2,256,1024]{2,1,0:T(8,128)(2,1)S(1)}, bf16[2,256,1024]{2,1,0:T(8,128)(2,1)}, u32[]{:S(2)}) copy-start(bf16[2,256,1024]{2,1,0:T(8,128)(2,1)} %param.20) | copy-start | bytes 3145732
  428.4 57.1 %all-gather.28.cloned.1.call-start = ((), (), s32[]{:S(2)}) async-start(), calls=%async_computation.24 | async-start | bytes 1310720 | tf_op jit(solution)/shard_map/all_gather | solution.py:247
  457.8 32.6 %copy-start.7 = (f32[128,1024]{1,0:T(8,128)}, f32[128,1024]{1,0:T(8,128)S(1)}, u32[]{:S(2)}) copy-start(f32[128,1024]{1,0:T(8,128)S(1)} %get-tuple-element.170) | copy-start | bytes 1572868
  458.7 76.2 %reduce-scatter.25.cloned.1.call-start = ((), (), s32[]{:S(2)}) async-start(), calls=%async_computation.25 | async-start | bytes 1310720 | tf_op jit(solution)/shard_map/reduce_scatter | solution.py:242
  485.5 4.9 copy-start.20
  487.3 3.5 copy-start.1
  493.6 1.6 copy-start.10
  495.2 2.1 copy-start.43
  497.2 4.1 copy-start.42
  497.2 91.0 %reduce-scatter.29.cloned.1.call-start = ((), (), s32[]{:S(2)}) async-start(), calls=%async_computation.29 | async-start | bytes 7077888 | tf_op jit(solution)/shard_map/reduce_scatter | solution.py:260
  497.2 4.0 copy-start.48
  501.2 2.6 copy-start.24
  501.2 2.6 copy-start.41
  506.3 2.9 copy-start.18
  509.1 1.8 copy-start.6
  516.4 5.1 copy-start.40
  516.4 137.8 %reduce-scatter.27.cloned.1.call-start = ((), (), s32[]{:S(2)}) async-start(), calls=%async_computation.27 | async-start | bytes 7077888 | tf_op jit(solution)/shard_map/reduce_scatter | solution.py:260
  517.6 3.9 copy-start.50
  521.5 2.6 copy-start.26
  534.3 149.3 %all-gather.20.cloned.1.call-start = ((), (), s32[]{:S(2)}) async-start(), calls=%async_computation.17 | async-start | bytes 1310720 | tf_op jit(solution)/shard_map/all_gather | solution.py:253
  534.9 182.1 %all-gather.30.cloned.1.call-start = ((), (), s32[]{:S(2)}) async-start(), calls=%async_computation.26 | async-start | bytes 1310720 | tf_op jit(solution)/shard_map/all_gather | solution.py:253
  537.2 223.8 %all-gather.34.cloned.1.call-start = ((), (), s32[]{:S(2)}) async-start(), calls=%async_computation.30 | async-start | bytes 7077888 | tf_op jit(solution)/shard_map/all_gather | solution.py:263
  588.3 220.2 %all-gather.32.cloned.1.call-start = ((), (), s32[]{:S(2)}) async-start(), calls=%async_computation.28 | async-start | bytes 7077888 | tf_op jit(solution)/shard_map/all_gather | solution.py:263
  761.0 1.4 slice-start
  827.6 2.9 copy-start.5
  (9 other events, 9.2 us)
Sparse Core Ops, SparseCore 0:
  23.6 29.8 reduce-scatter.10
  57.8 26.5 all-gather.13
  96.4 26.6 reduce-scatter.12
  125.6 26.5 all-gather.15
  160.7 26.6 reduce-scatter.14
  189.9 26.5 all-gather.17
  227.6 26.6 reduce-scatter.16
  259.8 26.5 all-gather.21
  295.1 26.6 reduce-scatter.18
  325.3 26.5 all-gather.23
  363.9 26.6 reduce-scatter.20
  394.2 26.5 all-gather.25
  428.5 26.6 reduce-scatter.22
  458.9 26.5 all-gather.27
  497.3 26.6 reduce-scatter.24
  527.8 60.4 reduce-scatter.28
  592.4 61.7 reduce-scatter.26
  655.6 27.8 all-gather.19
  685.7 28.9 all-gather.29
  716.4 44.5 all-gather.33
  762.9 45.5 all-gather.31

commit v2 on v1

v2 whole, which is shorter than its diff:
```python
import functools
import math

import jax
import jax.numpy as jnp
from jax import lax
from jax.experimental import pallas as pl
from jax.experimental.pallas import tpu as pltpu
from jax.sharding import PartitionSpec as P

HEAD = 64


norm_eps = 1e-12
masked_value = -1000000000.0


def masked_scores(query_rows, key_rows, seg_row):
    score_scale = query_rows.shape[-1] ** (-0.5)
    raw_scores = (
        jnp.einsum("qhd,khd->hqk", query_rows, key_rows, preferred_element_type=jnp.float32)
        * score_scale
    )
    same_doc = seg_row[:, None] == seg_row[None, :]
    return jnp.where(same_doc[None], raw_scores, masked_value)


def attend_forward(block_items):
    query_rows, key_rows, value_rows, seg_row = block_items
    scores = masked_scores(query_rows, key_rows, seg_row)
    row_max = jnp.max(scores, axis=-1, keepdims=True)
    exponent = jnp.exp(scores - row_max)
    row_total = jnp.sum(exponent, axis=-1, keepdims=True)
    probs_low = (exponent / row_total).astype(jnp.bfloat16)
    context = jnp.einsum("hqk,khd->qhd", probs_low, value_rows, preferred_element_type=jnp.float32)
    return (context.astype(jnp.bfloat16), row_max + jnp.log(row_total))


def attend_backward(block_items):
    query_rows, key_rows, value_rows, seg_row, log_total, grad_context = block_items
    score_scale = query_rows.shape[-1] ** (-0.5)
    scores = masked_scores(query_rows, key_rows, seg_row)
    probability = jnp.exp(scores - log_total)
    grad_probs = jnp.einsum(
        "qhd,khd->hqk", grad_context, value_rows, preferred_element_type=jnp.float32
    )
    row_inner = jnp.sum(probability * grad_probs, axis=-1, keepdims=True)
    grad_scores = (probability * (grad_probs - row_inner)).astype(jnp.bfloat16)
    grad_query = (
        jnp.einsum("hqk,khd->qhd", grad_scores, key_rows, preferred_element_type=jnp.float32)
        * score_scale
    )
    grad_key = (
        jnp.einsum("hqk,qhd->khd", grad_scores, query_rows, preferred_element_type=jnp.float32)
        * score_scale
    )
    grad_value = jnp.einsum(
        "hqk,qhd->khd",
        probability.astype(jnp.bfloat16),
        grad_context,
        preferred_element_type=jnp.float32,
    )
    return jnp.stack([grad_query, grad_key, grad_value], axis=1).astype(jnp.bfloat16)


MESH = pl.DeviceIdType.MESH
F32 = jnp.float32
LOW = jnp.bfloat16
CHUNK = 32
LAG = 2
BLOCK = 64


def dot(a, b):
    return jnp.dot(a, b, preferred_element_type=F32)


def dot_t(a, b):
    return lax.dot_general(a, b, (((1,), (1,)), ((), ())), preferred_element_type=F32)


def dot_tn(a, b):
    return lax.dot_general(a, b, (((0,), (0,)), ((), ())), preferred_element_type=F32)


def greet(size):
    row, place = lax.axis_index("dp"), lax.axis_index("tensor")
    barrier = pltpu.get_barrier_semaphore()
    left, right = place > 0, place < size - 1

    @pl.when(left)
    def _():
        pl.semaphore_signal(barrier, inc=1, device_id=(row, place - 1), device_id_type=MESH)

    @pl.when(right)
    def _():
        pl.semaphore_signal(barrier, inc=1, device_id=(row, place + 1), device_id_type=MESH)

    @pl.when(left & right)
    def _():
        pl.semaphore_wait(barrier, 2)

    @pl.when(jnp.logical_not(left & right))
    def _():
        pl.semaphore_wait(barrier, 1)


def line_reduce(size, produce, finish, part, recv, outs, sems):
    sum_sent, sum_got, row_sent, row_got = sems
    row, place = lax.axis_index("dp"), lax.axis_index("tensor")
    half = part.shape[0] // 2
    chunks = half // CHUNK
    end = size - 1

    def rows_of(side, chunk):
        return pl.ds(pl.multiple_of(side * half + chunk * CHUNK, CHUNK), CHUNK)

    def sum_copy(side, chunk, target):
        rows = rows_of(side, chunk)
        return pltpu.make_async_remote_copy(
            src_ref=part.at[rows],
            dst_ref=recv.at[rows],
            send_sem=sum_sent.at[side, chunk],
            recv_sem=sum_got.at[side, chunk],
            device_id=(row, target),
            device_id_type=MESH,
        )

    def row_copy(which, side, chunk, target):
        rows = rows_of(side, chunk)
        return pltpu.make_async_remote_copy(
            src_ref=outs[which].at[rows],
            dst_ref=outs[which].at[rows],
            send_sem=row_sent.at[which, side, chunk],
            recv_sem=row_got.at[which, side, chunk],
            device_id=(row, target),
            device_id_type=MESH,
        )

    def side_facts(side):
        if side == 0:
            return place, place + 1, place - 1
        return end - place, place - 1, place + 1

    per_block = BLOCK // CHUNK

    def step(now, carry):
        @pl.when((now < chunks) & (lax.rem(now, per_block) == 0))
        def _():
            for side in range(2):
                produce(pl.ds(pl.multiple_of(side * half + now * CHUNK, CHUNK), BLOCK))

        for side in range(2):
            at, onward, back = side_facts(side)
            chunk = now - LAG * at

            @pl.when((chunk >= 0) & (chunk < chunks))
            def _():
                @pl.when(at > 0)
                def _():
                    sum_copy(side, chunk, onward).wait_recv()

                @pl.when(at < end)
                def _():
                    @pl.when(at > 0)
                    def _():
                        rows = rows_of(side, chunk)
                        part[rows] = (part[rows].astype(F32) + recv[rows].astype(F32)).astype(LOW)

                    sum_copy(side, chunk, onward).start()

                @pl.when(at == end)
                def _():
                    rows = rows_of(side, chunk)
                    own = pl.ds(pl.multiple_of(chunk * CHUNK, CHUNK), CHUNK)
                    finish(rows, own, part[rows].astype(F32) + recv[rows].astype(F32))
                    for which in range(len(outs)):
                        row_copy(which, side, chunk, back).start()

        for side in range(2):
            at, onward, back = side_facts(side)
            chunk = now - LAG * end - LAG * (end - at)

            @pl.when((at < end) & (chunk >= 0) & (chunk < chunks))
            def _():
                for which in range(len(outs)):
                    row_copy(which, side, chunk, back).wait_recv()

                    @pl.when(at > 0)
                    def _():
                        row_copy(which, side, chunk, back).start()

        return carry

    lax.fori_loop(0, chunks + 2 * LAG * end, step, 0)

    def drain(chunk, carry):
        for side in range(2):
            at, onward, back = side_facts(side)

            @pl.when(at < end)
            def _():
                sum_copy(side, chunk, onward).wait_send()

            @pl.when(at > 0)
            def _():
                for which in range(len(outs)):
                    row_copy(which, side, chunk, back).wait_send()

        return carry

    lax.fori_loop(0, chunks, drain, 0)


def normalize(residual):
    centred = residual - jnp.mean(residual, axis=-1, keepdims=True)
    inverse = lax.rsqrt(jnp.mean(centred * centred, axis=-1, keepdims=True) + norm_eps)
    return centred * inverse, inverse


def norm_back(grad, gain, unit, inverse):
    scaled = grad * gain
    return (
        scaled
        - jnp.mean(scaled, axis=-1, keepdims=True)
        - unit * jnp.mean(scaled * unit, axis=-1, keepdims=True)
    ) * inverse


def tally(total, values):
    total[...] += jnp.sum(values.reshape(-1, 8, values.shape[-1]), axis=0)


def line_call(size, collective, body, ins, out_shapes, rows, width, out_count, scratch=()):
    chunks = rows // 2 // CHUNK
    vmem = pl.BlockSpec(memory_space=pltpu.VMEM)
    return pl.pallas_call(
        body,
        out_shape=out_shapes,
        in_specs=[vmem] * len(ins),
        out_specs=[vmem] * len(out_shapes),
        scratch_shapes=[
            pltpu.VMEM((rows, width), LOW),
            pltpu.VMEM((rows, width), LOW),
            pltpu.SemaphoreType.DMA((2, chunks)),
            pltpu.SemaphoreType.DMA((2, chunks)),
            pltpu.SemaphoreType.DMA((out_count, 2, chunks)),
            pltpu.SemaphoreType.DMA((out_count, 2, chunks)),
            *scratch,
        ],
        compiler_params=pltpu.CompilerParams(
            collective_id=collective, has_side_effects=True, vmem_limit_bytes=56 << 20
        ),
    )(*ins)


def shape(*dims, kind=F32):
    return jax.ShapeDtypeStruct(dims, kind)


def attn_forward(size, collective, context, proj_w, proj_b, residual, gain, shift):
    rows, width = context.shape[0], proj_w.shape[1]
    half = rows // 2
    whole = residual.shape[0] == rows

    def body(context, proj_w, proj_b, residual, gain, shift, unit, inverse, normed, low, part, recv, *sems):
        greet(size)

        def produce(block):
            part[block] = dot(context[block], proj_w[...]).astype(LOW)

        def finish(at, own, total):
            came = residual[at if whole else own].astype(F32)
            unit_now, inverse_now = normalize(came + total + proj_b[...])
            unit[own] = unit_now
            inverse[own] = inverse_now
            result = unit_now * gain[...] + shift[...]
            normed[own] = result
            low[at] = result.astype(LOW)

        line_reduce(size, produce, finish, part, recv, [low], sems)

    return line_call(
        size,
        collective,
        body,
        (context, proj_w, proj_b, residual, gain, shift),
        (shape(half, width), shape(half, 1), shape(half, width), shape(rows, width, kind=LOW)),
        rows,
        width,
        1,
    )


def ffn_forward(size, collective, normed_low, normed, up_w, up_b, down_w, down_b, gain, shift, cotangent=None):
    rows, width = normed_low.shape
    hidden = up_w.shape[1]
    half = rows // 2
    last = cotangent is not None

    def body(*refs):
        normed_low, normed, up_w, up_b, down_w, down_b, gain, shift = refs[:8]
        rest = refs[8:]
        if last:
            cotangent, *rest = rest
            act, slope, grad, low, mixed, gain_sum, shift_sum, bias_sum, part, recv, *sems = rest
            outs = [low, mixed]
            for total in (gain_sum, shift_sum, bias_sum):
                total[...] = jnp.zeros_like(total)
        else:
            act, slope, unit, inverse, out, low, part, recv, *sems = rest
            outs = [low]
        greet(size)

        def produce(block):
            pre = dot(normed_low[block], up_w[...]) + up_b[...]
            cdf = 0.5 * lax.erf(pre * math.sqrt(0.5)) + 0.5
            act_now = (pre * cdf).astype(LOW)
            slope[block] = (
                cdf + pre * jnp.exp(-0.5 * pre * pre) * (1.0 / math.sqrt(2 * math.pi))
            ).astype(LOW)
            act[block] = act_now
            part[block] = dot(act_now, down_w[...]).astype(LOW)

        def finish(at, own, total):
            unit_now, inverse_now = normalize(normed[own] + total + down_b[...])
            result = unit_now * gain[...] + shift[...]
            if last:
                mixed[at] = result.astype(LOW)
                grad_in = cotangent[at].astype(F32)
                grad_now = norm_back(grad_in, gain[...], unit_now, inverse_now)
                grad[own] = grad_now
                grad_low = grad_now.astype(LOW)
                low[at] = grad_low
                tally(gain_sum, grad_in * unit_now)
                tally(shift_sum, grad_in)
                tally(bias_sum, grad_low.astype(F32))
            else:
                unit[own] = unit_now
                inverse[own] = inverse_now
                out[own] = result
                low[at] = result.astype(LOW)

        line_reduce(size, produce, finish, part, recv, outs, sems)

    ins = [normed_low, normed, up_w, up_b, down_w, down_b, gain, shift]
    outs = [shape(rows, hidden, kind=LOW), shape(rows, hidden, kind=LOW)]
    if last:
        ins += [cotangent]
        outs += [shape(half, width), shape(rows, width, kind=LOW), shape(rows, width, kind=LOW)]
        outs += [shape(8, width)] * 3
    else:
        outs += [shape(half, width), shape(half, 1), shape(half, width), shape(rows, width, kind=LOW)]
    return line_call(size, collective, body, ins, outs, rows, width, 2 if last else 1)


def ffn_backward(size, collective, branch_low, grad_second, slope, up_w, down_w, unit, inverse, gain):
    rows, width = branch_low.shape
    hidden = up_w.shape[1]
    half = rows // 2

    def body(branch_low, grad_second, slope, up_w, down_w, unit, inverse, gain, pre, grad, low, gain_sum, shift_sum, bias_sum, part, recv, *sems):
        for total in (gain_sum, shift_sum, bias_sum):
            total[...] = jnp.zeros_like(total)
        greet(size)

        def produce(block):
            pre_now = (dot_t(branch_low[block], down_w[...]) * slope[block].astype(F32)).astype(LOW)
            pre[block] = pre_now
            part[block] = dot_t(pre_now, up_w[...]).astype(LOW)

        def finish(at, own, total):
            grad_in = grad_second[own] + total
            unit_now = unit[own]
            grad_now = norm_back(grad_in, gain[...], unit_now, inverse[own])
            grad[own] = grad_now
            grad_low = grad_now.astype(LOW)
            low[at] = grad_low
            tally(gain_sum, grad_in * unit_now)
            tally(shift_sum, grad_in)
            tally(bias_sum, grad_low.astype(F32))

        line_reduce(size, produce, finish, part, recv, [low], sems)

    return line_call(
        size,
        collective,
        body,
        (branch_low, grad_second, slope, up_w, down_w, unit, inverse, gain),
        [shape(rows, hidden, kind=LOW), shape(half, width), shape(rows, width, kind=LOW)]
        + [shape(8, width)] * 3,
        rows,
        width,
        1,
    )


def attn_backward(size, collective, grad_proj, grad_first, qkv_w, below=None):
    rows, width = grad_proj.shape[0], qkv_w.shape[0]
    half = rows // 2
    inner = below is not None

    def body(grad_proj, grad_first, qkv_w, *rest):
        if inner:
            unit, inverse, gain, grad, low, gain_sum, shift_sum, bias_sum, part, recv, *sems = rest
            for total in (gain_sum, shift_sum, bias_sum):
                total[...] = jnp.zeros_like(total)
        else:
            low, part, recv, *sems = rest
        greet(size)

        def produce(block):
            part[block] = dot_t(grad_proj[block], qkv_w[...]).astype(LOW)

        def finish(at, own, total):
            grad_in = grad_first[own] + total
            if not inner:
                low[at] = grad_in.astype(LOW)
                return
            unit_now = unit[own]
            grad_now = norm_back(grad_in, gain[...], unit_now, inverse[own])
            grad[own] = grad_now
            grad_low = grad_now.astype(LOW)
            low[at] = grad_low
            tally(gain_sum, grad_in * unit_now)
            tally(shift_sum, grad_in)
            tally(bias_sum, grad_low.astype(F32))

        line_reduce(size, produce, finish, part, recv, [low], sems)

    ins = [grad_proj, grad_first, qkv_w]
    outs = [shape(rows, width, kind=LOW)]
    if inner:
        ins += list(below)
        outs = [shape(half, width), *outs] + [shape(8, width)] * 3
    return line_call(size, collective, body, ins, outs, rows, width, 1)


def local(
    tokens,
    segment_ids,
    cotangent,
    qkv_weight,
    qv_bias,
    proj_weight,
    proj_bias,
    first_gain,
    first_shift,
    up_weight,
    up_bias,
    down_weight,
    down_bias,
    second_gain,
    second_shift,
):
    seq_count, length, width = tokens.shape
    rows = seq_count * length
    layers = qkv_weight.shape[0]
    size = lax.axis_size("tensor")
    part_width = qkv_weight.shape[-1]
    heads = part_width // HEAD
    seg_row = segment_ids.reshape(length)

    def row_of(stacked, layer):
        return stacked[layer].astype(F32).reshape(1, -1)

    low = tokens.reshape(rows, width)
    residual = low
    cot = cotangent.reshape(rows, width)
    kept = []
    for layer in range(layers):
        qkv = qkv_weight[layer].reshape(width, 3 * part_width)
        bias = jnp.concatenate([qv_bias[layer, 0], jnp.zeros_like(qv_bias[layer, 0]), qv_bias[layer, 1]])
        projected = (dot(low, qkv) + bias.astype(F32)).astype(LOW)
        split = projected.reshape(length, 3, heads, HEAD)
        context, log_total = attend_forward((split[:, 0], split[:, 1], split[:, 2], seg_row))
        context = context.reshape(rows, part_width)
        unit_one, inverse_one, normed, normed_low = attn_forward(
            size,
            2 * layer,
            context,
            proj_weight[layer],
            row_of(proj_bias, layer),
            residual,
            row_of(first_gain, layer),
            row_of(first_shift, layer),
        )
        ffn_in = (
            normed_low,
            normed,
            up_weight[layer],
            row_of(up_bias, layer),
            down_weight[layer],
            row_of(down_bias, layer),
            row_of(second_gain, layer),
            row_of(second_shift, layer),
        )
        keep = (low, qkv, split, log_total, context, unit_one, inverse_one, normed_low)
        if layer + 1 < layers:
            act, slope, unit_two, inverse_two, residual, low = ffn_forward(size, 2 * layer + 1, *ffn_in)
            kept.append((*keep, act, slope, unit_two, inverse_two))
        else:
            act, slope, grad, branch_low, mixed, *two_sums = ffn_forward(size, 2 * layer + 1, *ffn_in, cot)
            kept.append((*keep, act, slope, None, None))

    def whole_grads(grads):
        low_grads = [g.astype(LOW).reshape(-1, width) for g in grads]
        counts = [g.shape[0] for g in low_grads]
        share = lax.psum_scatter(jnp.concatenate(low_grads), "dp", scatter_dimension=0, tiled=True)
        whole = lax.all_gather(share, "dp", axis=0, tiled=True)
        parts, at = [], 0
        for g, count in zip(grads, counts):
            parts.append(whole[at : at + count].reshape(g.shape))
            at += count
        return parts

    big = [None] * layers
    sharded = [None] * layers
    shared = [None] * layers
    for layer in range(layers - 1, -1, -1):
        (low, qkv, split, log_total, context, unit_one, inverse_one, normed_low, act, slope, _, _) = kept[layer]
        pre, grad_first, attn_low, *one_sums = ffn_backward(
            size,
            2 * layers + 2 * layer,
            branch_low,
            grad,
            slope,
            up_weight[layer],
            down_weight[layer],
            unit_one,
            inverse_one,
            row_of(first_gain, layer),
        )
        grad_context = dot_t(attn_low, proj_weight[layer]).astype(LOW)
        grad_heads = attend_backward(
            (
                split[:, 0],
                split[:, 1],
                split[:, 2],
                seg_row,
                log_total,
                grad_context.reshape(length, heads, HEAD),
            )
        )
        grad_proj = grad_heads.reshape(rows, 3 * part_width)
        grad_down = dot_tn(act, branch_low)
        grad_up = dot_tn(normed_low, pre)
        layer_sums = (one_sums, two_sums)
        if layer > 0:
            unit_two, inverse_two = kept[layer - 1][-2:]
            grad, branch_low, *two_sums = attn_backward(
                size,
                2 * layers + 2 * layer + 1,
                grad_proj,
                grad_first,
                qkv,
                (unit_two, inverse_two, row_of(second_gain, layer - 1)),
            )
        else:
            (input_grad,) = attn_backward(size, 2 * layers + 1, grad_proj, grad_first, qkv)
        grad_proj_w = dot_tn(context, attn_low)
        grad_qkv = dot_tn(low, grad_proj).reshape(width, 3, part_width)
        big[layer] = whole_grads([grad_qkv, grad_proj_w, grad_up, grad_down])
        sums = jnp.sum(grad_proj.astype(F32).reshape(rows, 3, part_width), axis=0)
        sharded[layer] = (jnp.stack([sums[0], sums[2]]), jnp.sum(pre.astype(F32), axis=0))
        (gain_one, shift_one, proj_b), (gain_two, shift_two, down_b) = layer_sums
        shared[layer] = (proj_b, gain_one, shift_one, down_b, gain_two, shift_two)

    whole_big = [
        jnp.stack([big[layer][member].astype(F32) for layer in range(layers)]) for member in range(4)
    ]
    sharded_flat = jnp.concatenate(
        [jnp.stack([sharded[p][member] for p in range(layers)]).reshape(-1) for member in range(2)]
    )
    shared_flat = jnp.concatenate(
        [jnp.sum(shared[p][member], axis=0) for member in range(6) for p in range(layers)]
    )
    tensor_sums = lax.all_gather(shared_flat, "tensor").sum(axis=0)
    totals = lax.all_gather(jnp.concatenate([sharded_flat, tensor_sums]), "dp").sum(axis=0)
    at = layers * 2 * part_width
    qv_total = totals[:at].reshape(layers, 2, part_width)
    to = at + layers * up_bias.shape[-1]
    up_total = totals[at:to].reshape(layers, -1)
    rest = totals[to:].reshape(6, layers, width)
    return (
        mixed.astype(F32).reshape(tokens.shape),
        input_grad.astype(F32).reshape(tokens.shape),
        whole_big[0],
        qv_total,
        whole_big[1],
        rest[0],
        rest[1],
        rest[2],
        whole_big[2],
        up_total,
        whole_big[3],
        rest[3],
        rest[4],
        rest[5],
    )


def solution(mesh):
    return jax.shard_map(
        local,
        mesh=mesh,
        in_specs=(
            P("dp", None, None),
            P("dp", None),
            P("dp", None, None),
            P(None, None, None, "tensor"),
            P(None, None, "tensor"),
            P(None, "tensor", None),
            P(),
            P(),
            P(),
            P(None, None, "tensor"),
            P(None, "tensor"),
            P(None, "tensor", None),
            P(),
            P(),
            P(),
        ),
        out_specs=(
            P("dp", None, None),
            P("dp", None, None),
            P(None, None, None, "tensor"),
            P(None, None, "tensor"),
            P(None, "tensor", None),
            P(),
            P(),
            P(),
            P(None, None, "tensor"),
            P(None, "tensor"),
            P(None, "tensor", None),
            P(),
            P(),
            P(),
        ),
        check_vma=False,
    )
```

time: 852 us -> 596 us (0.70)
  waiting for transfers between devices: 600 us -> 64.2 us
  Pallas kernels: 0 us -> 344 us
  matrix products: 85.2 us -> 36.1 us
  other arithmetic: 62.1 us -> 43.3 us
  local copies, waits for them, and re-layouts: 54.3 us -> 64.5 us
    pallas_call x0 -> x8, Pallas kernels: none -> 344 us  [line_call(): pl.pallas_call(body, out_shape=out_shapes, in_specs=[vmem] * len(ins), ou...]
    reduce_scatter x10 -> x2, waiting for transfers between devices: 307 us -> 62.3 us  [whole_grads(): lax.psum_scatter(jnp.concatenate(low_grads), 'dp', scatter_dimension=0, t...]
    all_gather x9 -> x0, waiting for transfers between devices: 213 us -> none  [the longest x7 184 us: widen_rows(): return lax.all_gather(low_rows, 'tensor', axis=0, tiled=True)]
    all_gather x2, waiting for transfers between devices: 80 us -> 1.14 us  [whole_grads(): whole = lax.all_gather(share, 'dp', axis=0, tiled=True)]
    dot_general x24 -> x12, matrix products: 71.1 us -> 24.2 us  [the longest x8 14.8 us: dot_tn(): lax.dot_general(a, b, (((0,), (0,)), ((), ())), preferred_element_type=F32)]
    reduce_sum x25 -> x18, other arithmetic: 22.5 us -> 8.58 us  [the longest x12 6.33 us: local(): jnp.sum(shared[p][member], axis=0)]
    unnamed x112 -> x90, local copies, waits for them, and re-layouts: 18.1 us -> 10.7 us
    convert_element_type x5 -> x9, local copies, waits for them, and re-layouts: 10.8 us -> 17.4 us  [the longest x2 9.2 us: local(): big[layer][member].astype(F32)]
  transfers between devices with their start and end apart: 21 -> 4, of which waited for: 19 -> 2; matrix products, arithmetic and copies ran while one was open for 7% -> 8% of each run, Pallas kernels for 0% -> 21%
where the time goes in v2:
time: 596 us; the launch traced here: 592 us
  Pallas kernels  344 us (58%)
  local copies, waits for them, and re-layouts  64.5 us (11%)
  waiting for transfers between devices  64.2 us (11%)
  other arithmetic  43.3 us (7%)
  matrix products  36.1 us (6%)
  blocking collectives  25.5 us (4%)
  between operations  14.9 us (2%)
    pallas_call x8, Pallas kernels, line_call(): pl.pallas_call(body, out_shape=out_shapes, in_specs=[vmem] * len(ins), ou...  344 us
    reduce_scatter x2, waiting for transfers between devices, whole_grads(): lax.psum_scatter(jnp.concatenate(low_grads), 'dp', scatter_dimension=0, t...  62.3 us
    dot_general x8, matrix products, dot_tn(): lax.dot_general(a, b, (((0,), (0,)), ((), ())), preferred_element_type=F32)  14.8 us
    all_gather x1, blocking collectives, local(): tensor_sums = lax.all_gather(shared_flat, 'tensor').sum(axis=0)  13.9 us
    another operation x4, other arithmetic, local(): jnp.stack([big[layer][member].astype(F32) for layer in range(layers)])  13.6 us
  transfers between devices with their start and end apart: 4, of which 2 were waited for; matrix products, arithmetic and copies ran while one was open for 8% of the time, Pallas kernels for 21%

profile of v2, /device:TPU:0, one launch (start us, length us, event | category | flops | bytes accessed | tf_op | source)
XLA Modules:
  0.0 592.4 jit_solution(4804074522866036280)
XLA Ops:
  8.0 1.4 slice_convert_fusion.6
  9.4 1.0 broadcast_compare_fusion
  10.3 2.2 slice_bitcast_fusion.10
  12.6 3.2 fusion.34
  16.7 2.3 copy.130
  19.0 3.7 add_convert_fusion.1
  22.7 2.3 copy.99
  25.0 1.9 fusion.38
  27.6 2.3 fusion.24
  32.6 5.9 %slice_bitcast_fusion.4 = (bf16[1024,1024]{1,0:T(8,128)(2,1)}, bf16[1024,1024]{1,0:T(8,128)(2,1)}, bf16[1024,1024]{1,0:T(8,128)(2,1)}, bf16[1024,1024]{1,0:T(8,128)(2,1)}) fusion(bf16[2,1024,1024]{2,1,0:T(8,128)(2,1)} %param.26, bf16[2,1024,1024]{2,1,0:T(8,128)(2,1)} %param.24), kind=kLoop, calls=%fused_computation.31 | loop fusion | bytes 16777216 | tf_op jit(solution)/shard_map/squeeze | solution.py:493
  38.5 42.7 %shard_map.254 = (f32[256,1024]{1,0:T(8,128)}, f32[256,1]{1,0:T(8,128)}, f32[256,1024]{1,0:T(8,128)}, bf16[512,1024]{1,0:T(8,128)(2,1)}) custom-call(bf16[512,256]{1,0:T(8,128)(2,1)} %copy.101.context, bf16[256,1024]{1,0:T(8,128)(2,1)} %get-tuple-element.153.proj_w, f32[1,1024]{1,0:T(1,128)} %get-tuple-element.178.proj_b, bf16[512,1024]{1,0:T(8,128)(2,1)} %bitcast.188, ...), custom_call_target="tpu_custom_call" | custom-call | tf_op jit(solution)/shard_map/pallas_call | solution.py:237
  81.3 42.1 %shard_map.255 = (bf16[512,1024]{1,0:T(8,128)(2,1)}, bf16[512,1024]{1,0:T(8,128)(2,1)}, f32[256,1024]{1,0:T(8,128)}, f32[256,1]{1,0:T(8,128)}, f32[256,1024]{1,0:T(8,128)}, /*index=5*/bf16[512,1024]{1,0:T(8,128)(2,1)}) custom-call(bf16[512,1024]{1,0:T(8,128)(2,1)} %get-tuple-element.53.refs_0_, f32[256,1024]{1,0:T(8,128)} %get-tuple-element.54.refs_1_, ...), custom_call_target="tpu_custom_call" | custom-call | tf_op jit(solution)/shard_map/pallas_call | solution.py:237
  123.4 2.2 add_convert_fusion
  126.0 0.9 fusion.39
  129.7 48.5 %shard_map.256 = (f32[256,1024]{1,0:T(8,128)}, f32[256,1]{1,0:T(8,128)}, f32[256,1024]{1,0:T(8,128)}, bf16[512,1024]{1,0:T(8,128)(2,1)}) custom-call(bf16[512,256]{1,0:T(8,128)(2,1)} %copy.105.context, bf16[256,1024]{1,0:T(8,128)(2,1)} %get-tuple-element.152.proj_w, f32[1,1024]{1,0:T(1,128)} %get-tuple-element.177.proj_b, ...), custom_call_target="tpu_custom_call" | custom-call | tf_op jit(solution)/shard_map/pallas_call | solution.py:237
  178.2 47.6 %shard_map.257 = (bf16[512,1024]{1,0:T(8,128)(2,1)}, bf16[512,1024]{1,0:T(8,128)(2,1)}, f32[256,1024]{1,0:T(8,128)}, bf16[512,1024]{1,0:T(8,128)(2,1)}, bf16[512...) custom-call(bf16[512,1024]{1,0:T(8,128)(2,1)} %get-tuple-element.57.refs_0_, ...), custom_call_target="tpu_custom_call" | custom-call | tf_op jit(solution)/shard_map/pallas_call | solution.py:237
  225.8 39.7 %shard_map.258 = (bf16[512,1024]{1,0:T(8,128)(2,1)}, f32[256,1024]{1,0:T(8,128)}, bf16[512,1024]{1,0:T(8,128)(2,1)}, f32[8,1024]{1,0:T(8,128)}, f32[8,1024]{1,0:T(8,128)}, /*index=5*/f32[8,1024]{1,0:T(8,128)}) custom-call(bf16[512,1024]{1,0:T(8,128)(2,1)} %get-tuple-element.60.branch_low, f32[256,1024]{1,0:T(8,128)} %get-tuple-element.61.grad_second, ...), custom_call_target="tpu_custom_call" | custom-call | tf_op jit(solution)/shard_map/pallas_call | solution.py:237
  265.5 1.7 convolution_convert_fusion.6
  267.2 1.7 convolution_convert_fusion.9
  269.7 1.0 multiply_reduce_fusion.1
  270.7 1.2 multiply_convert_fusion.1
  273.4 2.6 convolution_convert_fusion.1
  276.1 2.6 convolution_convert_fusion
  278.9 1.0 convolution_convert_fusion.4
  279.9 1.4 copy.118
  281.3 2.9 reshape.342
  284.2 5.7 pad_maximum_fusion.1
  290.0 1.3 copy-done.7
  291.3 1.6 copy.110.qkv_w
  292.9 1.2 copy.109.grad_proj
  294.0 40.4 %shard_map.259 = (f32[256,1024]{1,0:T(8,128)}, bf16[512,1024]{1,0:T(8,128)(2,1)}, f32[8,1024]{1,0:T(8,128)}, f32[8,1024]{1,0:T(8,128)}, f32[8,1024]{1,0:T(8,128)}) custom-call(bf16[512,768]{1,0:T(8,128)(2,1)} %copy.109.grad_proj, f32[256,1024]{1,0:T(8,128)} %get-tuple-element.66.grad_first, bf16[1024,768]{1,0:T(8,128)(2,1)} %copy.110.qkv_w, ...), custom_call_target="tpu_custom_call" | custom-call | tf_op jit(solution)/shard_map/pallas_call | solution.py:237
  334.5 40.4 %shard_map.260 = (bf16[512,1024]{1,0:T(8,128)(2,1)}, f32[256,1024]{1,0:T(8,128)}, bf16[512,1024]{1,0:T(8,128)(2,1)}, f32[8,1024]{1,0:T(8,128)}, f32[8,1024]{1,0:T(8,128)}, /*index=5*/f32[8,1024]{1,0:T(8,128)}) custom-call(bf16[512,1024]{1,0:T(8,128)(2,1)} %get-tuple-element.69.branch_low, f32[256,1024]{1,0:T(8,128)} %get-tuple-element.70.grad_second, ...), custom_call_target="tpu_custom_call" | custom-call | tf_op jit(solution)/shard_map/pallas_call | solution.py:237
  374.9 1.7 convolution_convert_fusion.8
  376.6 1.0 multiply_reduce_fusion
  377.6 1.2 multiply_convert_fusion
  381.0 0.9 copy-done.9
  381.9 1.0 fusion.12
  383.6 1.3 convert_element_type.253
  384.9 1.7 convolution_convert_fusion.7
  386.6 3.0 convolution_convert_fusion.2
  389.6 1.3 convolution_convert_fusion.3
  390.9 3.2 pad_maximum_fusion
  395.0 62.3 %reduce-scatter.3.cloned.1.call-done = bf16[384,1024]{1,0:T(8,128)(2,1)} async-done(((bf16[3072,1024]{1,0:T(8,128)(2,1)}), bf16[384,1024]{1,0:T(8,128)(2,1)}) %reduce-scatter.3.cloned.1.call-update) | async-done | bytes 786448 | tf_op jit(solution)/shard_map/reduce_scatter | solution.py:509
  457.4 1.6 copy.115.qkv_w
  458.9 1.2 copy.114.grad_proj
  464.4 1.4 convert_reduce_fusion.1
  468.5 13.9 %all-gather = f32[49152]{0:T(1024)S(1)} all-gather(f32[12288]{0:T(1024)S(1)} %constant_dynamic-update-slice_fusion), channel_id=2, replica_groups=mesh['dp'=8,'tensor'=4] {'tensor'}, dimensions={0}, use_global_device_ids=true | all-gather | bytes 245760 | tf_op jit(solution)/shard_map/all_gather | solution.py:578
  482.8 11.6 %all-gather.1 = f32[122880]{0:T(1024)S(1)} all-gather(f32[15360]{0:T(1024)S(1)} %pad_maximum_fusion.2), channel_id=3, replica_groups=mesh['dp'=8,'tensor'=4] {'dp'}, dimensions={0}, use_global_device_ids=true | all-gather | bytes 552960 | tf_op jit(solution)/shard_map/all_gather | solution.py:579
  499.5 42.3 %shard_map.261 = bf16[512,1024]{1,0:T(8,128)(2,1)} custom-call(bf16[512,768]{1,0:T(8,128)(2,1)} %copy.114.grad_proj, f32[256,1024]{1,0:T(8,128)} %get-tuple-element.75.grad_first, bf16[1024,768]{1,0:T(8,128)(2,1)} %copy.115.qkv_w), custom_call_target="tpu_custom_call" | custom-call | tf_op jit(solution)/shard_map/pallas_call | solution.py:237
  541.8 1.6 bitcast_convert_fusion.1
  543.4 2.8 bitcast_convert_fusion
  546.2 2.7 slice.359
  548.9 4.0 convert_element_type.262
  552.9 1.1 all-gather.5.cloned.1.call-done
  554.0 2.7 slice.358
  556.7 5.2 convert_element_type.257
  561.9 4.3 maximum_convert_fusion
  566.2 3.9 copy.119
  570.1 1.1 slice_bitcast_fusion.8
  571.2 1.1 slice_bitcast_fusion.9
  572.3 1.5 maximum_convert_fusion.5
  573.7 3.2 slice_bitcast_fusion
  577.8 3.9 maximum_convert_fusion.2
  581.7 3.9 maximum_convert_fusion.1
  (160 shorter events, 27.4 us)
Async XLA Ops:
  7.2 387.1 %reduce-scatter.5.cloned.1.call-start = ((), (), s32[]{:S(2)}) async-start(), calls=%async_computation.4 | async-start | bytes 7077888 | tf_op jit(solution)/shard_map/reduce_scatter | solution.py:509
  16.7 106.7 %copy-start.6 = (bf16[1,1024,3,256]{1,3,2,0:T(8,128)(2,1)}, bf16[1,1024,3,256]{1,3,2,0:T(8,128)(2,1)S(1)}, u32[]{:S(2)}) copy-start(bf16[1,1024,3,256]{1,3,2,0:T(8,128)(2,1)S(1)} %copy.131) | copy-start | bytes 4718596
  19.0 8.0 %copy-start.4 = (bf16[1,1024,3,256]{1,3,2,0:T(8,128)(2,1)}, bf16[1,1024,3,256]{1,3,2,0:T(8,128)(2,1)S(1)}, u32[]{:S(2)}) copy-start(bf16[1,1024,3,256]{1,3,2,0:T(8,128)(2,1)S(1)} %copy.130) | copy-start | bytes 4718596
  27.0 2.9 copy-start
  27.6 3.2 copy-start.27
  27.6 3.2 copy-start.28
  27.6 3.8 copy-start.29
  27.6 3.8 copy-start.30
  27.6 4.4 copy-start.31
  27.6 4.4 copy-start.32
  29.9 8.6 %copy-start.14 = (bf16[4,64,512]{2,1,0:T(8,128)(2,1)}, bf16[4,64,512]{2,1,0:T(8,128)(2,1)S(1)}, u32[]{:S(2)}) copy-start(bf16[4,64,512]{2,1,0:T(8,128)(2,1)S(1)} %fusion.24) | copy-start | bytes 786436
  126.9 2.0 copy-start.2
  225.8 41.4 %copy-start.16 = (bf16[2,256,1024]{2,1,0:T(8,128)(2,1)S(1)}, bf16[2,256,1024]{2,1,0:T(8,128)(2,1)}, u32[]{:S(2)}) copy-start(bf16[2,256,1024]{2,1,0:T(8,128)(2,1)} %param.20) | copy-start | bytes 3145732
  225.8 43.1 %copy-start.3 = (f32[4,512,512]{1,2,0:T(8,128)S(1)}, f32[4,512,512]{1,2,0:T(8,128)}, u32[]{:S(2)}) copy-start(f32[4,512,512]{1,2,0:T(8,128)} %copy-done.2) | copy-start | bytes 12582916
  271.9 1.2 copy-start.12
  271.9 1.5 copy-start.18
  273.4 2.6 copy-start.22
  273.4 2.6 copy-start.34
  276.1 2.8 copy-start.33
  289.9 1.4 copy-start.7
  289.9 167.4 %reduce-scatter.3.cloned.1.call-start = ((), (), s32[]{:S(2)}) async-start(), calls=%async_computation.2 | async-start | bytes 7077888 | tf_op jit(solution)/shard_map/reduce_scatter | solution.py:509
  334.4 40.5 %copy-start.17 = (bf16[2,256,1024]{2,1,0:T(8,128)(2,1)S(1)}, bf16[2,256,1024]{2,1,0:T(8,128)(2,1)}, u32[]{:S(2)}) copy-start(bf16[2,256,1024]{2,1,0:T(8,128)(2,1)} %param.20) | copy-start | bytes 3145732
  334.4 42.2 %copy-start.1 = (f32[4,512,512]{1,2,0:T(8,128)S(1)}, f32[4,512,512]{1,2,0:T(8,128)}, u32[]{:S(2)}) copy-start(f32[4,512,512]{1,2,0:T(8,128)} %copy-done) | copy-start | bytes 12582916
  334.4 42.2 %copy-start.8 = (bf16[512,768]{0,1:T(8,128)(2,1)S(1)}, bf16[512,768]{0,1:T(8,128)(2,1)}, u32[]{:S(2)}) copy-start(bf16[512,768]{0,1:T(8,128)(2,1)} %copy.99) | copy-start | bytes 2359300
  379.6 2.3 copy-start.13
  381.0 0.9 copy-start.9
  382.9 2.0 copy-start.15
  386.6 3.0 copy-start.20
  386.6 3.0 copy-start.21
  394.1 63.2 %copy-start.5 = (bf16[1,1024,3,256]{1,3,2,0:T(8,128)(2,1)S(1)}, bf16[1,1024,3,256]{1,3,2,0:T(8,128)(2,1)}, u32[]{:S(2)}) copy-start(bf16[1,1024,3,256]{1,3,2,0:T(8,128)(2,1)} %copy-done.4) | copy-start | bytes 4718596
  394.1 64.8 %copy-start.10 = (bf16[512,3,4,64]{0,3,2,1:T(8,128)(2,1)S(1)}, bf16[512,3,4,64]{0,3,2,1:T(8,128)(2,1)}, u32[]{:S(2)}) copy-start(bf16[512,3,4,64]{0,3,2,1:T(8,128)(2,1)} %copy-done.9) | copy-start | bytes 2359300
  394.2 67.5 %copy-start.26 = (f32[8,1024]{1,0:T(8,128)S(1)}, f32[8,1024]{1,0:T(8,128)}, u32[]{:S(2)}) copy-start(f32[8,1024]{1,0:T(8,128)} %get-tuple-element.85) | copy-start | bytes 98308
  394.2 67.5 %copy-start.25 = (f32[8,1024]{1,0:T(8,128)S(1)}, f32[8,1024]{1,0:T(8,128)}, u32[]{:S(2)}) copy-start(f32[8,1024]{1,0:T(8,128)} %get-tuple-element.87) | copy-start | bytes 98308
  394.2 67.5 %copy-start.24 = (f32[8,1024]{1,0:T(8,128)S(1)}, f32[8,1024]{1,0:T(8,128)}, u32[]{:S(2)}) copy-start(f32[8,1024]{1,0:T(8,128)} %get-tuple-element.89) | copy-start | bytes 98308
  394.2 67.5 %copy-start.23 = (f32[8,1024]{1,0:T(8,128)S(1)}, f32[8,1024]{1,0:T(8,128)}, u32[]{:S(2)}) copy-start(f32[8,1024]{1,0:T(8,128)} %get-tuple-element.91) | copy-start | bytes 98308
  394.2 70.0 %copy-start.19 = (bf16[512,1024]{1,0:T(8,128)(2,1)S(1)}, bf16[512,1024]{1,0:T(8,128)(2,1)}, u32[]{:S(2)}) copy-start(bf16[512,1024]{1,0:T(8,128)(2,1)} %get-tuple-element.78) | copy-start | bytes 3145732
  394.2 151.9 %all-gather.7.cloned.1.call-start = ((), (), s32[]{:S(2)}) async-start(), calls=%async_computation.5 | async-start | bytes 7077888 | tf_op jit(solution)/shard_map/all_gather | solution.py:510
  395.0 159.1 %all-gather.5.cloned.1.call-start = ((), (), s32[]{:S(2)}) async-start(), calls=%async_computation.3 | async-start | bytes 7077888 | tf_op jit(solution)/shard_map/all_gather | solution.py:510
  465.9 75.9 %copy-start.11 = (bf16[512,1024]{1,0:T(8,128)(2,1)S(1)}, bf16[512,1024]{1,0:T(8,128)(2,1)}, u32[]{:S(2)}) copy-start(bf16[512,1024]{1,0:T(8,128)(2,1)} %get-tuple-element.59) | copy-start | bytes 3145732
  572.2 4.7 slice-start
  573.7 3.6 slice-start.1
Sparse Core Ops, SparseCore 0:
  290.0 62.6 reduce-scatter.4
  394.3 62.9 reduce-scatter.2
  459.2 47.4 all-gather.6
  508.4 45.5 all-gather.4

commit v3 on v2

v3 whole, which is shorter than its diff:
```python
import math
import types

import jax
import jax.numpy as jnp
from jax import lax
from jax.experimental import pallas as pl
from jax.experimental.pallas import tpu as pltpu
from jax.sharding import PartitionSpec as P

HEAD = 64


norm_eps = 1e-12
masked_value = -1000000000.0


def masked_scores(query_rows, key_rows, seg_row):
    score_scale = query_rows.shape[-1] ** (-0.5)
    raw_scores = (
        jnp.einsum("qhd,khd->hqk", query_rows, key_rows, preferred_element_type=jnp.float32)
        * score_scale
    )
    same_doc = seg_row[:, None] == seg_row[None, :]
    return jnp.where(same_doc[None], raw_scores, masked_value)


def attend_forward(block_items):
    query_rows, key_rows, value_rows, seg_row = block_items
    scores = masked_scores(query_rows, key_rows, seg_row)
    row_max = jnp.max(scores, axis=-1, keepdims=True)
    exponent = jnp.exp(scores - row_max)
    row_total = jnp.sum(exponent, axis=-1, keepdims=True)
    probs_low = (exponent / row_total).astype(jnp.bfloat16)
    context = jnp.einsum("hqk,khd->qhd", probs_low, value_rows, preferred_element_type=jnp.float32)
    return (context.astype(jnp.bfloat16), row_max + jnp.log(row_total))


def attend_backward(block_items):
    query_rows, key_rows, value_rows, seg_row, log_total, grad_context = block_items
    score_scale = query_rows.shape[-1] ** (-0.5)
    scores = masked_scores(query_rows, key_rows, seg_row)
    probability = jnp.exp(scores - log_total)
    grad_probs = jnp.einsum(
        "qhd,khd->hqk", grad_context, value_rows, preferred_element_type=jnp.float32
    )
    row_inner = jnp.sum(probability * grad_probs, axis=-1, keepdims=True)
    grad_scores = (probability * (grad_probs - row_inner)).astype(jnp.bfloat16)
    grad_query = (
        jnp.einsum("hqk,khd->qhd", grad_scores, key_rows, preferred_element_type=jnp.float32)
        * score_scale
    )
    grad_key = (
        jnp.einsum("hqk,qhd->khd", grad_scores, query_rows, preferred_element_type=jnp.float32)
        * score_scale
    )
    grad_value = jnp.einsum(
        "hqk,qhd->khd",
        probability.astype(jnp.bfloat16),
        grad_context,
        preferred_element_type=jnp.float32,
    )
    return jnp.stack([grad_query, grad_key, grad_value], axis=1).astype(jnp.bfloat16)


MESH = pl.DeviceIdType.MESH
F32 = jnp.float32
LOW = jnp.bfloat16
CHUNK = 32
LAG = 2
PIECE = 256


def dot(a, b):
    return jnp.dot(a, b, preferred_element_type=F32)


def dot_t(a, b):
    return lax.dot_general(a, b, (((1,), (1,)), ((), ())), preferred_element_type=F32)


def dot_tn(a, b):
    return lax.dot_general(a, b, (((0,), (0,)), ((), ())), preferred_element_type=F32)


def here():
    return lax.axis_index("dp"), lax.axis_index("tensor")


def greet(size, line=True, targets=()):
    row, place = here()
    barrier = pltpu.get_barrier_semaphore()
    for count, target in targets:

        def signal(index, carry):
            pl.semaphore_signal(barrier, inc=1, device_id=target(index), device_id_type=MESH)
            return carry

        lax.fori_loop(0, count, signal, 0)
    expected = sum(count for count, _ in targets)
    if not line:
        pl.semaphore_wait(barrier, expected)
        return
    left, right = place > 0, place < size - 1

    @pl.when(left)
    def _():
        pl.semaphore_signal(barrier, inc=1, device_id=(row, place - 1), device_id_type=MESH)

    @pl.when(right)
    def _():
        pl.semaphore_signal(barrier, inc=1, device_id=(row, place + 1), device_id_type=MESH)

    @pl.when(left & right)
    def _():
        pl.semaphore_wait(barrier, expected + 2)

    @pl.when(jnp.logical_not(left & right))
    def _():
        pl.semaphore_wait(barrier, expected + 1)


def partner():
    row, place = here()
    return (row + 1 - 2 * lax.rem(row, 2), place)


def plane_peer(chips, index):
    row, place = here()
    return (lax.rem(row // 2 + index + 1, chips) * 2 + lax.rem(row, 2), place)


def line_loop(size, stages, extras=()):
    row, place = here()
    half = stages[0].part.shape[0] // 2
    chunks = half // CHUNK
    end = size - 1
    span = 2 * LAG * end

    def rows_of(side, chunk):
        return pl.ds(pl.multiple_of(side * half + chunk * CHUNK, CHUNK), CHUNK)

    def sum_copy(stage, side, chunk, target):
        rows = rows_of(side, chunk)
        return pltpu.make_async_remote_copy(
            src_ref=stage.part.at[rows],
            dst_ref=stage.recv.at[rows],
            send_sem=stage.sems[0].at[side, chunk],
            recv_sem=stage.sems[1].at[side, chunk],
            device_id=(row, target),
            device_id_type=MESH,
        )

    def row_copy(stage, which, side, chunk, target):
        rows = rows_of(side, chunk)
        return pltpu.make_async_remote_copy(
            src_ref=stage.outs[which].at[rows],
            dst_ref=stage.outs[which].at[rows],
            send_sem=stage.sems[2].at[which, side, chunk],
            recv_sem=stage.sems[3].at[which, side, chunk],
            device_id=(row, target),
            device_id_type=MESH,
        )

    def side_facts(side):
        if side == 0:
            return place, place + 1, place - 1
        return end - place, place - 1, place + 1

    def bring_back(stage, since):
        for side in range(2):
            at, onward, back = side_facts(side)
            chunk = since - LAG * end - LAG * (end - at)

            @pl.when((at < end) & (chunk >= 0) & (chunk < chunks))
            def _():
                for which in range(len(stage.outs)):
                    row_copy(stage, which, side, chunk, back).wait_recv()

                    @pl.when(at > 0)
                    def _():
                        row_copy(stage, which, side, chunk, back).start()

    def sum_up(stage, since):
        for side in range(2):
            at, onward, back = side_facts(side)
            chunk = since - LAG * at

            @pl.when((chunk >= 0) & (chunk < chunks))
            def _():
                @pl.when(at > 0)
                def _():
                    sum_copy(stage, side, chunk, onward).wait_recv()

                @pl.when(at < end)
                def _():
                    @pl.when(at > 0)
                    def _():
                        rows = rows_of(side, chunk)
                        total = stage.part[rows].astype(F32) + stage.recv[rows].astype(F32)
                        stage.part[rows] = total.astype(LOW)

                    sum_copy(stage, side, chunk, onward).start()

                @pl.when(at == end)
                def _():
                    rows = rows_of(side, chunk)
                    own = pl.ds(pl.multiple_of(chunk * CHUNK, CHUNK), CHUNK)
                    stage.finish(rows, own, stage.part[rows].astype(F32) + stage.recv[rows].astype(F32))
                    for which in range(len(stage.outs)):
                        row_copy(stage, which, side, chunk, back).start()

    def step(now, carry):
        for number, stage in enumerate(stages):
            bring_back(stage, now - number * span)
        for number, stage in enumerate(stages):
            since = now - number * span

            @pl.when((since >= 0) & (since < chunks))
            def _():
                for side in range(2):
                    stage.produce(rows_of(side, since))

            sum_up(stage, since)
        for first, count, work in extras:

            @pl.when((now >= first) & (now < first + count))
            def _():
                work(now - first)

        return carry

    lax.fori_loop(0, chunks + span * len(stages), step, 0)

    def drain(chunk, carry):
        for stage in stages:
            for side in range(2):
                at, onward, back = side_facts(side)

                @pl.when(at < end)
                def _():
                    sum_copy(stage, side, chunk, onward).wait_send()

                @pl.when(at > 0)
                def _():
                    for which in range(len(stage.outs)):
                        row_copy(stage, which, side, chunk, back).wait_send()

        return carry

    lax.fori_loop(0, chunks, drain, 0)


def by_rows(count, work, block=32):
    def one(index, carry):
        work(pl.ds(pl.multiple_of(index * block, block), block), index * block)
        return carry

    block = min(block, count)
    lax.fori_loop(0, count // block, one, 0)


class Spread:
    def __init__(self, chips, rows, width, grads, near, far, share, whole, sems):
        self.chips, self.half = chips, rows // 2
        self.count = self.half // chips
        self.grads, self.near, self.far, self.share, self.whole = grads, near, far, share, whole
        self.near_sems, self.far_sems, self.back_sems, self.last_sems = sems
        row, _ = here()
        self.core, self.chip = lax.rem(row, 2), row // 2

    @staticmethod
    def scratch(chips, rows, width):
        half = rows // 2
        pair = pltpu.SemaphoreType.DMA((2,))
        many = pltpu.SemaphoreType.DMA((2, chips - 1))
        return [
            pltpu.VMEM((half, width), LOW),
            pltpu.VMEM((chips - 1, half // chips, width), LOW),
            pair,
            many,
            many,
            pair,
        ]

    def half_rows(self, core):
        return pl.ds(pl.multiple_of(core * self.half, 16), self.half)

    def near_copy(self):
        return pltpu.make_async_remote_copy(
            src_ref=self.grads.at[self.half_rows(1 - self.core)],
            dst_ref=self.near,
            send_sem=self.near_sems.at[0],
            recv_sem=self.near_sems.at[1],
            device_id=partner(),
            device_id_type=MESH,
        )

    def far_copy(self, index):
        chip = lax.rem(self.chip + index + 1, self.chips)
        return pltpu.make_async_remote_copy(
            src_ref=self.near.at[pl.ds(pl.multiple_of(chip * self.count, 16), self.count)],
            dst_ref=self.far.at[index],
            send_sem=self.far_sems.at[0, index],
            recv_sem=self.far_sems.at[1, index],
            device_id=plane_peer(self.chips, index),
            device_id_type=MESH,
        )

    def back_copy(self, index):
        to = pl.multiple_of(self.core * self.half + self.chip * self.count, 16)
        return pltpu.make_async_remote_copy(
            src_ref=self.share,
            dst_ref=self.whole.at[pl.ds(to, self.count)],
            send_sem=self.back_sems.at[0, index],
            recv_sem=self.back_sems.at[1, index],
            device_id=plane_peer(self.chips, index),
            device_id_type=MESH,
        )

    def last_copy(self):
        rows = self.half_rows(self.core)
        return pltpu.make_async_remote_copy(
            src_ref=self.whole.at[rows],
            dst_ref=self.whole.at[rows],
            send_sem=self.last_sems.at[0],
            recv_sem=self.last_sems.at[1],
            device_id=partner(),
            device_id_type=MESH,
        )

    def each(self, work):
        def one(index, carry):
            work(index)
            return carry

        lax.fori_loop(0, self.chips - 1, one, 0)

    def to_partner(self):
        self.near_copy().start()

    def to_chips(self):
        self.near_copy().wait_recv()
        base = self.core * self.half

        def add(rows, first):
            own = self.grads[pl.ds(pl.multiple_of(base + first, 16), rows.size)]
            self.near[rows] = (self.near[rows].astype(F32) + own.astype(F32)).astype(LOW)

        by_rows(self.half, add)
        self.each(lambda index: self.far_copy(index).start())

    def sum_share(self):
        self.each(lambda index: self.far_copy(index).wait_recv())
        base = self.chip * self.count

        def add(rows, first):
            total = self.near[pl.ds(pl.multiple_of(base + first, 16), rows.size)].astype(F32)
            if self.chips <= 4:
                for index in range(self.chips - 1):
                    total += self.far[index, rows].astype(F32)
            else:
                total = lax.fori_loop(
                    0, self.chips - 1, lambda index, so_far: so_far + self.far[index, rows].astype(F32), total
                )
            self.share[rows] = total.astype(LOW)

        by_rows(self.count, add)

    def settle_sum(self):
        self.near_copy().wait_send()
        self.each(lambda index: self.far_copy(index).wait_send())

    def give_share(self):
        self.each(lambda index: self.back_copy(index).start())
        base = self.core * self.half + self.chip * self.count

        def keep(rows, first):
            self.whole[pl.ds(pl.multiple_of(base + first, 16), rows.size)] = self.share[rows]

        by_rows(self.count, keep)

    def to_other_core(self):
        self.each(lambda index: self.back_copy(index).wait_recv())
        self.last_copy().start()

    def settle_whole(self):
        self.last_copy().wait_recv()
        self.last_copy().wait_send()
        self.each(lambda index: self.back_copy(index).wait_send())


def normalize(residual):
    centred = residual - jnp.mean(residual, axis=-1, keepdims=True)
    inverse = lax.rsqrt(jnp.mean(centred * centred, axis=-1, keepdims=True) + norm_eps)
    return centred * inverse, inverse


def norm_back(grad, gain, unit, inverse):
    scaled = grad * gain
    return (
        scaled
        - jnp.mean(scaled, axis=-1, keepdims=True)
        - unit * jnp.mean(scaled * unit, axis=-1, keepdims=True)
    ) * inverse


def tally(total, values):
    total[...] += jnp.sum(values.reshape(-1, 8, values.shape[-1]), axis=0)


def call(collective, body, ins, outs, scratch):
    vmem = pl.BlockSpec(memory_space=pltpu.VMEM)
    names = [*ins, *outs]
    extra = {name: spec if isinstance(spec, list) else [spec] for name, spec in scratch.items()}

    def run(*refs):
        named = dict(zip(names, refs))
        rest = list(refs[len(names) :])
        for name, specs in extra.items():
            taken = [rest.pop(0) for _ in specs]
            named[name] = taken if isinstance(scratch[name], list) else taken[0]
        body(types.SimpleNamespace(**named))

    results = pl.pallas_call(
        run,
        out_shape=list(outs.values()),
        in_specs=[vmem] * len(ins),
        out_specs=[vmem] * len(outs),
        scratch_shapes=[spec for specs in extra.values() for spec in specs],
        compiler_params=pltpu.CompilerParams(
            collective_id=collective, has_side_effects=True, vmem_limit_bytes=60 << 20
        ),
    )(*ins.values())
    return types.SimpleNamespace(**dict(zip(outs, results)))


def shape(*dims, kind=F32):
    return jax.ShapeDtypeStruct(dims, kind)


def line_scratch(rows, width, outs=1):
    chunks = rows // 2 // CHUNK
    return [
        pltpu.VMEM((rows, width), LOW),
        pltpu.VMEM((rows, width), LOW),
        pltpu.SemaphoreType.DMA((2, chunks)),
        pltpu.SemaphoreType.DMA((2, chunks)),
        pltpu.SemaphoreType.DMA((outs, 2, chunks)),
        pltpu.SemaphoreType.DMA((outs, 2, chunks)),
    ]


def stage_of(produce, finish, outs, scratch):
    part, recv, *sems = scratch
    return types.SimpleNamespace(
        produce=produce, finish=finish, outs=outs, part=part, recv=recv, sems=sems
    )


def clear(*refs):
    for ref in refs:
        ref[...] = jnp.zeros_like(ref)


def proj_stage(r, whole):
    def produce(block):
        r.proj_line[0][block] = dot(r.context[block], r.proj_w[...]).astype(LOW)

    def finish(at, own, total):
        came = r.residual[at if whole else own].astype(F32)
        unit, inverse = normalize(came + total + r.proj_b[...])
        r.unit_one[own] = unit
        r.inverse_one[own] = inverse
        result = unit * r.gain_one[...] + r.shift_one[...]
        r.normed[own] = result
        r.normed_low[at] = result.astype(LOW)

    return stage_of(produce, finish, [r.normed_low], r.proj_line)


def ffn_stage(r, last):
    def produce(block):
        pre = dot(r.normed_low[block], r.up_w[...]) + r.up_b[...]
        cdf = 0.5 * lax.erf(pre * math.sqrt(0.5)) + 0.5
        act = (pre * cdf).astype(LOW)
        slope = cdf + pre * jnp.exp(-0.5 * pre * pre) * (1.0 / math.sqrt(2 * math.pi))
        r.slope[block] = slope.astype(LOW)
        r.act[block] = act
        r.ffn_line[0][block] = dot(act, r.down_w[...]).astype(LOW)

    def finish(at, own, total):
        unit, inverse = normalize(r.normed[own] + total + r.down_b[...])
        result = unit * r.gain_two[...] + r.shift_two[...]
        if last:
            r.mixed_own[own] = result.astype(LOW)
            grad_in = r.cotangent[at].astype(F32)
            grad = norm_back(grad_in, r.gain_two[...], unit, inverse)
            r.grad_second[own] = grad
            r.branch[at] = grad.astype(LOW)
            tally(r.sums.at[0], grad_in * unit)
            tally(r.sums.at[1], grad_in)
            tally(r.sums.at[2], grad.astype(LOW).astype(F32))
        else:
            r.unit_two[own] = unit
            r.inverse_two[own] = inverse
            r.hidden[own] = result
            r.low[at] = result.astype(LOW)

    return stage_of(produce, finish, [r.branch if last else r.low], r.ffn_line)


def ffn_back_stage(r):
    def produce(block):
        pre = (dot_t(r.branch[block], r.down_w[...]) * r.slope[block].astype(F32)).astype(LOW)
        r.pre[block] = pre
        tally(r.up_sum, pre.astype(F32))
        r.back_line[0][block] = dot_t(pre, r.up_w[...]).astype(LOW)

    def finish(at, own, total):
        grad_in = r.grad_second[own] + total
        unit = r.unit_one[own]
        grad = norm_back(grad_in, r.gain_one[...], unit, r.inverse_one[own])
        r.grad_first[own] = grad
        r.attn_low[at] = grad.astype(LOW)
        tally(r.sums.at[3], grad_in * unit)
        tally(r.sums.at[4], grad_in)
        tally(r.sums.at[5], grad.astype(LOW).astype(F32))

    return stage_of(produce, finish, [r.attn_low], r.back_line)


def columns(piece):
    return pl.ds(pl.multiple_of(piece * PIECE, PIECE), PIECE)


def ffn_grads(r, out, first):
    width, hidden = r.up_w.shape

    def up(piece):
        rows = pl.ds(pl.multiple_of(piece * PIECE, PIECE), PIECE)
        out[rows] = dot_tn(r.normed_low[:, columns(piece)], r.pre[...]).astype(LOW)

    def down(piece):
        rows = pl.ds(pl.multiple_of(width + piece * PIECE, PIECE), PIECE)
        out[rows] = dot_tn(r.act[:, columns(piece)], r.branch[...]).astype(LOW)

    return [(first, width // PIECE, up), (first + width // PIECE, hidden // PIECE, down)]


def attn_grads(r, out, first):
    split = r.grad_proj.shape[1]

    def piece_of(piece):
        rows = pl.ds(pl.multiple_of(piece * PIECE, PIECE), PIECE)
        out[rows, :split] = dot_tn(r.low_in[:, columns(piece)], r.grad_proj[...]).astype(LOW)
        out[rows, split:] = dot_tn(r.attn_low_in[:, columns(piece)], r.context_in[...]).astype(LOW)

    return [(first, r.low_in.shape[1] // PIECE, piece_of)]


def at_step(step, work):
    return (step, 1, lambda index: work())


def forward_kernel(size, collective, context, proj, residual, ffn):
    rows, width = context.shape[0], proj[0].shape[1]
    half, hidden = rows // 2, ffn[0].shape[1]
    whole = residual.shape[0] == rows

    def body(r):
        greet(size)
        line_loop(size, [proj_stage(r, whole), ffn_stage(r, False)])

    ins = dict(context=context, residual=residual)
    ins.update(zip(("proj_w", "proj_b", "gain_one", "shift_one"), proj))
    ins.update(zip(("up_w", "up_b", "down_w", "down_b", "gain_two", "shift_two"), ffn))
    outs = dict(
        unit_one=shape(half, width),
        inverse_one=shape(half, 1),
        normed_low=shape(rows, width, kind=LOW),
        act=shape(rows, hidden, kind=LOW),
        slope=shape(rows, hidden, kind=LOW),
        unit_two=shape(half, width),
        inverse_two=shape(half, 1),
        hidden=shape(half, width),
        low=shape(rows, width, kind=LOW),
    )
    scratch = dict(
        normed=pltpu.VMEM((half, width), F32),
        proj_line=line_scratch(rows, width),
        ffn_line=line_scratch(rows, width),
    )
    return call(collective, body, ins, outs, scratch)


def turn_kernel(size, collective, context, proj, residual, ffn, cotangent):
    rows, width = context.shape[0], proj[0].shape[1]
    half, hidden = rows // 2, ffn[0].shape[1]
    chunks = half // CHUNK
    whole = residual.shape[0] == rows

    def body(r):
        clear(r.sums, r.up_sum)
        greet(size)
        stages = [proj_stage(r, whole), ffn_stage(r, True), ffn_back_stage(r)]
        first = 4 * LAG * (size - 1) + chunks
        line_loop(size, stages, ffn_grads(r, r.ffn_grad, first))

    ins = dict(context=context, residual=residual, cotangent=cotangent)
    ins.update(zip(("proj_w", "proj_b", "gain_one", "shift_one"), proj))
    ins.update(zip(("up_w", "up_b", "down_w", "down_b", "gain_two", "shift_two"), ffn))
    outs = dict(
        mixed_own=shape(half, width, kind=LOW),
        grad_first=shape(half, width),
        attn_low=shape(rows, width, kind=LOW),
        ffn_grad=shape(width + hidden, width, kind=LOW),
        up_sum=shape(8, hidden),
        sums=shape(6, 8, width),
    )
    scratch = dict(
        normed=pltpu.VMEM((half, width), F32),
        unit_one=pltpu.VMEM((half, width), F32),
        inverse_one=pltpu.VMEM((half, 1), F32),
        normed_low=pltpu.VMEM((rows, width), LOW),
        act=pltpu.VMEM((rows, hidden), LOW),
        slope=pltpu.VMEM((rows, hidden), LOW),
        pre=pltpu.VMEM((rows, hidden), LOW),
        branch=pltpu.VMEM((rows, width), LOW),
        grad_second=pltpu.VMEM((half, width), F32),
        proj_line=line_scratch(rows, width),
        ffn_line=line_scratch(rows, width),
        back_line=line_scratch(rows, width),
    )
    return call(collective, body, ins, outs, scratch)


def qkv_back_stage(r, inner):
    def produce(block):
        r.qkv_line[0][block] = dot_t(r.grad_proj[block], r.qkv_w[...]).astype(LOW)

    def finish(at, own, total):
        grad_in = r.grad_first_in[own] + total
        if not inner:
            r.grad_low[at] = grad_in.astype(LOW)
            r.mixed[at] = r.mixed_own[own]
            return
        unit = r.unit_two[own]
        grad = norm_back(grad_in, r.gain_two[...], unit, r.inverse_two[own])
        r.grad_second[own] = grad
        r.branch[at] = grad.astype(LOW)
        tally(r.sums.at[0], grad_in * unit)
        tally(r.sums.at[1], grad_in)
        tally(r.sums.at[2], grad.astype(LOW).astype(F32))

    return stage_of(produce, finish, [r.branch] if inner else [r.grad_low, r.mixed], r.qkv_line)


def spread_targets(chips):
    return [(1, lambda index: partner()), (chips - 1, lambda index: plane_peer(chips, index))]


def backward_kernel(size, chips, collective, attn, below, ffn, ffn_grad):
    rows, width = attn["grad_proj"].shape[0], attn["low_in"].shape[1]
    half, hidden = rows // 2, ffn["up_w"].shape[1]
    chunks = half // CHUNK
    span = 2 * LAG * (size - 1)
    ffn_rows = width + hidden

    def body(r):
        clear(r.sums, r.up_sum)
        greet(size, targets=spread_targets(chips))
        near, far, *sems = r.ffn_spread
        ffn_sum = Spread(chips, ffn_rows, width, r.ffn_grad_in, near, far, r.ffn_share, r.ffn_whole, sems)
        near, far, *sems = r.attn_spread
        attn_sum = Spread(chips, width, width, r.attn_grad, near, far, r.attn_share, None, sems)
        ffn_sum.to_partner()
        extras = [
            at_step(2, ffn_sum.to_chips),
            *attn_grads(r, r.attn_grad, 3),
            at_step(8, attn_sum.to_partner),
            at_step(span + 3, lambda: (ffn_sum.sum_share(), ffn_sum.give_share())),
            at_step(span + 4, attn_sum.to_chips),
            *ffn_grads(r, r.ffn_grad, span + chunks),
            at_step(2 * span + 3, ffn_sum.to_other_core),
        ]
        line_loop(size, [qkv_back_stage(r, True), ffn_back_stage(r)], extras)
        attn_sum.sum_share()
        attn_sum.settle_sum()
        ffn_sum.settle_sum()
        ffn_sum.settle_whole()

    ins = dict(**attn, **below, **ffn, ffn_grad_in=ffn_grad)
    outs = dict(
        grad_first=shape(half, width),
        attn_low=shape(rows, width, kind=LOW),
        ffn_grad=shape(ffn_rows, width, kind=LOW),
        up_sum=shape(8, hidden),
        sums=shape(6, 8, width),
        attn_share=shape(width // 2 // chips, width, kind=LOW),
        ffn_whole=shape(ffn_rows, width, kind=LOW),
    )
    scratch = dict(
        pre=pltpu.VMEM((rows, hidden), LOW),
        branch=pltpu.VMEM((rows, width), LOW),
        grad_second=pltpu.VMEM((half, width), F32),
        attn_grad=pltpu.VMEM((width, width), LOW),
        ffn_share=pltpu.VMEM((ffn_rows // 2 // chips, width), LOW),
        qkv_line=line_scratch(rows, width),
        back_line=line_scratch(rows, width),
        ffn_spread=Spread.scratch(chips, ffn_rows, width),
        attn_spread=Spread.scratch(chips, width, width),
    )
    return call(collective, body, ins, outs, scratch)


def last_kernel(size, chips, collective, attn, mixed_own, ffn_grad, attn_share, small, own_rows):
    rows, width = attn["grad_proj"].shape[0], attn["low_in"].shape[1]
    chunks = rows // 2 // CHUNK
    span = 2 * LAG * (size - 1)
    ffn_rows = ffn_grad.shape[0]
    count = small.shape[0]
    teams = 2 * chips

    def row_peer(index):
        row, place = here()
        return (lax.rem(row + index + 1, teams), place)

    def line_peer(index):
        row, place = here()
        return (row, lax.rem(place + index + 1, size))

    def body(r):
        row, place = here()
        clear(r.ends)
        greet(size, line=False, targets=[(teams - 1, row_peer), (size - 1, line_peer)])
        near, far, *sems = r.ffn_spread
        ffn_sum = Spread(chips, ffn_rows, width, r.ffn_grad_in, near, far, r.ffn_share, r.ffn_whole, sems)
        near, far, *sems = r.attn_spread
        attn_sum = Spread(chips, width, width, r.attn_grad, near, far, r.attn_share, r.attn_whole, sems)
        near, far, *sems = r.above_spread
        above_sum = Spread(chips, width, width, None, near, far, r.above_share, r.above_whole, sems)

        def end_copy(slot, index):
            return pltpu.make_async_remote_copy(
                src_ref=r.small,
                dst_ref=r.ends.at[slot],
                send_sem=r.end_sent.at[slot, index],
                recv_sem=r.end_got.at[slot],
                device_id=line_peer(index),
                device_id_type=MESH,
            )

        def team_copy(index, slot):
            return pltpu.make_async_remote_copy(
                src_ref=r.mine,
                dst_ref=r.others.at[slot],
                send_sem=r.team_sent.at[index],
                recv_sem=r.team_got.at[slot],
                device_id=row_peer(index),
                device_id_type=MESH,
            )

        def each(number, work):
            def one(index, carry):
                work(index)
                return carry

            lax.fori_loop(0, number, one, 0)

        end_places = ((0, 0), (1, size - 1))

        def small_to_line():
            for slot, end in end_places:

                @pl.when(place == end)
                def _():
                    each(size - 1, lambda index: end_copy(slot, index).start())

        def small_to_teams():
            for slot, end in end_places:

                @pl.when(place != end)
                def _():
                    end_copy(slot, 0).wait_recv()

            line_total = r.small[...] + r.ends[0] + r.ends[1]
            number = lax.broadcasted_iota(jnp.int32, (count, width), 0)
            r.mine[...] = jnp.where(number < own_rows, r.small[...], line_total)
            each(teams - 1, lambda index: team_copy(index, row).start())
            r.others[row] = r.mine[...]

        def small_finish():
            each(teams - 1, lambda index: team_copy(index, row_peer(index)[0]).wait_recv())
            r.small_total[...] = lax.fori_loop(
                1, teams, lambda index, total: total + r.others[index], r.others[0]
            )
            each(teams - 1, lambda index: team_copy(index, row).wait_send())
            for slot, end in end_places:

                @pl.when(place == end)
                def _():
                    each(size - 1, lambda index: end_copy(slot, index).wait_send())

        ffn_sum.to_partner()
        above_sum.give_share()
        small_to_line()
        extras = [
            *attn_grads(r, r.attn_grad, 0),
            at_step(1, ffn_sum.to_chips),
            at_step(4, attn_sum.to_partner),
            at_step(5, small_to_teams),
            at_step(6, attn_sum.to_chips),
            at_step(span, above_sum.to_other_core),
        ]
        line_loop(size, [qkv_back_stage(r, False)], extras)
        ffn_sum.sum_share()
        ffn_sum.give_share()
        attn_sum.sum_share()
        attn_sum.give_share()
        small_finish()
        above_sum.settle_whole()
        ffn_sum.settle_sum()
        attn_sum.settle_sum()
        ffn_sum.to_other_core()
        attn_sum.to_other_core()
        ffn_sum.settle_whole()
        attn_sum.settle_whole()

    ins = dict(**attn, mixed_own=mixed_own, ffn_grad_in=ffn_grad, above_share=attn_share, small=small)
    outs = dict(
        grad_low=shape(rows, width, kind=LOW),
        mixed=shape(rows, width, kind=LOW),
        ffn_whole=shape(ffn_rows, width, kind=LOW),
        attn_whole=shape(width, width, kind=LOW),
        above_whole=shape(width, width, kind=LOW),
        small_total=shape(count, width),
    )
    scratch = dict(
        attn_grad=pltpu.VMEM((width, width), LOW),
        ffn_share=pltpu.VMEM((ffn_rows // 2 // chips, width), LOW),
        attn_share=pltpu.VMEM((width // 2 // chips, width), LOW),
        ends=pltpu.VMEM((2, count, width), F32),
        mine=pltpu.VMEM((count, width), F32),
        others=pltpu.VMEM((teams, count, width), F32),
        end_sent=pltpu.SemaphoreType.DMA((2, size - 1)),
        end_got=pltpu.SemaphoreType.DMA((2,)),
        team_sent=pltpu.SemaphoreType.DMA((teams - 1,)),
        team_got=pltpu.SemaphoreType.DMA((teams,)),
        qkv_line=line_scratch(rows, width, 2),
        ffn_spread=Spread.scratch(chips, ffn_rows, width),
        attn_spread=Spread.scratch(chips, width, width),
        above_spread=Spread.scratch(chips, width, width),
    )
    return call(collective, body, ins, outs, scratch)


def local(
    tokens,
    segment_ids,
    cotangent,
    qkv_weight,
    qv_bias,
    proj_weight,
    proj_bias,
    first_gain,
    first_shift,
    up_weight,
    up_bias,
    down_weight,
    down_bias,
    second_gain,
    second_shift,
):
    seq_count, length, width = tokens.shape
    rows = seq_count * length
    layers = qkv_weight.shape[0]
    size = lax.axis_size("tensor")
    chips = lax.axis_size("dp") // 2
    part_width = qkv_weight.shape[-1]
    hidden = up_weight.shape[-1]
    heads = part_width // HEAD
    seg_row = segment_ids.reshape(length)

    def row_of(stacked, layer):
        return stacked[layer].astype(F32).reshape(1, -1)

    low = tokens.reshape(rows, width)
    residual = low
    cot = cotangent.reshape(rows, width)
    kept = []
    for layer in range(layers):
        qkv = qkv_weight[layer].reshape(width, 3 * part_width)
        bias = jnp.concatenate([qv_bias[layer, 0], jnp.zeros_like(qv_bias[layer, 0]), qv_bias[layer, 1]])
        projected = (dot(low, qkv) + bias.astype(F32)).astype(LOW)
        split = projected.reshape(length, 3, heads, HEAD)
        context, log_total = attend_forward((split[:, 0], split[:, 1], split[:, 2], seg_row))
        context = context.reshape(rows, part_width)
        proj = (
            proj_weight[layer],
            row_of(proj_bias, layer),
            row_of(first_gain, layer),
            row_of(first_shift, layer),
        )
        ffn = (
            up_weight[layer],
            row_of(up_bias, layer),
            down_weight[layer],
            row_of(down_bias, layer),
            row_of(second_gain, layer),
            row_of(second_shift, layer),
        )
        keep = types.SimpleNamespace(low=low, qkv=qkv, split=split, log_total=log_total, context=context)
        if layer + 1 < layers:
            keep.done = forward_kernel(size, layer, context, proj, residual, ffn)
            residual, low = keep.done.hidden, keep.done.low
        else:
            above = turn_kernel(size, layer, context, proj, residual, ffn, cot)
            mixed_own = above.mixed_own
        kept.append(keep)

    sums = [None] * layers
    norm_sums = [None] * layers
    up_sums = [None] * layers
    qv_sums = [None] * layers
    ffn_whole = [None] * layers
    attn_whole = [None] * layers
    norm_sums[layers - 1] = above.sums.sum(axis=1)
    up_sums[layers - 1] = above.up_sum.sum(axis=0)
    attn_share = None
    for layer in range(layers - 1, -1, -1):
        keep = kept[layer]
        split = keep.split
        grad_context = dot_t(above.attn_low, proj_weight[layer]).astype(LOW)
        grad_heads = attend_backward(
            (
                split[:, 0],
                split[:, 1],
                split[:, 2],
                seg_row,
                keep.log_total,
                grad_context.reshape(length, heads, HEAD),
            )
        )
        grad_proj = grad_heads.reshape(rows, 3 * part_width)
        qkv_sums = jnp.sum(grad_proj.astype(F32).reshape(rows, 3, part_width), axis=0)
        qv_sums[layer] = jnp.concatenate([qkv_sums[0], qkv_sums[2]])
        attn = dict(
            grad_proj=grad_proj,
            grad_first_in=above.grad_first,
            qkv_w=keep.qkv,
            low_in=keep.low,
            attn_low_in=above.attn_low,
            context_in=keep.context,
        )
        if layer > 0:
            done = kept[layer - 1].done
            below = dict(
                unit_two=done.unit_two,
                inverse_two=done.inverse_two,
                gain_two=row_of(second_gain, layer - 1),
            )
            ffn = dict(
                act=done.act,
                slope=done.slope,
                normed_low=done.normed_low,
                unit_one=done.unit_one,
                inverse_one=done.inverse_one,
                gain_one=row_of(first_gain, layer - 1),
                up_w=up_weight[layer - 1],
                down_w=down_weight[layer - 1],
            )
            above = backward_kernel(
                size, chips, 2 * layers - layer, attn, below, ffn, above.ffn_grad
            )
            norm_sums[layer - 1] = above.sums.sum(axis=1)
            up_sums[layer - 1] = above.up_sum.sum(axis=0)
            ffn_whole[layer] = above.ffn_whole
            attn_share = above.attn_share
        else:
            norm_rows = jnp.stack(norm_sums, axis=1).reshape(6 * layers, width)
            own = jnp.concatenate([*qv_sums, *up_sums]).reshape(-1, width)
            used = own.shape[0] + norm_rows.shape[0]
            small = jnp.concatenate([own, norm_rows, jnp.zeros((-used % 8, width), F32)])
            last = last_kernel(
                size, chips, 2 * layers, attn, mixed_own, above.ffn_grad, attn_share, small, own.shape[0]
            )
            ffn_whole[0] = last.ffn_whole
            attn_whole[0] = last.attn_whole
            attn_whole[1] = last.above_whole

    totals = last.small_total
    flat = totals[: own.shape[0]].reshape(-1)
    at = layers * 2 * part_width
    qv_total = flat[:at].reshape(layers, 2, part_width)
    up_total = flat[at:].reshape(layers, hidden)
    rest = totals[own.shape[0] : used].reshape(6, layers, width)
    split_at = 3 * part_width

    def stack(parts):
        return jnp.stack([part.astype(F32) for part in parts])

    return (
        last.mixed.astype(F32).reshape(tokens.shape),
        last.grad_low.astype(F32).reshape(tokens.shape),
        stack([part[:, :split_at].reshape(width, 3, part_width) for part in attn_whole]),
        qv_total,
        stack([part[:, split_at:].T for part in attn_whole]),
        rest[5],
        rest[3],
        rest[4],
        stack([part[:width] for part in ffn_whole]),
        up_total,
        stack([part[width:] for part in ffn_whole]),
        rest[2],
        rest[0],
        rest[1],
    )


def solution(mesh):
    return jax.shard_map(
        local,
        mesh=mesh,
        in_specs=(
            P("dp", None, None),
            P("dp", None),
            P("dp", None, None),
            P(None, None, None, "tensor"),
            P(None, None, "tensor"),
            P(None, "tensor", None),
            P(),
            P(),
            P(),
            P(None, None, "tensor"),
            P(None, "tensor"),
            P(None, "tensor", None),
            P(),
            P(),
            P(),
        ),
        out_specs=(
            P("dp", None, None),
            P("dp", None, None),
            P(None, None, None, "tensor"),
            P(None, None, "tensor"),
            P(None, "tensor", None),
            P(),
            P(),
            P(),
            P(None, None, "tensor"),
            P(None, "tensor"),
            P(None, "tensor", None),
            P(),
            P(),
            P(),
        ),
        check_vma=False,
    )
```

time: 596 us -> 465 us (0.78)
  waiting for transfers between devices: 64.2 us -> 0 us
  blocking collectives: 25.5 us -> 0 us
  Pallas kernels: 344 us -> 361 us
  local copies, waits for them, and re-layouts: 64.5 us -> 48.9 us
  between operations: 14.9 us -> 1 us
  matrix products: 36.1 us -> 22.8 us
  other arithmetic: 43.3 us -> 30.4 us
    reduce_scatter x2 -> x0, waiting for transfers between devices: 62.3 us -> none  [whole_grads(): lax.psum_scatter(jnp.concatenate(low_grads), 'dp', scatter_dimension=0, t...]
    all_gather x2 -> x0, blocking collectives: 25.5 us -> none  [the longest x1 13.9 us: local(): tensor_sums = lax.all_gather(shared_flat, 'tensor').sum(axis=0)]
    pallas_call x8 -> x4, Pallas kernels: 344 us -> 361 us  [call(): pl.pallas_call(run, out_shape=list(outs.values()), in_specs=[vmem] * len(...]
    dot_general x8 -> x0, matrix products: 14.8 us -> none  [dot_tn(): lax.dot_general(a, b, (((0,), (0,)), ((), ())), preferred_element_type=F32)]
    convert_element_type x5 -> x0, local copies, waits for them, and re-layouts: 12.5 us -> none  [the longest x2 9.2 us: local(): big[layer][member].astype(F32)]
    concatenate x3 -> x1, other arithmetic: 8.98 us -> 0.7 us  [local(): jnp.concatenate([own, norm_rows, jnp.zeros((-used % 8, width), F32)])]
    another operation x6 -> x5, other arithmetic: 13.6 us -> 11.2 us  [the longest x4 11.1 us: stack(): return jnp.stack([part.astype(F32) for part in parts])]
    unnamed x90 -> x27, local copies, waits for them, and re-layouts: 10.7 us -> 12.7 us
  transfers between devices with their start and end apart: 4 -> 0, of which waited for: 2 -> 0; matrix products, arithmetic and copies ran while one was open for 8% -> 0% of each run, Pallas kernels for 21% -> 0%
where the time goes in v3:
time: 465 us; the launch traced here: 464 us
  Pallas kernels  361 us (78%)
  local copies, waits for them, and re-layouts  48.9 us (11%)
  other arithmetic  30.4 us (7%)
  matrix products  22.8 us (5%)
    pallas_call x4, Pallas kernels, call(): pl.pallas_call(run, out_shape=list(outs.values()), in_specs=[vmem] * len(...  361 us
    unnamed x27, local copies, waits for them, and re-layouts  12.7 us
    another operation x4, other arithmetic, stack(): return jnp.stack([part.astype(F32) for part in parts])  11.1 us

profile of v3, /device:TPU:0, one launch (start us, length us, event | category | flops | bytes accessed | tf_op | source)
XLA Modules:
  0.0 464.1 jit_solution(13709128924443687646)
XLA Ops:
  0.7 0.8 slice_reduce_fusion.2
  1.5 1.4 slice_convert_fusion.6
  2.9 1.4 slice_convert_fusion.4
  4.3 1.4 slice_convert_fusion.2
  5.7 1.4 slice_convert_fusion
  7.0 1.0 broadcast_compare_fusion
  8.0 2.2 slice_bitcast_fusion.10
  10.2 3.2 fusion.31
  13.5 0.9 copy.85
  14.3 1.6 copy.64.refs_2_
  15.9 1.7 copy.84
  17.6 3.1 add_convert_fusion.1
  20.8 1.6 copy.70.refs_2_
  22.3 1.4 copy.53
  23.8 0.9 fusion.35
  24.7 0.6 fusion
  25.3 0.9 fusion.23
  26.1 0.5 copy-done
  26.7 0.8 copy.55.refs_0_.refs_5_
  27.5 5.9 %slice_bitcast_fusion.4 = (bf16[1024,1024]{1,0:T(8,128)(2,1)}, bf16[1024,1024]{1,0:T(8,128)(2,1)}, bf16[1024,1024]{1,0:T(8,128)(2,1)}, bf16[1024,1024]{1,0:T(8,128)(2,1)}) fusion(bf16[2,1024,1024]{2,1,0:T(8,128)(2,1)} %param.26, bf16[2,1024,1024]{2,1,0:T(8,128)(2,1)} %param.24), kind=kLoop, calls=%fused_computation.25 | loop fusion | bytes 16777216 | tf_op jit(solution)/shard_map/squeeze | solution.py:908
  33.5 73.1 %shard_map.254 = (f32[256,1024]{1,0:T(8,128)}, f32[256,1]{1,0:T(8,128)}, bf16[512,1024]{1,0:T(8,128)(2,1)}, bf16[512,1024]{1,0:T(8,128)(2,1)}, bf16[512,1024]{1,...) custom-call(bf16[512,256]{1,0:T(8,128)(2,1)} %copy.55.refs_0_.refs_5_, ...), custom_call_target="tpu_custom_call" | custom-call | tf_op jit(solution)/shard_map/pallas_call | solution.py:425
  106.6 2.2 add_convert_fusion
  109.2 0.9 fusion.36
  110.1 0.6 fusion.1
  110.7 0.9 fusion.22
  112.1 0.8 copy.59.refs_0_.refs_5_
  112.9 101.5 %shard_map.255 = (bf16[256,1024]{1,0:T(8,128)(2,1)}, f32[256,1024]{1,0:T(8,128)}, bf16[512,1024]{1,0:T(8,128)(2,1)}, bf16[2048,1024]{1,0:T(8,128)(2,1)}, f32[8,1024]{1,0:T(8,128)}, /*index=5*/f32[6,8,1024]{2,1,0:T(8,128)}) custom-call(bf16[512,256]{1,0:T(8,128)(2,1)} %copy.59.refs_0_.refs_5_, f32[256,1024]{1,0:T(8,128)} %get-tuple-element.43.refs_1_, ...), custom_call_target="tpu_custom_call" | custom-call | tf_op jit(solution)/shard_map/pallas_call | solution.py:425
  214.4 0.8 reduce_sum.97
  215.2 1.0 reduce_sum.99
  216.2 1.8 convolution_convert_fusion.1
  218.1 3.0 fusion.15
  221.0 0.9 multiply_reduce_fusion.1
  222.0 1.2 multiply_convert_fusion.1
  223.2 0.8 fusion.20
  224.7 1.2 copy.63.refs_0_
  225.9 87.0 %shard_map.256 = (f32[256,1024]{1,0:T(8,128)}, bf16[512,1024]{1,0:T(8,128)(2,1)}, bf16[2048,1024]{1,0:T(8,128)(2,1)}, f32[8,1024]{1,0:T(8,128)}, f32[6,8,1024]{2...) custom-call(bf16[512,768]{1,0:T(8,128)(2,1)} %copy.63.refs_0_, ...), custom_call_target="tpu_custom_call" | custom-call | tf_op jit(solution)/shard_map/pallas_call | solution.py:425
  313.0 0.8 reduce_sum.96
  313.7 1.0 reduce_sum.98
  314.9 1.9 convolution_convert_fusion
  316.7 3.0 fusion.12
  319.7 0.9 multiply_reduce_fusion
  320.6 1.2 multiply_convert_fusion
  321.8 0.8 fusion.18
  323.4 1.2 copy.69.refs_0_
  324.7 0.7 maximum_maximum_fusion.refs_9_
  325.4 99.3 %shard_map.257 = (bf16[512,1024]{1,0:T(8,128)(2,1)}, bf16[512,1024]{1,0:T(8,128)(2,1)}, bf16[2048,1024]{1,0:T(8,128)(2,1)}, bf16[1024,1024]{1,0:T(8,128)(2,1)}, ...) custom-call(bf16[512,768]{1,0:T(8,128)(2,1)} %copy.69.refs_0_, f32[256,1024]{1,0:T(8,128)} %get-tuple-element.55.refs_1_, ...), custom_call_target="tpu_custom_call" | custom-call | tf_op jit(solution)/shard_map/pallas_call | solution.py:425
  424.7 0.8 slice_reduce_fusion
  425.5 1.6 fusion.32
  427.1 0.6 reshape.262
  427.7 1.1 slice_bitcast_fusion.9
  428.8 1.5 slice.226
  430.3 1.6 copy.72
  431.9 1.1 slice_bitcast_fusion.8
  433.0 1.5 slice.227
  434.5 1.6 copy.73
  436.3 1.8 copy.75
  438.1 2.9 bitcast_convert_fusion.1
  441.1 1.6 bitcast_convert_fusion
  442.6 3.1 maximum_convert_fusion.2
  445.7 6.6 %copy.74 = f32[2,1024,3,256]{3,1,2,0:T(8,128)} copy(f32[2,1024,3,256]{1,3,2,0:T(8,128)} %maximum_convert_fusion.2) | data formatting | bytes 12582912
  452.3 2.8 slice_bitcast_fusion.1
  455.2 0.6 copy-done.6
  456.2 3.9 maximum_convert_fusion.1
  460.1 3.9 maximum_convert_fusion
  (46 shorter events, 3.4 us)
Async XLA Ops:
  24.7 2.0 copy-start
  110.1 2.0 copy-start.2
  112.1 104.1 %copy-start.8 = (bf16[2,256,1024]{2,1,0:T(8,128)(2,1)S(1)}, bf16[2,256,1024]{2,1,0:T(8,128)(2,1)}, u32[]{:S(2)}) copy-start(bf16[2,256,1024]{2,1,0:T(8,128)(2,1)} %param.20) | copy-start | bytes 3145732
  216.2 4.9 %copy-start.3 = (f32[4,512,512]{1,2,0:T(8,128)S(1)}, f32[4,512,512]{1,2,0:T(8,128)}, u32[]{:S(2)}) copy-start(f32[4,512,512]{1,2,0:T(8,128)} %copy-done.2) | copy-start | bytes 12582916
  314.8 4.8 %copy-start.1 = (f32[4,512,512]{1,2,0:T(8,128)S(1)}, f32[4,512,512]{1,2,0:T(8,128)}, u32[]{:S(2)}) copy-start(f32[4,512,512]{1,2,0:T(8,128)} %copy-done) | copy-start | bytes 12582916
  436.3 4.8 %copy-start.7 = (bf16[512,1024]{1,0:T(8,128)(2,1)S(1)}, bf16[512,1024]{1,0:T(8,128)(2,1)}, u32[]{:S(2)}) copy-start(bf16[512,1024]{1,0:T(8,128)(2,1)} %get-tuple-element.64) | copy-start | bytes 3145732
  438.1 4.5 copy-start.4
  438.1 4.5 copy-start.5
  452.3 3.4 copy-start.6

commit v4 on v3

--- a/solution.py
+++ b/solution.py
@@ -15,60 +15,13 @@
 masked_value = -1000000000.0
 
 
-def masked_scores(query_rows, key_rows, seg_row):
-    score_scale = query_rows.shape[-1] ** (-0.5)
-    raw_scores = (
-        jnp.einsum("qhd,khd->hqk", query_rows, key_rows, preferred_element_type=jnp.float32)
-        * score_scale
-    )
-    same_doc = seg_row[:, None] == seg_row[None, :]
-    return jnp.where(same_doc[None], raw_scores, masked_value)
-
-
-def attend_forward(block_items):
-    query_rows, key_rows, value_rows, seg_row = block_items
-    scores = masked_scores(query_rows, key_rows, seg_row)
-    row_max = jnp.max(scores, axis=-1, keepdims=True)
-    exponent = jnp.exp(scores - row_max)
-    row_total = jnp.sum(exponent, axis=-1, keepdims=True)
-    probs_low = (exponent / row_total).astype(jnp.bfloat16)
-    context = jnp.einsum("hqk,khd->qhd", probs_low, value_rows, preferred_element_type=jnp.float32)
-    return (context.astype(jnp.bfloat16), row_max + jnp.log(row_total))
-
-
-def attend_backward(block_items):
-    query_rows, key_rows, value_rows, seg_row, log_total, grad_context = block_items
-    score_scale = query_rows.shape[-1] ** (-0.5)
-    scores = masked_scores(query_rows, key_rows, seg_row)
-    probability = jnp.exp(scores - log_total)
-    grad_probs = jnp.einsum(
-        "qhd,khd->hqk", grad_context, value_rows, preferred_element_type=jnp.float32
-    )
-    row_inner = jnp.sum(probability * grad_probs, axis=-1, keepdims=True)
-    grad_scores = (probability * (grad_probs - row_inner)).astype(jnp.bfloat16)
-    grad_query = (
-        jnp.einsum("hqk,khd->qhd", grad_scores, key_rows, preferred_element_type=jnp.float32)
-        * score_scale
-    )
-    grad_key = (
-        jnp.einsum("hqk,qhd->khd", grad_scores, query_rows, preferred_element_type=jnp.float32)
-        * score_scale
-    )
-    grad_value = jnp.einsum(
-        "hqk,qhd->khd",
-        probability.astype(jnp.bfloat16),
-        grad_context,
-        preferred_element_type=jnp.float32,
-    )
-    return jnp.stack([grad_query, grad_key, grad_value], axis=1).astype(jnp.bfloat16)
-
-
 MESH = pl.DeviceIdType.MESH
 F32 = jnp.float32
 LOW = jnp.bfloat16
 CHUNK = 32
 LAG = 2
 PIECE = 256
+QUERIES = 128
 
 
 def dot(a, b):
@@ -98,26 +51,31 @@
 
         lax.fori_loop(0, count, signal, 0)
     expected = sum(count for count, _ in targets)
-    if not line:
-        pl.semaphore_wait(barrier, expected)
-        return
     left, right = place > 0, place < size - 1
-
-    @pl.when(left)
-    def _():
-        pl.semaphore_signal(barrier, inc=1, device_id=(row, place - 1), device_id_type=MESH)
-
-    @pl.when(right)
-    def _():
-        pl.semaphore_signal(barrier, inc=1, device_id=(row, place + 1), device_id_type=MESH)
-
-    @pl.when(left & right)
-    def _():
-        pl.semaphore_wait(barrier, expected + 2)
-
-    @pl.when(jnp.logical_not(left & right))
-    def _():
-        pl.semaphore_wait(barrier, expected + 1)
+    if line:
+
+        @pl.when(left)
+        def _():
+            pl.semaphore_signal(barrier, inc=1, device_id=(row, place - 1), device_id_type=MESH)
+
+        @pl.when(right)
+        def _():
+            pl.semaphore_signal(barrier, inc=1, device_id=(row, place + 1), device_id_type=MESH)
+
+    def wait():
+        if not line:
+            pl.semaphore_wait(barrier, expected)
+            return
+
+        @pl.when(left & right)
+        def _():
+            pl.semaphore_wait(barrier, expected + 2)
+
+        @pl.when(jnp.logical_not(left & right))
+        def _():
+            pl.semaphore_wait(barrier, expected + 1)
+
+    return wait
 
 
 def partner():
@@ -409,29 +367,51 @@
     total[...] += jnp.sum(values.reshape(-1, 8, values.shape[-1]), axis=0)
 
 
+class Layer:
+    def __init__(self, array, layer):
+        self.array, self.layer = array, layer
+
+
 def call(collective, body, ins, outs, scratch):
     vmem = pl.BlockSpec(memory_space=pltpu.VMEM)
     names = [*ins, *outs]
+    fetched = {name: value for name, value in ins.items() if isinstance(value, Layer)}
     extra = {name: spec if isinstance(spec, list) else [spec] for name, spec in scratch.items()}
 
     def run(*refs):
         named = dict(zip(names, refs))
         rest = list(refs[len(names) :])
+        copies = {}
+        arrivals = rest.pop(0)
+        for number, (name, value) in enumerate(fetched.items()):
+            room = rest.pop(0)
+            copies[name] = pltpu.make_async_copy(named[name].at[value.layer], room, arrivals.at[number])
+            copies[name].start()
+            named[name] = room
         for name, specs in extra.items():
             taken = [rest.pop(0) for _ in specs]
             named[name] = taken if isinstance(scratch[name], list) else taken[0]
-        body(types.SimpleNamespace(**named))
+
+        def need(*wanted):
+            for name in wanted:
+                copies[name].wait()
+
+        body(types.SimpleNamespace(**named, need=need))
 
     results = pl.pallas_call(
         run,
         out_shape=list(outs.values()),
-        in_specs=[vmem] * len(ins),
+        in_specs=[pl.BlockSpec(memory_space=pl.ANY) if name in fetched else vmem for name in ins],
         out_specs=[vmem] * len(outs),
-        scratch_shapes=[spec for specs in extra.values() for spec in specs],
+        scratch_shapes=[
+            pltpu.SemaphoreType.DMA((len(fetched),)),
+            *(pltpu.VMEM(value.array.shape[1:], value.array.dtype) for value in fetched.values()),
+            *(spec for specs in extra.values() for spec in specs),
+        ],
         compiler_params=pltpu.CompilerParams(
             collective_id=collective, has_side_effects=True, vmem_limit_bytes=60 << 20
         ),
-    )(*ins.values())
+    )(*(value.array if isinstance(value, Layer) else value for value in ins.values()))
     return types.SimpleNamespace(**dict(zip(outs, results)))
 
 
@@ -463,25 +443,123 @@
         ref[...] = jnp.zeros_like(ref)
 
 
-def proj_stage(r, whole):
+def vector(ref, layer):
+    return ref[...].astype(F32)[layer : layer + 1]
+
+
+def head_lanes(values, head):
+    lane = lax.broadcasted_iota(jnp.int32, values.shape, 1)
+    return jnp.where(lane // HEAD == head, values, jnp.zeros_like(values))
+
+
+def turned(values):
+    return jnp.transpose(values.astype(F32)).astype(LOW)
+
+
+def mark_segments(r):
+    length = r.seg_row.shape[1]
+    wide = jnp.broadcast_to(r.seg_row[...].astype(F32), (QUERIES, length))
+    r.seg_cols[...] = jnp.transpose(wide)
+
+
+def masked_block(r, keys, queries, at):
+    same = r.seg_cols[...] == r.seg_row[:, at].astype(F32)
+    return jnp.where(same, dot_t(keys, queries) * HEAD ** (-0.5), masked_value)
+
+
+def project(r, layer):
+    bias = r.qv_bias[layer].astype(F32)
+    for member in range(3):
+        rows = dot(r.low_in[...], r.qkv_w[member])
+        if member != 1:
+            rows += bias[member // 2 : member // 2 + 1]
+        r.projected[member] = rows.astype(LOW)
+    r.turned_rows[...] = turned(r.projected[2])
+    mark_segments(r)
+
+
+def attend(r, block):
+    at = pl.ds(pl.multiple_of(block * QUERIES, QUERIES), QUERIES)
+    queries = r.projected[0, at]
+    heads = queries.shape[1] // HEAD
+    parts = []
+    for head in range(heads):
+        scores = masked_block(r, r.projected[1], head_lanes(queries, head), at)
+        row_max = jnp.max(scores, axis=0, keepdims=True)
+        exponent = jnp.exp(scores - row_max)
+        row_total = jnp.sum(exponent, axis=0, keepdims=True)
+        r.log_total[head : head + 1, at] = row_max + jnp.log(row_total)
+        probs = (exponent * (1.0 / row_total)).astype(LOW)
+        parts.append(dot(r.turned_rows[head * HEAD : (head + 1) * HEAD], probs))
+    r.context[at] = jnp.transpose(jnp.concatenate(parts, axis=0)).astype(LOW)
+
+
+def attend_first(r, half):
+    per_side = half // QUERIES
+    for side in range(2):
+        attend(r, side * per_side)
+    extras = []
+    for block in range(1, per_side):
+        for side in range(2):
+            step = max(0, block * QUERIES // CHUNK - 2 + side)
+            extras.append(at_step(step, lambda block=side * per_side + block: attend(r, block)))
+    return extras
+
+
+def attend_back(r, between=()):
+    rows = r.attn_low_in.shape[0]
+    heads = r.qkv_w.shape[2] // HEAD
+    scale = HEAD ** (-0.5)
+    mark_segments(r)
+    r.grad_context[...] = dot_t(r.attn_low_in[...], r.proj_w[...]).astype(LOW)
+    r.turned_rows[...] = turned(r.projected[1])
+    clear(r.grad_key, r.grad_value)
+    for number in range(rows // QUERIES):
+        at = slice(number * QUERIES, (number + 1) * QUERIES)
+        queries, context_rows = r.projected[0, at], r.grad_context[at]
+        parts = []
+        for head in range(heads):
+            to = slice(head * QUERIES, (head + 1) * QUERIES)
+            r.head_queries[to] = head_lanes(queries, head)
+            r.head_context[to] = head_lanes(context_rows, head)
+            scores = masked_block(r, r.projected[1], r.head_queries[to], at)
+            probability = jnp.exp(scores - r.log_total[head : head + 1, at])
+            grad_probs = dot_t(r.projected[2], r.head_context[to])
+            inner = jnp.sum(probability * grad_probs, axis=0, keepdims=True)
+            grad_scores = (probability * (grad_probs - inner)).astype(LOW)
+            r.score_rows[:, to] = grad_scores
+            r.prob_rows[:, to] = probability.astype(LOW)
+            parts.append(dot(r.turned_rows[head * HEAD : (head + 1) * HEAD], grad_scores))
+        r.grad_key[...] += dot(r.score_rows[...], r.head_queries[...])
+        r.grad_value[...] += dot(r.prob_rows[...], r.head_context[...])
+        r.grad_proj[0, at] = (jnp.transpose(jnp.concatenate(parts, axis=0)) * scale).astype(LOW)
+        if number < len(between):
+            between[number]()
+    r.grad_proj[1] = (r.grad_key[...] * scale).astype(LOW)
+    r.grad_proj[2] = r.grad_value[...].astype(LOW)
+    for slot, member in ((0, 0), (1, 2)):
+        r.qv_sum[slot] = jnp.sum(r.grad_proj[member].astype(F32).reshape(-1, 8, r.qv_sum.shape[2]), axis=0)
+
+
+def proj_stage(r, layer, whole):
     def produce(block):
         r.proj_line[0][block] = dot(r.context[block], r.proj_w[...]).astype(LOW)
 
     def finish(at, own, total):
         came = r.residual[at if whole else own].astype(F32)
-        unit, inverse = normalize(came + total + r.proj_b[...])
+        unit, inverse = normalize(came + total + vector(r.proj_b, layer))
         r.unit_one[own] = unit
         r.inverse_one[own] = inverse
-        result = unit * r.gain_one[...] + r.shift_one[...]
+        result = unit * vector(r.first_gain, layer) + vector(r.first_shift, layer)
         r.normed[own] = result
         r.normed_low[at] = result.astype(LOW)
 
     return stage_of(produce, finish, [r.normed_low], r.proj_line)
 
 
-def ffn_stage(r, last):
+def ffn_stage(r, layer, last):
     def produce(block):
-        pre = dot(r.normed_low[block], r.up_w[...]) + r.up_b[...]
+        pre = dot(r.normed_low[block], r.up_w[...]) + vector(r.up_b, layer)
         cdf = 0.5 * lax.erf(pre * math.sqrt(0.5)) + 0.5
         act = (pre * cdf).astype(LOW)
         slope = cdf + pre * jnp.exp(-0.5 * pre * pre) * (1.0 / math.sqrt(2 * math.pi))
@@ -490,12 +568,13 @@
         r.ffn_line[0][block] = dot(act, r.down_w[...]).astype(LOW)
 
     def finish(at, own, total):
-        unit, inverse = normalize(r.normed[own] + total + r.down_b[...])
-        result = unit * r.gain_two[...] + r.shift_two[...]
+        unit, inverse = normalize(r.normed[own] + total + vector(r.down_b, layer))
+        gain = vector(r.second_gain, layer)
+        result = unit * gain + vector(r.second_shift, layer)
         if last:
             r.mixed_own[own] = result.astype(LOW)
             grad_in = r.cotangent[at].astype(F32)
-            grad = norm_back(grad_in, r.gain_two[...], unit, inverse)
+            grad = norm_back(grad_in, gain, unit, inverse)
             r.grad_second[own] = grad
             r.branch[at] = grad.astype(LOW)
             tally(r.sums.at[0], grad_in * unit)
@@ -510,7 +589,7 @@
     return stage_of(produce, finish, [r.branch if last else r.low], r.ffn_line)
 
 
-def ffn_back_stage(r):
+def ffn_back_stage(r, layer):
     def produce(block):
         pre = (dot_t(r.branch[block], r.down_w[...]) * r.slope[block].astype(F32)).astype(LOW)
         r.pre[block] = pre
@@ -520,7 +599,7 @@
     def finish(at, own, total):
         grad_in = r.grad_second[own] + total
         unit = r.unit_one[own]
-        grad = norm_back(grad_in, r.gain_one[...], unit, r.inverse_one[own])
+        grad = norm_back(grad_in, vector(r.first_gain, layer), unit, r.inverse_one[own])
         r.grad_first[own] = grad
         r.attn_low[at] = grad.astype(LOW)
         tally(r.sums.at[3], grad_in * unit)
@@ -530,6 +609,28 @@
     return stage_of(produce, finish, [r.attn_low], r.back_line)
 
 
+def qkv_back_stage(r, layer, inner):
+    def produce(block):
+        total = sum(dot_t(r.grad_proj[member, block], r.qkv_w[member]) for member in range(3))
+        r.qkv_line[0][block] = total.astype(LOW)
+
+    def finish(at, own, total):
+        grad_in = r.grad_first_in[own] + total
+        if not inner:
+            r.grad_low[at] = grad_in.astype(LOW)
+            r.mixed[at] = r.mixed_own[own]
+            return
+        unit = r.unit_two[own]
+        grad = norm_back(grad_in, vector(r.second_gain, layer), unit, r.inverse_two[own])
+        r.grad_second[own] = grad
+        r.branch[at] = grad.astype(LOW)
+        tally(r.sums.at[0], grad_in * unit)
+        tally(r.sums.at[1], grad_in)
+        tally(r.sums.at[2], grad.astype(LOW).astype(F32))
+
+    return stage_of(produce, finish, [r.branch] if inner else [r.grad_low, r.mixed], r.qkv_line)
+
+
 def columns(piece):
     return pl.ds(pl.multiple_of(piece * PIECE, PIECE), PIECE)
 
@@ -549,33 +650,59 @@
 
 
 def attn_grads(r, out, first):
-    split = r.grad_proj.shape[1]
+    width, part = r.low_in.shape[1], r.context_in.shape[1]
 
     def piece_of(piece):
-        rows = pl.ds(pl.multiple_of(piece * PIECE, PIECE), PIECE)
-        out[rows, :split] = dot_tn(r.low_in[:, columns(piece)], r.grad_proj[...]).astype(LOW)
-        out[rows, split:] = dot_tn(r.attn_low_in[:, columns(piece)], r.context_in[...]).astype(LOW)
-
-    return [(first, r.low_in.shape[1] // PIECE, piece_of)]
+        for member in range(3):
+            rows = pl.ds(pl.multiple_of(member * width + piece * part, part), part)
+            taken = r.low_in[:, pl.ds(pl.multiple_of(piece * part, part), part)]
+            out[rows] = dot_tn(taken, r.grad_proj[member]).astype(LOW)
+        rows = pl.ds(pl.multiple_of(3 * width + piece * part, part), part)
+        taken = r.attn_low_in[:, pl.ds(pl.multiple_of(piece * part, part), part)]
+        out[rows] = dot_tn(r.context_in[...], taken).astype(LOW)
+
+    return [(first, width // part, piece_of)]
 
 
 def at_step(step, work):
     return (step, 1, lambda index: work())
 
 
-def forward_kernel(size, collective, context, proj, residual, ffn):
-    rows, width = context.shape[0], proj[0].shape[1]
-    half, hidden = rows // 2, ffn[0].shape[1]
-    whole = residual.shape[0] == rows
+def forward_scratch(rows, width, part):
+    return dict(
+        normed=pltpu.VMEM((rows // 2, width), F32),
+        turned_rows=pltpu.VMEM((part, rows), LOW),
+        seg_cols=pltpu.VMEM((rows, QUERIES), F32),
+        proj_line=line_scratch(rows, width),
+        ffn_line=line_scratch(rows, width),
+    )
+
+
+def kept_attention(rows, part):
+    return dict(
+        projected=shape(3, rows, part, kind=LOW),
+        log_total=shape(part // HEAD, rows),
+        context=shape(rows, part, kind=LOW),
+    )
+
+
+def forward_kernel(size, collective, layer, ins):
+    rows, width = ins["low_in"].shape
+    part, hidden = ins["proj_w"].array.shape[1], ins["up_w"].array.shape[2]
+    half = rows // 2
+    whole = ins["residual"].shape[0] == rows
 
     def body(r):
-        greet(size)
-        line_loop(size, [proj_stage(r, whole), ffn_stage(r, False)])
-
-    ins = dict(context=context, residual=residual)
-    ins.update(zip(("proj_w", "proj_b", "gain_one", "shift_one"), proj))
-    ins.update(zip(("up_w", "up_b", "down_w", "down_b", "gain_two", "shift_two"), ffn))
+        wait = greet(size)
+        r.need("qkv_w")
+        project(r, layer)
+        extras = attend_first(r, half)
+        r.need("proj_w", "up_w", "down_w")
+        wait()
+        line_loop(size, [proj_stage(r, layer, whole), ffn_stage(r, layer, False)], extras)
+
     outs = dict(
+        **kept_attention(rows, part),
         unit_one=shape(half, width),
         inverse_one=shape(half, 1),
         normed_low=shape(rows, width, kind=LOW),
@@ -586,31 +713,30 @@
         hidden=shape(half, width),
         low=shape(rows, width, kind=LOW),
     )
-    scratch = dict(
-        normed=pltpu.VMEM((half, width), F32),
-        proj_line=line_scratch(rows, width),
-        ffn_line=line_scratch(rows, width),
-    )
-    return call(collective, body, ins, outs, scratch)
-
-
-def turn_kernel(size, collective, context, proj, residual, ffn, cotangent):
-    rows, width = context.shape[0], proj[0].shape[1]
-    half, hidden = rows // 2, ffn[0].shape[1]
+    return call(collective, body, ins, outs, forward_scratch(rows, width, part))
+
+
+def turn_kernel(size, collective, layer, ins):
+    rows, width = ins["low_in"].shape
+    part, hidden = ins["proj_w"].array.shape[1], ins["up_w"].array.shape[2]
+    half = rows // 2
     chunks = half // CHUNK
-    whole = residual.shape[0] == rows
+    whole = ins["residual"].shape[0] == rows
 
     def body(r):
+        wait = greet(size)
         clear(r.sums, r.up_sum)
-        greet(size)
-        stages = [proj_stage(r, whole), ffn_stage(r, True), ffn_back_stage(r)]
+        r.need("qkv_w")
+        project(r, layer)
+        extras = attend_first(r, half)
+        r.need("proj_w", "up_w", "down_w")
+        wait()
+        stages = [proj_stage(r, layer, whole), ffn_stage(r, layer, True), ffn_back_stage(r, layer)]
         first = 4 * LAG * (size - 1) + chunks
-        line_loop(size, stages, ffn_grads(r, r.ffn_grad, first))
-
-    ins = dict(context=context, residual=residual, cotangent=cotangent)
-    ins.update(zip(("proj_w", "proj_b", "gain_one", "shift_one"), proj))
-    ins.update(zip(("up_w", "up_b", "down_w", "down_b", "gain_two", "shift_two"), ffn))
+        line_loop(size, stages, [*extras, *ffn_grads(r, r.ffn_grad, first)])
+
     outs = dict(
+        **kept_attention(rows, part),
         mixed_own=shape(half, width, kind=LOW),
         grad_first=shape(half, width),
         attn_low=shape(rows, width, kind=LOW),
@@ -619,7 +745,7 @@
         sums=shape(6, 8, width),
     )
     scratch = dict(
-        normed=pltpu.VMEM((half, width), F32),
+        **forward_scratch(rows, width, part),
         unit_one=pltpu.VMEM((half, width), F32),
         inverse_one=pltpu.VMEM((half, 1), F32),
         normed_low=pltpu.VMEM((rows, width), LOW),
@@ -628,99 +754,106 @@
         pre=pltpu.VMEM((rows, hidden), LOW),
         branch=pltpu.VMEM((rows, width), LOW),
         grad_second=pltpu.VMEM((half, width), F32),
-        proj_line=line_scratch(rows, width),
-        ffn_line=line_scratch(rows, width),
         back_line=line_scratch(rows, width),
     )
     return call(collective, body, ins, outs, scratch)
 
 
-def qkv_back_stage(r, inner):
-    def produce(block):
-        r.qkv_line[0][block] = dot_t(r.grad_proj[block], r.qkv_w[...]).astype(LOW)
-
-    def finish(at, own, total):
-        grad_in = r.grad_first_in[own] + total
-        if not inner:
-            r.grad_low[at] = grad_in.astype(LOW)
-            r.mixed[at] = r.mixed_own[own]
-            return
-        unit = r.unit_two[own]
-        grad = norm_back(grad_in, r.gain_two[...], unit, r.inverse_two[own])
-        r.grad_second[own] = grad
-        r.branch[at] = grad.astype(LOW)
-        tally(r.sums.at[0], grad_in * unit)
-        tally(r.sums.at[1], grad_in)
-        tally(r.sums.at[2], grad.astype(LOW).astype(F32))
-
-    return stage_of(produce, finish, [r.branch] if inner else [r.grad_low, r.mixed], r.qkv_line)
+def back_scratch(rows, part):
+    heads = part // HEAD
+    return dict(
+        seg_cols=pltpu.VMEM((rows, QUERIES), F32),
+        turned_rows=pltpu.VMEM((part, rows), LOW),
+        grad_context=pltpu.VMEM((rows, part), LOW),
+        grad_key=pltpu.VMEM((rows, part), F32),
+        grad_value=pltpu.VMEM((rows, part), F32),
+        grad_proj=pltpu.VMEM((3, rows, part), LOW),
+        head_queries=pltpu.VMEM((heads * QUERIES, part), LOW),
+        head_context=pltpu.VMEM((heads * QUERIES, part), LOW),
+        score_rows=pltpu.VMEM((rows, heads * QUERIES), LOW),
+        prob_rows=pltpu.VMEM((rows, heads * QUERIES), LOW),
+    )
 
 
 def spread_targets(chips):
     return [(1, lambda index: partner()), (chips - 1, lambda index: plane_peer(chips, index))]
 
 
-def backward_kernel(size, chips, collective, attn, below, ffn, ffn_grad):
-    rows, width = attn["grad_proj"].shape[0], attn["low_in"].shape[1]
-    half, hidden = rows // 2, ffn["up_w"].shape[1]
+def backward_kernel(size, chips, collective, layer, ins):
+    rows, width = ins["low_in"].shape
+    part, hidden = ins["proj_w"].array.shape[1], ins["up_w"].array.shape[2]
+    half = rows // 2
     chunks = half // CHUNK
     span = 2 * LAG * (size - 1)
-    ffn_rows = width + hidden
+    ffn_rows, attn_rows = width + hidden, 4 * width
 
     def body(r):
+        wait = greet(size, targets=spread_targets(chips))
         clear(r.sums, r.up_sum)
-        greet(size, targets=spread_targets(chips))
         near, far, *sems = r.ffn_spread
         ffn_sum = Spread(chips, ffn_rows, width, r.ffn_grad_in, near, far, r.ffn_share, r.ffn_whole, sems)
         near, far, *sems = r.attn_spread
-        attn_sum = Spread(chips, width, width, r.attn_grad, near, far, r.attn_share, None, sems)
+        attn_sum = Spread(chips, attn_rows, part, r.attn_grad, near, far, r.attn_share, None, sems)
+        wait()
         ffn_sum.to_partner()
+        r.need("proj_w")
+        attend_back(r, [lambda: None, ffn_sum.to_chips])
+        r.need("qkv_w", "up_w", "down_w")
         extras = [
-            at_step(2, ffn_sum.to_chips),
-            *attn_grads(r, r.attn_grad, 3),
+            *attn_grads(r, r.attn_grad, 1),
             at_step(8, attn_sum.to_partner),
-            at_step(span + 3, lambda: (ffn_sum.sum_share(), ffn_sum.give_share())),
-            at_step(span + 4, attn_sum.to_chips),
+            at_step(span, lambda: (ffn_sum.sum_share(), ffn_sum.give_share())),
+            at_step(span + 1, attn_sum.to_chips),
             *ffn_grads(r, r.ffn_grad, span + chunks),
-            at_step(2 * span + 3, ffn_sum.to_other_core),
+            at_step(2 * span + 2, ffn_sum.to_other_core),
         ]
-        line_loop(size, [qkv_back_stage(r, True), ffn_back_stage(r)], extras)
+        stages = [qkv_back_stage(r, layer - 1, True), ffn_back_stage(r, layer - 1)]
+        line_loop(size, stages, extras)
         attn_sum.sum_share()
         attn_sum.settle_sum()
         ffn_sum.settle_sum()
         ffn_sum.settle_whole()
 
-    ins = dict(**attn, **below, **ffn, ffn_grad_in=ffn_grad)
     outs = dict(
         grad_first=shape(half, width),
         attn_low=shape(rows, width, kind=LOW),
         ffn_grad=shape(ffn_rows, width, kind=LOW),
         up_sum=shape(8, hidden),
         sums=shape(6, 8, width),
-        attn_share=shape(width // 2 // chips, width, kind=LOW),
+        qv_sum=shape(2, 8, part),
+        attn_share=shape(attn_rows // 2 // chips, part, kind=LOW),
         ffn_whole=shape(ffn_rows, width, kind=LOW),
     )
     scratch = dict(
+        **back_scratch(rows, part),
         pre=pltpu.VMEM((rows, hidden), LOW),
         branch=pltpu.VMEM((rows, width), LOW),
         grad_second=pltpu.VMEM((half, width), F32),
-        attn_grad=pltpu.VMEM((width, width), LOW),
+        attn_grad=pltpu.VMEM((attn_rows, part), LOW),
         ffn_share=pltpu.VMEM((ffn_rows // 2 // chips, width), LOW),
         qkv_line=line_scratch(rows, width),
         back_line=line_scratch(rows, width),
         ffn_spread=Spread.scratch(chips, ffn_rows, width),
-        attn_spread=Spread.scratch(chips, width, width),
+        attn_spread=Spread.scratch(chips, attn_rows, part),
     )
     return call(collective, body, ins, outs, scratch)
 
 
-def last_kernel(size, chips, collective, attn, mixed_own, ffn_grad, attn_share, small, own_rows):
-    rows, width = attn["grad_proj"].shape[0], attn["low_in"].shape[1]
-    chunks = rows // 2 // CHUNK
+def last_kernel(size, chips, collective, layers, ins):
+    rows, width = ins["low_in"].shape
+    part, hidden = ins["proj_w"].array.shape[1], ins["up_sums"][0].shape[1]
     span = 2 * LAG * (size - 1)
-    ffn_rows = ffn_grad.shape[0]
-    count = small.shape[0]
+    ffn_rows, attn_rows = width + hidden, 4 * width
+    own_rows = layers * (2 * part + hidden) // width
+    count = -(-(own_rows + 6 * layers) // 8) * 8
     teams = 2 * chips
+    up_sums, all_sums, qv_sums = ins.pop("up_sums"), ins.pop("all_sums"), ins.pop("qv_sums")
+    ins = dict(
+        **ins,
+        **{"up_sum_%d" % n: value for n, value in enumerate(up_sums)},
+        **{"sums_%d" % n: value for n, value in enumerate(all_sums)},
+        **{"qv_sum_%d" % (n + 1): value for n, value in enumerate(qv_sums)},
+    )
 
     def row_peer(index):
         row, place = here()
@@ -730,16 +863,23 @@
         row, place = here()
         return (row, lax.rem(place + index + 1, size))
 
+    def each(number, work):
+        def one(index, carry):
+            work(index)
+            return carry
+
+        lax.fori_loop(0, number, one, 0)
+
     def body(r):
         row, place = here()
         clear(r.ends)
-        greet(size, line=False, targets=[(teams - 1, row_peer), (size - 1, line_peer)])
+        wait = greet(size, line=False, targets=[(teams - 1, row_peer), (size - 1, line_peer)])
         near, far, *sems = r.ffn_spread
         ffn_sum = Spread(chips, ffn_rows, width, r.ffn_grad_in, near, far, r.ffn_share, r.ffn_whole, sems)
         near, far, *sems = r.attn_spread
-        attn_sum = Spread(chips, width, width, r.attn_grad, near, far, r.attn_share, r.attn_whole, sems)
+        attn_sum = Spread(chips, attn_rows, part, r.attn_grad, near, far, r.attn_share, r.attn_whole, sems)
         near, far, *sems = r.above_spread
-        above_sum = Spread(chips, width, width, None, near, far, r.above_share, r.above_whole, sems)
+        above_sum = Spread(chips, attn_rows, part, None, near, far, r.above_share, r.above_whole, sems)
 
         def end_copy(slot, index):
             return pltpu.make_async_remote_copy(
@@ -761,16 +901,27 @@
                 device_id_type=MESH,
             )
 
-        def each(number, work):
-            def one(index, carry):
-                work(index)
-                return carry
-
-            lax.fori_loop(0, number, one, 0)
-
         end_places = ((0, 0), (1, size - 1))
 
         def small_to_line():
+            named = vars(r)
+            clear(r.small)
+            lines = []
+            for layer in range(layers):
+                sums = jnp.sum(named["qv_sum_%d" % layer if layer else "qv_sum"][...], axis=1)
+                lines += [sums[0:1], sums[1:2]]
+            flat = jnp.concatenate(lines, axis=1)
+            for layer in range(layers):
+                flat = jnp.concatenate(
+                    [flat, jnp.sum(named["up_sum_%d" % layer][...], axis=0, keepdims=True)], axis=1
+                )
+            for number in range(own_rows):
+                r.small[number : number + 1] = flat[:, number * width : (number + 1) * width]
+            for layer in range(layers):
+                sums = jnp.sum(named["sums_%d" % layer][...], axis=1)
+                for member in range(6):
+                    to = own_rows + member * layers + layer
+                    r.small[to : to + 1] = sums[member : member + 1]
             for slot, end in end_places:
 
                 @pl.when(place == end)
@@ -802,18 +953,21 @@
                 def _():
                     each(size - 1, lambda index: end_copy(slot, index).wait_send())
 
+        wait()
         ffn_sum.to_partner()
         above_sum.give_share()
+        r.need("proj_w")
+        attend_back(r, [lambda: None, ffn_sum.to_chips])
+        r.need("qkv_w")
         small_to_line()
         extras = [
             *attn_grads(r, r.attn_grad, 0),
-            at_step(1, ffn_sum.to_chips),
             at_step(4, attn_sum.to_partner),
             at_step(5, small_to_teams),
             at_step(6, attn_sum.to_chips),
             at_step(span, above_sum.to_other_core),
         ]
-        line_loop(size, [qkv_back_stage(r, False)], extras)
+        line_loop(size, [qkv_back_stage(r, 0, False)], extras)
         ffn_sum.sum_share()
         ffn_sum.give_share()
         attn_sum.sum_share()
@@ -827,19 +981,21 @@
         ffn_sum.settle_whole()
         attn_sum.settle_whole()
 
-    ins = dict(**attn, mixed_own=mixed_own, ffn_grad_in=ffn_grad, above_share=attn_share, small=small)
     outs = dict(
         grad_low=shape(rows, width, kind=LOW),
         mixed=shape(rows, width, kind=LOW),
         ffn_whole=shape(ffn_rows, width, kind=LOW),
-        attn_whole=shape(width, width, kind=LOW),
-        above_whole=shape(width, width, kind=LOW),
+        attn_whole=shape(attn_rows, part, kind=LOW),
+        above_whole=shape(attn_rows, part, kind=LOW),
         small_total=shape(count, width),
     )
     scratch = dict(
-        attn_grad=pltpu.VMEM((width, width), LOW),
+        **back_scratch(rows, part),
+        qv_sum=pltpu.VMEM((2, 8, part), F32),
+        small=pltpu.VMEM((count, width), F32),
+        attn_grad=pltpu.VMEM((attn_rows, part), LOW),
         ffn_share=pltpu.VMEM((ffn_rows // 2 // chips, width), LOW),
-        attn_share=pltpu.VMEM((width // 2 // chips, width), LOW),
+        attn_share=pltpu.VMEM((attn_rows // 2 // chips, part), LOW),
         ends=pltpu.VMEM((2, count, width), F32),
         mine=pltpu.VMEM((count, width), F32),
         others=pltpu.VMEM((teams, count, width), F32),
@@ -849,10 +1005,103 @@
         team_got=pltpu.SemaphoreType.DMA((teams,)),
         qkv_line=line_scratch(rows, width, 2),
         ffn_spread=Spread.scratch(chips, ffn_rows, width),
-        attn_spread=Spread.scratch(chips, width, width),
-        above_spread=Spread.scratch(chips, width, width),
-    )
-    return call(collective, body, ins, outs, scratch)
+        attn_spread=Spread.scratch(chips, attn_rows, part),
+        above_spread=Spread.scratch(chips, attn_rows, part),
+    )
+    return call(collective, body, ins, outs, scratch), own_rows
+
+
+def assemble(attn_wholes, ffn_wholes, mixed, grad_low, small, own_rows, part):
+    layers = len(attn_wholes)
+    rows, width = mixed.shape
+    hidden = ffn_wholes[0].shape[0] - width
+    steps = 8
+    cut = width // steps
+
+    def for_layer(number, spec_of):
+        def index(layer, step):
+            return spec_of(jnp.where(layer == number, step, jnp.where(layer < number, 0, steps - 1)))
+
+        return index
+
+    ins, in_specs = [], []
+    for number in range(layers):
+        ins += [
+            attn_wholes[number].reshape(4, width, part),
+            attn_wholes[number].reshape(-1, part, part),
+            ffn_wholes[number].reshape(-1, width, width),
+        ]
+        in_specs += [
+            pl.BlockSpec((3, cut, part), for_layer(number, lambda step: (0, step, 0))),
+            pl.BlockSpec((width // part, part // steps, part), for_layer(number, lambda step: (3, step, 0))),
+            pl.BlockSpec((1 + hidden // width, cut, width), for_layer(number, lambda step: (0, step, 0))),
+        ]
+    slab = rows // (layers * steps)
+    ins += [mixed, grad_low, small]
+    row_spec = pl.BlockSpec((slab, width), lambda layer, step: (layer * steps + step, 0))
+    in_specs += [row_spec, row_spec, pl.BlockSpec(small.shape, lambda layer, step: (0, 0))]
+    def all_of(*dims):
+        return pl.BlockSpec(dims, lambda layer, step: (0,) * len(dims))
+
+    out_shape = [
+        shape(rows, width),
+        shape(rows, width),
+        shape(layers, 3, width, part),
+        shape(layers, part, width),
+        shape(layers, width, hidden),
+        shape(layers, hidden, width),
+        shape(layers, 2, part),
+        shape(layers, hidden),
+    ] + [shape(layers, width)] * 6
+    out_specs = [
+        row_spec,
+        row_spec,
+        pl.BlockSpec((1, 3, cut, part), lambda layer, step: (layer, 0, step, 0)),
+        pl.BlockSpec((1, part // steps, width), lambda layer, step: (layer, step, 0)),
+        pl.BlockSpec((1, cut, hidden), lambda layer, step: (layer, step, 0)),
+        pl.BlockSpec((1, cut, width), lambda layer, step: (layer, step, 0)),
+        all_of(layers, 2, part),
+        all_of(layers, hidden),
+    ] + [all_of(layers, width)] * 6
+
+    def body(*refs):
+        sources = refs[: 3 * layers]
+        mixed_in, grad_in, small_in = refs[3 * layers : 3 * layers + 3]
+        mixed_out, grad_out, qkv, proj, up, down, qv, up_b, *norms = refs[3 * layers + 3 :]
+        mixed_out[...] = mixed_in[...].astype(F32)
+        grad_out[...] = grad_in[...].astype(F32)
+        for number in range(layers):
+            attn_in, proj_in, ffn_in = sources[3 * number : 3 * number + 3]
+
+            @pl.when(pl.program_id(0) == number)
+            def _():
+                qkv[0] = attn_in[...].astype(F32)
+                for block in range(width // part):
+                    proj[0, :, block * part : (block + 1) * part] = proj_in[block].astype(F32)
+                up[0] = ffn_in[0].astype(F32)
+                down[0] = ffn_in[1].astype(F32)
+
+        @pl.when((pl.program_id(0) == 0) & (pl.program_id(1) == 0))
+        def _():
+            values = small_in[...]
+            flat = jnp.concatenate([values[n : n + 1] for n in range(own_rows)], axis=1)
+            for layer in range(layers):
+                for member in range(2):
+                    at = (2 * layer + member) * part
+                    qv[layer, member : member + 1] = flat[:, at : at + part]
+                at = 2 * layers * part + layer * hidden
+                up_b[layer : layer + 1] = flat[:, at : at + hidden]
+            for member, norm in enumerate(norms):
+                norm[...] = values[own_rows + member * layers : own_rows + (member + 1) * layers]
+
+    return pl.pallas_call(
+        body,
+        grid=(layers, steps),
+        out_shape=out_shape,
+        in_specs=in_specs,
+        out_specs=out_specs,
+        compiler_params=pltpu.CompilerParams(vmem_limit_bytes=48 << 20),
+    )(*ins)
 
 
 def local(
@@ -877,144 +1126,117 @@
     layers = qkv_weight.shape[0]
     size = lax.axis_size("tensor")
     chips = lax.axis_size("dp") // 2
-    part_width = qkv_weight.shape[-1]
-    hidden = up_weight.shape[-1]
-    heads = part_width // HEAD
-    seg_row = segment_ids.reshape(length)
-
-    def row_of(stacked, layer):
-        return stacked[layer].astype(F32).reshape(1, -1)
-
+    part = qkv_weight.shape[-1]
+    qkv_stack = jnp.transpose(qkv_weight, (0, 2, 1, 3))
     low = tokens.reshape(rows, width)
     residual = low
-    cot = cotangent.reshape(rows, width)
     kept = []
     for layer in range(layers):
-        qkv = qkv_weight[layer].reshape(width, 3 * part_width)
-        bias = jnp.concatenate([qv_bias[layer, 0], jnp.zeros_like(qv_bias[layer, 0]), qv_bias[layer, 1]])
-        projected = (dot(low, qkv) + bias.astype(F32)).astype(LOW)
-        split = projected.reshape(length, 3, heads, HEAD)
-        context, log_total = attend_forward((split[:, 0], split[:, 1], split[:, 2], seg_row))
-        context = context.reshape(rows, part_width)
-        proj = (
-            proj_weight[layer],
-            row_of(proj_bias, layer),
-            row_of(first_gain, layer),
-            row_of(first_shift, layer),
+        ins = dict(
+            low_in=low,
+            residual=residual,
+            seg_row=segment_ids,
+            qkv_w=Layer(qkv_stack, layer),
+            qv_bias=qv_bias,
+            proj_w=Layer(proj_weight, layer),
+            proj_b=proj_bias,
+            first_gain=first_gain,
+            first_shift=first_shift,
+            up_w=Layer(up_weight, layer),
+            up_b=up_bias,
+            down_w=Layer(down_weight, layer),
+            down_b=down_bias,
+            second_gain=second_gain,
+            second_shift=second_shift,
         )
-        ffn = (
-            up_weight[layer],
-            row_of(up_bias, layer),
-            down_weight[layer],
-            row_of(down_bias, layer),
-            row_of(second_gain, layer),
-            row_of(second_shift, layer),
-        )
-        keep = types.SimpleNamespace(low=low, qkv=qkv, split=split, log_total=log_total, context=context)
         if layer + 1 < layers:
-            keep.done = forward_kernel(size, layer, context, proj, residual, ffn)
-            residual, low = keep.done.hidden, keep.done.low
+            done = forward_kernel(size, layer, layer, ins)
+            kept.append((low, done))
+            residual, low = done.hidden, done.low
         else:
-            above = turn_kernel(size, layer, context, proj, residual, ffn, cot)
-            mixed_own = above.mixed_own
-        kept.append(keep)
-
-    sums = [None] * layers
-    norm_sums = [None] * layers
-    up_sums = [None] * layers
-    qv_sums = [None] * layers
-    ffn_whole = [None] * layers
-    attn_whole = [None] * layers
-    norm_sums[layers - 1] = above.sums.sum(axis=1)
-    up_sums[layers - 1] = above.up_sum.sum(axis=0)
-    attn_share = None
+            done = turn_kernel(size, layer, layer, dict(**ins, cotangent=cotangent.reshape(rows, width)))
+            kept.append((low, done))
+
+    above = done
+    mixed_own = done.mixed_own
+    all_sums, up_sums, qv_sums = [done.sums], [done.up_sum], []
+    ffn_wholes, attn_wholes = [], []
     for layer in range(layers - 1, -1, -1):
-        keep = kept[layer]
-        split = keep.split
-        grad_context = dot_t(above.attn_low, proj_weight[layer]).astype(LOW)
-        grad_heads = attend_backward(
-            (
-                split[:, 0],
-                split[:, 1],
-                split[:, 2],
-                seg_row,
-                keep.log_total,
-                grad_context.reshape(length, heads, HEAD),
-            )
-        )
-        grad_proj = grad_heads.reshape(rows, 3 * part_width)
-        qkv_sums = jnp.sum(grad_proj.astype(F32).reshape(rows, 3, part_width), axis=0)
-        qv_sums[layer] = jnp.concatenate([qkv_sums[0], qkv_sums[2]])
-        attn = dict(
-            grad_proj=grad_proj,
+        low, done = kept[layer]
+        ins = dict(
+            low_in=low,
+            seg_row=segment_ids,
+            projected=done.projected,
+            log_total=done.log_total,
+            context_in=done.context,
+            attn_low_in=above.attn_low,
             grad_first_in=above.grad_first,
-            qkv_w=keep.qkv,
-            low_in=keep.low,
-            attn_low_in=above.attn_low,
-            context_in=keep.context,
+            qkv_w=Layer(qkv_stack, layer),
+            proj_w=Layer(proj_weight, layer),
+            ffn_grad_in=above.ffn_grad,
         )
         if layer > 0:
-            done = kept[layer - 1].done
-            below = dict(
-                unit_two=done.unit_two,
-                inverse_two=done.inverse_two,
-                gain_two=row_of(second_gain, layer - 1),
+            _, below = kept[layer - 1]
+            above = backward_kernel(
+                size,
+                chips,
+                2 * layers - layer,
+                layer,
+                dict(
+                    **ins,
+                    unit_two=below.unit_two,
+                    inverse_two=below.inverse_two,
+                    second_gain=second_gain,
+                    act=below.act,
+                    slope=below.slope,
+                    normed_low=below.normed_low,
+                    unit_one=below.unit_one,
+                    inverse_one=below.inverse_one,
+                    first_gain=first_gain,
+                    up_w=Layer(up_weight, layer - 1),
+                    down_w=Layer(down_weight, layer - 1),
+                ),
             )
-            ffn = dict(
-                act=done.act,
-                slope=done.slope,
-                normed_low=done.normed_low,
-                unit_one=done.unit_one,
-                inverse_one=done.inverse_one,
-                gain_one=row_of(first_gain, layer - 1),
-                up_w=up_weight[layer - 1],
-                down_w=down_weight[layer - 1],
+            all_sums.insert(0, above.sums)
+            up_sums.insert(0, above.up_sum)
+            qv_sums.insert(0, above.qv_sum)
+            ffn_wholes.insert(0, above.ffn_whole)
+        else:
+            last, own_rows = last_kernel(
+                size,
+                chips,
+                2 * layers,
+                layers,
+                dict(
+                    **ins,
+                    mixed_own=mixed_own,
+                    above_share=above.attn_share,
+                    up_sums=up_sums,
+                    all_sums=all_sums,
+                    qv_sums=qv_sums,
+                ),
             )
-            above = backward_kernel(
-                size, chips, 2 * layers - layer, attn, below, ffn, above.ffn_grad
-            )
-            norm_sums[layer - 1] = above.sums.sum(axis=1)
-            up_sums[layer - 1] = above.up_sum.sum(axis=0)
-            ffn_whole[layer] = above.ffn_whole
-            attn_share = above.attn_share
-        else:
-            norm_rows = jnp.stack(norm_sums, axis=1).reshape(6 * layers, width)
-            own = jnp.concatenate([*qv_sums, *up_sums]).reshape(-1, width)
-            used = own.shape[0] + norm_rows.shape[0]
-            small = jnp.concatenate([own, norm_rows, jnp.zeros((-used % 8, width), F32)])
-            last = last_kernel(
-                size, chips, 2 * layers, attn, mixed_own, above.ffn_grad, attn_share, small, own.shape[0]
-            )
-            ffn_whole[0] = last.ffn_whole
-            attn_whole[0] = last.attn_whole
-            attn_whole[1] = last.above_whole
-
-    totals = last.small_total
-    flat = totals[: own.shape[0]].reshape(-1)
-    at = layers * 2 * part_width
-    qv_total = flat[:at].reshape(layers, 2, part_width)
-    up_total = flat[at:].reshape(layers, hidden)
-    rest = totals[own.shape[0] : used].reshape(6, layers, width)
-    split_at = 3 * part_width
-
-    def stack(parts):
-        return jnp.stack([part.astype(F32) for part in parts])
-
+            ffn_wholes.insert(0, last.ffn_whole)
+            attn_wholes = [last.attn_whole, last.above_whole]
+
+    mixed, input_grad, qkv, proj, up, down, qv, up_b, *norms = assemble(
+        attn_wholes, ffn_wholes, last.mixed, last.grad_low, last.small_total, own_rows, part
+    )
     return (
-        last.mixed.astype(F32).reshape(tokens.shape),
-        last.grad_low.astype(F32).reshape(tokens.shape),
-        stack([part[:, :split_at].reshape(width, 3, part_width) for part in attn_whole]),
-        qv_total,
-        stack([part[:, split_at:].T for part in attn_whole]),
-        rest[5],
-        rest[3],
-        rest[4],
-        stack([part[:width] for part in ffn_whole]),
-        up_total,
-        stack([part[width:] for part in ffn_whole]),
-        rest[2],
-        rest[0],
-        rest[1],
+        mixed.reshape(tokens.shape),
+        input_grad.reshape(tokens.shape),
+        jnp.transpose(qkv, (0, 2, 1, 3)),
+        qv,
+        proj,
+        norms[5],
+        norms[3],
+        norms[4],
+        up,
+        up_b,
+        down,
+        norms[2],
+        norms[0],
+        norms[1],
     )
 
 

time: 465 us -> 416 us (0.89); the launches traced: 464 us -> 408 us
  local copies, waits for them, and re-layouts: 48.9 us -> 4.87 us
  Pallas kernels: 361 us -> 402 us
  other arithmetic: 30.4 us -> 0 us
  matrix products: 22.8 us -> 0 us
    pallas_call x4 -> x5, Pallas kernels: 361 us -> 402 us  [the longest x4 384 us: call(): pl.pallas_call(run, out_shape=list(outs.values()), in_specs=[pl.BlockSpec...]
    dot_general x16 -> x0, matrix products: 22.8 us -> none  [the longest x2 5.92 us: attend_backward(): jnp.einsum('hqk,qhd->khd', probability.astype(jnp.bfloat16), grad_context...]
    slice x10 -> x0, local copies, waits for them, and re-layouts: 12.7 us -> none  [the longest x4 6.27 us: local(): part[:, :split_at].reshape(width, 3, part_width)]
    another operation x5 -> x0, other arithmetic: 11.2 us -> none  [the longest x4 11.1 us: stack(): return jnp.stack([part.astype(F32) for part in parts])]
    another operation x8 -> x0, local copies, waits for them, and re-layouts: 8.62 us -> none  [the longest x4 5.42 us: stack(): return jnp.stack([part.astype(F32) for part in parts])]
    squeeze x6 -> x0, local copies, waits for them, and re-layouts: 8.51 us -> none  [the longest x1 5.94 us: local(): down_weight[layer]]
    convert_element_type x7 -> x0, other arithmetic: 7.93 us -> none  [the longest x4 5.5 us: row_of(): return stacked[layer].astype(F32).reshape(1, -1)]
    unnamed x27 -> x8, local copies, waits for them, and re-layouts: 12.7 us -> 4.87 us
where the time goes in v4:
time: 416 us; the launch traced here: 408 us
  Pallas kernels  402 us (97%)
  local copies, waits for them, and re-layouts  4.87 us (1%)
    pallas_call x4, Pallas kernels, call(): pl.pallas_call(run, out_shape=list(outs.values()), in_specs=[pl.BlockSpec...  384 us
    pallas_call x1, Pallas kernels, assemble(): pl.pallas_call(body, grid=(layers, steps), out_shape=out_shape, in_specs=...  17.1 us

profile of v4, /device:TPU:0, one launch (start us, length us, event | category | flops | bytes accessed | tf_op | source)
XLA Modules:
  0.0 407.6 jit_solution(10216030606612544791)
XLA Ops:
  0.6 78.5 %shard_map.254 = (bf16[3,512,256]{2,1,0:T(8,128)(2,1)}, f32[4,512]{1,0:T(4,128)}, bf16[512,256]{1,0:T(8,128)(2,1)}, f32[256,1024]{1,0:T(8,128)}, f32[256,1]{1,0:...) custom-call(bf16[512,1024]{1,0:T(8,128)(2,1)} %bitcast.18, ...), custom_call_target="tpu_custom_call" | custom-call | tf_op jit(solution)/shard_map/pallas_call | solution.py:401
  79.1 107.4 %shard_map.255 = (bf16[3,512,256]{2,1,0:T(8,128)(2,1)}, f32[4,512]{1,0:T(4,128)}, bf16[512,256]{1,0:T(8,128)(2,1)}, bf16[256,1024]{1,0:T(8,128)(2,1)}, f32[256,1...) custom-call(bf16[512,1024]{1,0:T(8,128)(2,1)} %get-tuple-element.66., ...), custom_call_target="tpu_custom_call" | custom-call | tf_op jit(solution)/shard_map/pallas_call | solution.py:401
  186.6 93.4 %shard_map.256 = (f32[256,1024]{1,0:T(8,128)}, bf16[512,1024]{1,0:T(8,128)(2,1)}, bf16[2048,1024]{1,0:T(8,128)(2,1)}, f32[8,1024]{1,0:T(8,128)}, f32[6,8,1024]{2...) custom-call(bf16[512,1024]{1,0:T(8,128)(2,1)} %get-tuple-element.66.refs_0_, ...), custom_call_target="tpu_custom_call" | custom-call | tf_op jit(solution)/shard_map/pallas_call | solution.py:401
  280.0 105.2 %shard_map.257 = (bf16[512,1024]{1,0:T(8,128)(2,1)}, bf16[512,1024]{1,0:T(8,128)(2,1)}, bf16[2048,1024]{1,0:T(8,128)(2,1)}, bf16[4096,256]{1,0:T(8,128)(2,1)}, b...) custom-call(bf16[512,1024]{1,0:T(8,128)(2,1)} %bitcast.20, s32[1,512]{1,0:T(1,128)} %refs_1_.3, ...), custom_call_target="tpu_custom_call" | custom-call | tf_op jit(solution)/shard_map/pallas_call | solution.py:401
  385.2 0.0 copy-start
  385.2 1.6 copy-done
  386.8 0.0 copy-start.1
  386.8 1.2 copy-done.1
  388.0 0.0 copy-start.2
  388.0 1.2 copy-done.2
  389.2 0.0 copy-start.3
  389.2 0.8 copy-done.3
  390.1 17.1 %shard_map.258 = (f32[512,1024]{1,0:T(8,128)}, f32[512,1024]{1,0:T(8,128)}, f32[2,3,1024,256]{3,2,1,0:T(8,128)}, f32[2,256,1024]{2,1,0:T(8,128)}, f32[2,1024,102...) custom-call(bf16[4,1024,256]{2,1,0:T(8,128)(2,1)S(1)} %bitcast.12, ...), custom_call_target="tpu_custom_call" | custom-call | tf_op jit(solution)/shard_map/pallas_call | solution.py:1097
Async XLA Ops:
  385.2 1.6 copy-start
  386.8 1.2 copy-start.1
  388.0 1.2 copy-start.2
  389.2 0.8 copy-start.3
